TPU v7x, 512 devices: a whole 4x4x16 slice. The times are simulated.
512 devices in a mesh: dp: 32 (over x_lo, z), tensor: 16 (over y, x_hi, core).
Axes of the slice: x: 4 (x_hi: 2, x_lo: 2; x = x_hi * 2 + x_lo), y: 4, z: 16, core: 2. Of those that a mesh axis runs over, the one named last changes fastest.
Arguments:
- gate_pre: bfloat16 [2048, 6656], P('dp', 'tensor'), may hold values from -6 to 6
- up_pre: bfloat16 [2048, 6656], P('dp', 'tensor'), may hold values from -6 to 6
- out_grad: bfloat16 [2048, 16384], P('tensor', 'dp'), may hold values from -6 to 6
- down_weight: bfloat16 [6656, 16384], P('tensor', 'dp'), may hold values from -0.046875 to 0.046875
Outputs:
- gate_grad: bfloat16 [2048, 6656], P('dp', 'tensor')
- up_grad: bfloat16 [2048, 6656], P('dp', 'tensor')
- weight_grad: float32 [6656, 16384], P('tensor', 'dp')
All inputs are finite; a program needn't handle non-finite values.
Results may differ from a plain program's by a relative error of at most 0.0029.
Values may be sent and summed in bfloat16 or wider, within the bound.
No kernel may reach another device: no remote copies, remote signals or barrier semaphores. Data moves between devices by JAX's collectives and lax.ppermute only.
A program may use at most 64 MiB of HBM per device.

v0:
```python
import jax
import jax.numpy as jnp
from jax import lax
from jax.sharding import PartitionSpec as P


def activate(gate_pre):
    gate_vals = gate_pre.astype(jnp.float32)
    sigmoid_gate = jax.nn.sigmoid(gate_vals)
    activated = gate_vals * sigmoid_gate
    return (gate_vals, sigmoid_gate, activated)


def weight_part(hidden, grad_all):
    summed = lax.dot_general(
        lax.all_gather(hidden, "dp", axis=0, tiled=True),
        grad_all,
        (((0,), (0,)), ((), ())),
        preferred_element_type=jnp.float32,
    )
    return summed * grad_all.shape[0] ** (-0.5)


def hidden_part(grad_all, down_weight):
    return lax.psum_scatter(
        lax.dot_general(
            grad_all, down_weight, (((1,), (1,)), ((), ())), preferred_element_type=jnp.float32
        ),
        "dp",
        scatter_dimension=0,
        tiled=True,
    )


def shards(gate_pre, up_pre, out_grad, down_weight):
    gate_vals, sigmoid_gate, activated = activate(gate_pre)
    up_vals = up_pre.astype(jnp.float32)
    hidden = (activated * up_vals).astype(jnp.bfloat16)
    grad_all = lax.all_gather(out_grad, "tensor", axis=0, tiled=True)
    hidden_grad = hidden_part(grad_all, down_weight)
    weight_grad = weight_part(hidden, grad_all)
    gate_grad = (
        hidden_grad * up_vals * sigmoid_gate * (1.0 + gate_vals * (1.0 - sigmoid_gate))
    ).astype(jnp.bfloat16)
    up_grad = (hidden_grad * activated).astype(jnp.bfloat16)
    return (gate_grad, up_grad, weight_grad)


def solution(mesh):
    placed = (P("dp", "tensor"), P("dp", "tensor"), P("tensor", "dp"), P("tensor", "dp"))
    return jax.shard_map(
        shards,
        mesh=mesh,
        in_specs=placed,
        out_specs=(P("dp", "tensor"), P("dp", "tensor"), P("tensor", "dp")),
        check_vma=False,
    )
```

profile of v0, /device:TPU:6, one launch (start us, length us, event | category | flops | bytes accessed | tf_op | source)
XLA Modules:
  0.0 362.8 jit_solution(10779584052765445997)
XLA Ops:
  7.2 0.0 copy-start
  7.2 0.0 all-gather.3.cloned.1.call-start
  7.2 0.7 all-gather.3.cloned.1.call-update
  7.9 0.0 reduce-scatter.2.cloned.1.call-start
  8.0 69.2 %all-gather.3.cloned.1.call-done = bf16[2048,512]{1,0:T(8,128)(2,1)} async-done(((bf16[128,512]{1,0:T(8,128)(2,1)}), bf16[2048,512]{1,0:T(8,128)(2,1)}) %all-gather.3.cloned.1.call-update) | async-done | bytes 2097168 | tf_op jit(solution)/shard_map/all_gather | solution.py:39
  77.1 0.0 copy-done
  77.1 4.8 %fusion.8 = f32[2048,416]{1,0:T(8,128)} fusion(bf16[2048,512]{1,0:T(8,128)(2,1)} %all-gather.3.cloned.1.call-done, bf16[416,512]{1,0:T(8,128)(2,1)S(1)} %copy-done), kind=kOutput, calls=%fused_computation.15 | convolution fusion | flops 872415232 | bytes 5931008 | tf_op jit(solution)/shard_map/dot_general | solution.py:26
  82.0 0.0 copy-start.2
  82.0 0.0 copy-start.3
  82.0 0.0 copy-start.1
  82.0 0.0 reduce-scatter.2.cloned.1.call-update
  82.0 0.0 all-gather.5.cloned.1.call-start
  82.1 143.4 %reduce-scatter.2.cloned.1.call-done = f32[64,416]{1,0:T(8,128)} async-done(((f32[2048,416]{1,0:T(8,128)}), f32[64,416]{1,0:T(8,128)}) %reduce-scatter.2.cloned.1.call-update) | async-done | bytes 106512 | tf_op jit(solution)/shard_map/reduce_scatter | solution.py:25
  225.5 0.0 copy-done.2
  225.5 0.0 copy-done.3
  225.5 1.7 multiply_convert_fusion
  227.1 0.0 all-gather.5.cloned.1.call-update
  227.2 125.5 %all-gather.5.cloned.1.call-done = bf16[2048,416]{1,0:T(8,128)(2,1)} async-done(((bf16[64,416]{1,0:T(8,128)(2,1)}), bf16[2048,416]{1,0:T(8,128)(2,1)}) %all-gather.5.cloned.1.call-update) | async-done | bytes 1703952 | tf_op jit(solution)/shard_map/all_gather | solution.py:16
  352.7 0.0 copy-done.1
  352.7 3.6 convolution_multiply_fusion
Async XLA Ops:
  7.2 70.0 %copy-start = (bf16[416,512]{1,0:T(8,128)(2,1)S(1)}, bf16[416,512]{1,0:T(8,128)(2,1)}, u32[]{:S(2)}) copy-start(bf16[416,512]{1,0:T(8,128)(2,1)} %param.7) | copy-start | bytes 1277956
  7.2 70.0 %all-gather.3.cloned.1.call-start = ((), (), s32[]{:S(2)}) async-start(), calls=%async_computation.1 | async-start | bytes 2228224 | tf_op jit(solution)/shard_map/all_gather | solution.py:39
  7.9 217.6 %reduce-scatter.2.cloned.1.call-start = ((), (), s32[]{:S(2)}) async-start(), calls=%async_computation.2 | async-start | bytes 4325376 | tf_op jit(solution)/shard_map/reduce_scatter | solution.py:25
  82.0 143.5 %copy-start.2 = (bf16[64,416]{1,0:T(8,128)(2,1)S(1)}, bf16[64,416]{1,0:T(8,128)(2,1)}, u32[]{:S(2)}) copy-start(bf16[64,416]{1,0:T(8,128)(2,1)} %param.4) | copy-start | bytes 159748
  82.0 143.5 %copy-start.3 = (bf16[64,416]{1,0:T(8,128)(2,1)S(1)}, bf16[64,416]{1,0:T(8,128)(2,1)}, u32[]{:S(2)}) copy-start(bf16[64,416]{1,0:T(8,128)(2,1)} %param.5) | copy-start | bytes 159748
  82.0 270.7 %copy-start.1 = (bf16[2048,512]{1,0:T(8,128)(2,1)S(1)}, bf16[2048,512]{1,0:T(8,128)(2,1)}, u32[]{:S(2)}) copy-start(bf16[2048,512]{1,0:T(8,128)(2,1)} %all-gather.3.cloned.1.call-done) | copy-start | bytes 6291460
  82.0 270.7 %all-gather.5.cloned.1.call-start = ((), (), s32[]{:S(2)}) async-start(), calls=%async_computation.3 | async-start | bytes 2162688 | tf_op jit(solution)/shard_map/all_gather | solution.py:16
Sparse Core Ops, SparseCore 0:
  11.4 65.7 all-gather.2
  82.1 143.3 reduce-scatter.1
  228.1 124.4 all-gather.4
where the time goes:
time: 364 us; the launch traced here: 363 us
  waiting for transfers between devices  339 us (93%)
  between operations  13.8 us (4%)
  matrix products  8.39 us (2%)
    reduce_scatter x1, waiting for transfers between devices, hidden_part(): lax.psum_scatter(lax.dot_general(grad_all, down_weight, (((1,), (1,)), ((...  143 us
    all_gather x1, waiting for transfers between devices, weight_part(): lax.all_gather(hidden, 'dp', axis=0, tiled=True)  125 us
    all_gather x1, waiting for transfers between devices, shards(): grad_all = lax.all_gather(out_grad, 'tensor', axis=0, tiled=True)  69.2 us
  transfers between devices with their start and end apart: 3, of which 3 were waited for; matrix products, arithmetic and copies ran while one was open for 0% of the time, Pallas kernels for 0%

commit v1 on v0

v1 whole, which is shorter than its diff:
```python
import jax
import jax.numpy as jnp
import numpy as np
from jax import lax
from jax.sharding import Mesh, PartitionSpec as P

Z = ("z3", "z2", "z1", "z0")
DP = ("xl",) + Z
YX = ("y1", "y0", "xh")
TENSOR = YX + ("c",)
SWAP = [(0, 1), (1, 0)]


def to_half(rows):
    top = jnp.max(jnp.abs(rows), axis=-1, keepdims=True)
    exponent = jnp.floor(jnp.log2(jnp.maximum(top, 1e-37)))
    scaled = (rows * jnp.exp2(-exponent)).astype(jnp.float16)
    return jnp.concatenate([scaled, exponent.astype(jnp.float16)], axis=-1)


def from_half(coded):
    return coded[..., :-1].astype(jnp.float32) * jnp.exp2(coded[..., -1:].astype(jnp.float32))


def times(grad, weight):
    return lax.dot_general(
        grad, weight, (((grad.ndim - 1,), (1,)), ((), ())), preferred_element_type=jnp.float32
    )


def shards(gate_pre, up_pre, out_grad, down_weight):
    xl, c = lax.axis_index("xl"), lax.axis_index("c")
    rows, hid = gate_pre.shape
    feats = out_grad.shape[1]
    gate_vals = gate_pre.astype(jnp.float32)
    sigmoid_gate = jax.nn.sigmoid(gate_vals)
    activated = gate_vals * sigmoid_gate
    up_vals = up_pre.astype(jnp.float32)
    hidden = (activated * up_vals).astype(jnp.bfloat16)

    theirs = lax.ppermute(hidden, "xl", SWAP)
    pair = jnp.where(xl == 0, jnp.stack([hidden, theirs]), jnp.stack([theirs, hidden]))
    hidden_all = lax.all_gather(pair, Z, axis=0)

    mine = lax.all_to_all(jnp.broadcast_to(out_grad[None], (8,) + out_grad.shape), YX, 0, 0)
    other = lax.ppermute(mine, "c", SWAP)
    grad_all = jnp.where(c == 0, jnp.stack([mine, other], 1), jnp.stack([other, mine], 1))
    halves = grad_all.reshape(2, 16 * rows, feats)

    sent = times(lax.dynamic_index_in_dim(halves, 1 - xl, 0, False), down_weight)
    got = lax.ppermute(to_half(sent), "xl", SWAP)
    kept = times(lax.dynamic_index_in_dim(halves, xl, 0, False), down_weight)
    summed = to_half(kept + from_half(got)).reshape(16, rows, hid + 1)
    hidden_grad = jnp.sum(from_half(lax.all_to_all(summed, Z, 0, 0)), axis=0)

    gate_grad = (
        hidden_grad * up_vals * sigmoid_gate * (1.0 + gate_vals * (1.0 - sigmoid_gate))
    ).astype(jnp.bfloat16)
    up_grad = (hidden_grad * activated).astype(jnp.bfloat16)

    tokens = hidden_all.transpose(1, 0, 2, 3).reshape(32 * rows, hid)
    weight_grad = lax.dot_general(
        tokens, grad_all.reshape(32 * rows, feats), (((0,), (0,)), ((), ())), preferred_element_type=jnp.float32
    ) * (32 * rows) ** (-0.5)
    return (gate_grad, up_grad, weight_grad)


def solution(mesh):
    bits = Mesh(np.asarray(mesh.devices).reshape((2,) * 9), DP + TENSOR)
    return jax.shard_map(
        shards,
        mesh=bits,
        in_specs=(P(DP, TENSOR), P(DP, TENSOR), P(TENSOR, DP), P(TENSOR, DP)),
        out_specs=(P(DP, TENSOR), P(DP, TENSOR), P(TENSOR, DP)),
        check_vma=False,
    )
```

time: 364 us -> 223 us (0.61)
  waiting for transfers between devices: 339 us -> 93.8 us
  blocking collectives: 0 us -> 87.6 us
  other arithmetic: 1.66 us -> 8.96 us
  starting transfers between devices: 0.12 us -> 7.42 us
  local copies, waits for them, and re-layouts: 0.02 us -> 5.86 us
  matrix products: 8.39 us -> 4.44 us
    reduce_scatter x1 -> x0, waiting for transfers between devices: 143 us -> none  [hidden_part(): lax.psum_scatter(lax.dot_general(grad_all, down_weight, (((1,), (1,)), ((...]
    all_gather x2 -> x1, waiting for transfers between devices: 195 us -> 67.2 us  [shards(): hidden_all = lax.all_gather(pair, Z, axis=0)]
    all_to_all x0 -> x2, blocking collectives: none -> 87.6 us  [the longest x1 65.9 us: shards(): hidden_grad = jnp.sum(from_half(lax.all_to_all(summed, Z, 0, 0)), axis=0)]
    ppermute x0 -> x3, waiting for transfers between devices: none -> 26.6 us  [the longest x1 20.6 us: shards(): got = lax.ppermute(to_half(sent), 'xl', SWAP)]
    ppermute x0 -> x3, starting transfers between devices: none -> 7.38 us  [the longest x1 2.74 us: shards(): got = lax.ppermute(to_half(sent), 'xl', SWAP)]
    dot_general x2 -> x3, matrix products: 8.39 us -> 4.44 us  [the longest x2 2.46 us: times(): lax.dot_general(grad, weight, (((grad.ndim - 1,), (1,)), ((), ())), prefe...]
  transfers between devices with their start and end apart: 3 -> 4, of which waited for: 3 -> 4; matrix products, arithmetic and copies ran while one was open for 0% -> 0% of each run, Pallas kernels for 0% -> 0%
where the time goes in v1:
time: 223 us; the launch traced here: 222 us
  waiting for transfers between devices  93.8 us (42%)
  blocking collectives  87.6 us (39%)
  between operations  14.2 us (6%)
  other arithmetic  8.96 us (4%)
  starting transfers between devices  7.42 us (3%)
  local copies, waits for them, and re-layouts  5.86 us (3%)
  matrix products  4.44 us (2%)
    all_gather x1, waiting for transfers between devices, shards(): hidden_all = lax.all_gather(pair, Z, axis=0)  67.2 us
    all_to_all x1, blocking collectives, shards(): hidden_grad = jnp.sum(from_half(lax.all_to_all(summed, Z, 0, 0)), axis=0)  65.9 us
    all_to_all x1, blocking collectives, shards(): lax.all_to_all(jnp.broadcast_to(out_grad[None], (8,) + out_grad.shape), Y...  21.8 us
    ppermute x1, waiting for transfers between devices, shards(): got = lax.ppermute(to_half(sent), 'xl', SWAP)  20.6 us
  transfers between devices with their start and end apart: 4, of which 4 were waited for; matrix products, arithmetic and copies ran while one was open for 0% of the time, Pallas kernels for 0%

profile of v1, /device:TPU:6, one launch (start us, length us, event | category | flops | bytes accessed | tf_op | source)
XLA Modules:
  0.0 222.3 jit_solution(5873937109698178302)
XLA Ops:
  7.2 0.0 copy-start
  7.2 0.0 all-gather.2.cloned.1.call-start
  7.2 1.0 broadcast_in_dim.2
  8.3 21.8 %all_to_all.10 = bf16[8,128,512]{2,1,0:T(8,128)(2,1)S(1)} all-to-all(bf16[8,128,512]{2,1,0:T(8,128)(2,1)S(1)} %broadcast_in_dim.2), channel_id=1, replica_groups=mesh['xl'=2,'z3'=2,'z2'=2,'z1'=2,'z0'=2,'y1'=2,'y0'=2,'xh'=2,'c'=2] {'y1..., dimensions={0} | all-to-all | bytes 2097152 | tf_op jit(solution)/shard_map/all_to_all | solution.py:45
  30.0 1.9 collective-permute-start
  32.0 2.6 %collective-permute-done = bf16[8,128,512]{2,1,0:T(8,128)(2,1)S(1)} collective-permute-done((bf16[8,128,512]{2,1,0:T(8,128)(2,1)S(1)}, bf16[8,128,512]{2,1,0:T(8,128)(2,1)S(1)}, u32[]{:S(2)}, u32[]{:S(2)}) %collective-permute-start) | collective-permute-done | bytes 1048608 | tf_op jit(solution)/shard_map/ppermute | solution.py:46
  34.6 1.0 copy-done.2
  35.5 2.6 %maximum_select_fusion = bf16[8,2,128,512]{3,2,1,0:T(8,128)(2,1)S(1)} fusion(bf16[8,1,128,512]{3,2,1,0:T(8,128)(2,1)} %bitcast.31, bf16[8,1,128,512]{3,2,1,0:T(8,128)(2,1)} %bitcast.27, pred[]{:T(512)S(6)} %eq.6), kind=kLoop, calls=%fused_computation | loop fusion | flops 3145728 | bytes 4194305 | tf_op jit(solution)/shard_map/jit(_where)/select_n | solution.py:47
  38.1 0.7 abs_reduce_fusion.1
  38.8 0.2 multiply_convert_fusion.1
  39.0 0.2 pad_maximum_fusion.1
  39.3 2.7 %collective-permute-start.1 = (f16[1024,417]{0,1:T(8,128)(2,1)S(1)}, f16[1024,417]{0,1:T(8,128)(2,1)}, u32[]{:S(2)}, u32[]{:S(2)}) collective-permute-start(f16[1024,417]{0,1:T(8,128)(2,1)S(1)} %pad_maximum_fusion.1), channel_id=1, source_target_pairs={{0,256},{256,0},{1,257},{257,1},{2,258},{258,2},{3,259},{259,3},{4... | collective-permute-start | bytes 2562056 | tf_op jit(solution)/shard_map/ppermute | solution.py:51
  42.0 20.6 %collective-permute-done.1 = f16[1024,417]{0,1:T(8,128)(2,1)} collective-permute-done((f16[1024,417]{0,1:T(8,128)(2,1)S(1)}, f16[1024,417]{0,1:T(8,128)(2,1)}, u32[]{:S(2)}, u32[]{:S(2)}) %collective-permute-start.1) | collective-permute-done | bytes 854048 | tf_op jit(solution)/shard_map/ppermute | solution.py:51
  62.6 0.7 fusion.15
  63.3 1.8 abs_reduce_fusion
  65.2 1.5 multiply_convert_fusion
  66.7 1.6 copy.12
  68.3 0.5 floor.40
  68.7 1.6 pad_maximum_fusion
  70.3 0.0 copy-start.3
  70.3 0.0 copy-start.4
  70.3 65.9 %all_to_all.11 = f16[16,64,417]{2,1,0:T(8,128)(2,1)S(1)} all-to-all(f16[16,64,417]{2,1,0:T(8,128)(2,1)S(1)} %pad_maximum_fusion), channel_id=1, replica_groups=mesh['xl'=2,'z3'=2,'z2'=2,'z1'=2,'z0'=2,'y1'=2,'y0'=2,'xh'=2,'c'=2] {'z3..., dimensions={0} | all-to-all | bytes 1708032 | tf_op jit(solution)/shard_map/all_to_all | solution.py:54
  136.2 0.4 exponential_reduce_fusion
  136.6 0.3 multiply_reduce_fusion
  136.9 0.7 multiply_convert_fusion.2
  137.6 2.7 %collective-permute-start.2 = (bf16[64,416]{1,0:T(8,128)(2,1)S(1)}, bf16[64,416]{1,0:T(8,128)(2,1)S(1)}, u32[]{:S(2)}, u32[]{:S(2)}) collective-permute-start(bf16[64,416]{1,0:T(8,128)(2,1)S(1)} %get-tuple-element.5), channel_id=1, source_target_pairs={{0,256},{256,0},{1,257},{257,1},{2,258},{258,2},{3,259},{259,3},{4... | collective-permute-start | bytes 159752 | tf_op jit(solution)/shard_map/ppermute | solution.py:41
  140.4 3.4 %collective-permute-done.2 = bf16[64,416]{1,0:T(8,128)(2,1)S(1)} collective-permute-done((bf16[64,416]{1,0:T(8,128)(2,1)S(1)}, bf16[64,416]{1,0:T(8,128)(2,1)S(1)}, u32[]{:S(2)}, u32[]{:S(2)}) %collective-permute-start.2) | collective-permute-done | bytes 53280 | tf_op jit(solution)/shard_map/ppermute | solution.py:41
  143.8 0.7 maximum_select_fusion.1
  144.5 0.0 all-gather.2.cloned.1.call-update
  144.5 67.2 %all-gather.2.cloned.1.call-done = bf16[16,2,64,416]{3,2,1,0:T(8,128)(2,1)} async-done(((bf16[1,2,64,416]{3,2,1,0:T(8,128)(2,1)}), bf16[16,2,64,416]{3,2,1,0:T(8,128)(2,1)}) %all-gather.2.cloned.1.call-update) | async-done | bytes 1703952 | tf_op jit(solution)/shard_map/all_gather | solution.py:43
  211.7 1.8 copy.14
  213.5 2.0 convolution_multiply_fusion
  (9 shorter events, 0.0 us)
Async XLA Ops:
  7.2 30.9 %copy-start = (bf16[416,512]{1,0:T(8,128)(2,1)S(1)}, bf16[416,512]{1,0:T(8,128)(2,1)}, u32[]{:S(2)}) copy-start(bf16[416,512]{1,0:T(8,128)(2,1)} %param.7) | copy-start | bytes 1277956
  7.2 204.5 %all-gather.2.cloned.1.call-start = ((), (), s32[]{:S(2)}) async-start(), calls=%async_computation.2 | async-start | bytes 2228224 | tf_op jit(solution)/shard_map/all_gather | solution.py:43
  30.0 4.5 %copy-start.1 = (bf16[8,128,512]{2,1,0:T(8,128)(2,1)}, bf16[8,128,512]{2,1,0:T(8,128)(2,1)S(1)}, u32[]{:S(2)}) copy-start(bf16[8,128,512]{2,1,0:T(8,128)(2,1)S(1)} %all_to_all.10) | copy-start | bytes 3145732
  30.0 4.5 %collective-permute-start = (bf16[8,128,512]{2,1,0:T(8,128)(2,1)S(1)}, bf16[8,128,512]{2,1,0:T(8,128)(2,1)S(1)}, u32[]{:S(2)}, u32[]{:S(2)}) collective-permute-start(bf16[8,128,512]{2,1,0:T(8,128)(2,1)S(1)} %all_to_all.10), channel_id=1, source_target_pairs={{0,1},{1,0},{2,3},{3,2},{4,5},{5,4},{6,7},{7,6},{8,9},{9,8},{10,11... | collective-permute-start | bytes 3145736 | tf_op jit(solution)/shard_map/ppermute | solution.py:46
  34.6 1.0 copy-start.2
  39.3 23.3 %collective-permute-start.1 = (f16[1024,417]{0,1:T(8,128)(2,1)S(1)}, f16[1024,417]{0,1:T(8,128)(2,1)}, u32[]{:S(2)}, u32[]{:S(2)}) collective-permute-start(f16[1024,417]{0,1:T(8,128)(2,1)S(1)} %pad_maximum_fusion.1), channel_id=1, source_target_pairs={{0,256},{256,0},{1,257},{257,1},{2,258},{258,2},{3,259},{259,3},{4... | collective-permute-start | bytes 2562056 | tf_op jit(solution)/shard_map/ppermute | solution.py:51
  70.3 66.6 %copy-start.3 = (bf16[64,416]{1,0:T(8,128)(2,1)S(1)}, bf16[64,416]{1,0:T(8,128)(2,1)}, u32[]{:S(2)}) copy-start(bf16[64,416]{1,0:T(8,128)(2,1)} %param.4) | copy-start | bytes 159748
  70.3 66.6 %copy-start.4 = (bf16[64,416]{1,0:T(8,128)(2,1)S(1)}, bf16[64,416]{1,0:T(8,128)(2,1)}, u32[]{:S(2)}) copy-start(bf16[64,416]{1,0:T(8,128)(2,1)} %param.5) | copy-start | bytes 159748
  137.6 6.1 %collective-permute-start.2 = (bf16[64,416]{1,0:T(8,128)(2,1)S(1)}, bf16[64,416]{1,0:T(8,128)(2,1)S(1)}, u32[]{:S(2)}, u32[]{:S(2)}) collective-permute-start(bf16[64,416]{1,0:T(8,128)(2,1)S(1)} %get-tuple-element.5), channel_id=1, source_target_pairs={{0,256},{256,0},{1,257},{257,1},{2,258},{258,2},{3,259},{259,3},{4... | collective-permute-start | bytes 159752 | tf_op jit(solution)/shard_map/ppermute | solution.py:41
Sparse Core Ops, SparseCore 0:
  144.6 66.9 all-gather.1

commit v2 on v1

v2 whole, which is shorter than its diff:
```python
import functools

import jax
import jax.numpy as jnp
import numpy as np
from jax import lax
from jax.experimental import pallas as pl
from jax.experimental.pallas import tpu as pltpu
from jax.sharding import Mesh, PartitionSpec as P

Z = ("z3", "z2", "z1", "z0")
FAR = Z[:2]
DP = ("xl",) + Z
YX = ("y1", "y0", "xh")
TENSOR = YX + ("c",)
SWAP = [(0, 1), (1, 0)]
LANES = 128
VMEM_BYTES = 32 * 1024 * 1024
whole = pl.BlockSpec(memory_space=pltpu.VMEM)
scalars = pl.BlockSpec(memory_space=pltpu.SMEM)


def pack(block):
    tail = block[:, 3 * LANES :]
    packed = tail[0:16]
    for k in range(1, 4):
        packed += pltpu.roll(tail[16 * k : 16 * k + 16], 32 * k, 1)
    return jnp.concatenate([block[:, LANES * k : LANES * (k + 1)] for k in range(3)] + [packed], axis=0)


def encode(packed):
    top = jnp.max(jnp.max(jnp.abs(packed), axis=0, keepdims=True), axis=1, keepdims=True)
    exponent = jnp.floor(jnp.log2(jnp.maximum(top, 1e-37)))
    scaled = packed * jnp.exp2(-exponent)
    return jnp.concatenate([scaled, jnp.broadcast_to(exponent, (16, LANES))], axis=0)


def decode(coded):
    return coded[:208] * jnp.exp2(coded[208:209])


def times(rows, weight):
    return lax.dot_general(rows, weight, (((1,), (1,)), ((), ())), preferred_element_type=jnp.float32)


def send_kernel(place_ref, rows_ref, weight_ref, out_ref, padded):
    hid = weight_ref.shape[0]
    padded[hid:] = jnp.zeros_like(padded[hid:])
    padded[:hid] = weight_ref[...]
    rows = rows_ref[pl.ds((1 - place_ref[0]) * 4, 4)].reshape(512, rows_ref.shape[2])
    product = times(rows, padded[...])
    for far in range(4):
        for half in range(2):
            start = far * 128 + half * 64
            out_ref[half, far] = encode(pack(product[start : start + 64]))


def send_part(place, rows, weight):
    return pl.pallas_call(
        send_kernel,
        out_shape=jax.ShapeDtypeStruct((2, 4, 224, LANES), jnp.float32),
        in_specs=[scalars] + [whole] * 2,
        out_specs=whole,
        scratch_shapes=[pltpu.VMEM((512, weight.shape[1]), weight.dtype)],
        compiler_params=pltpu.CompilerParams(vmem_limit_bytes=VMEM_BYTES),
        cost_estimate=pl.CostEstimate(flops=2 * 512 * 512 * 512, bytes_accessed=2 << 20, transcendentals=0),
        name="send_part",
    )(place, rows, weight)


def keep_kernel(place_ref, mine_ref, other_ref, weight_ref, got_mine_ref, got_other_ref, out_ref, padded):
    hid = weight_ref.shape[0]
    padded[hid:] = jnp.zeros_like(padded[hid:])
    padded[:hid] = weight_ref[...]
    xl, c = place_ref[0], place_ref[1]
    for ref, got_ref, core in ((mine_ref, got_mine_ref, c), (other_ref, got_other_ref, 1 - c)):
        rows = ref[pl.ds(xl * 4, 4)].reshape(512, ref.shape[2])
        product = times(rows, padded[...])
        for far in range(4):
            for half in range(2):
                start = far * 128 + half * 64
                vals = pack(product[start : start + 64]) + decode(got_ref[half, far])
                out_ref[core, half, far] = encode(vals)


def keep_part(place, mine, other, weight, got_mine, got_other):
    return pl.pallas_call(
        keep_kernel,
        out_shape=jax.ShapeDtypeStruct((2, 2, 4, 224, LANES), jnp.float32),
        in_specs=[scalars] + [whole] * 5,
        out_specs=whole,
        scratch_shapes=[pltpu.VMEM((512, weight.shape[1]), weight.dtype)],
        compiler_params=pltpu.CompilerParams(vmem_limit_bytes=VMEM_BYTES),
        cost_estimate=pl.CostEstimate(flops=2 * 1024 * 512 * 512, bytes_accessed=4 << 20, transcendentals=0),
        name="keep_part",
    )(place, mine, other, weight, got_mine, got_other)


def merge_kernel(place_ref, got_ref, own_ref, *out_refs):
    for k in range(4):
        far = lax.rem(place_ref[2] + k, 4)
        vals = decode(got_ref[0, far])
        for near in range(1, 4):
            vals += decode(got_ref[near, far])
        if k == 0:
            own_ref[...] = vals
        else:
            out_refs[k - 1][...] = encode(vals)


def merge(place, got):
    return pl.pallas_call(
        merge_kernel,
        out_shape=(jax.ShapeDtypeStruct((208, LANES), jnp.float32),)
        + (jax.ShapeDtypeStruct((224, LANES), jnp.float32),) * 3,
        in_specs=[scalars, whole],
        out_specs=(whole,) * 4,
        compiler_params=pltpu.CompilerParams(vmem_limit_bytes=VMEM_BYTES),
        cost_estimate=pl.CostEstimate(flops=1 << 20, bytes_accessed=1 << 20, transcendentals=0),
        name="merge_parts",
    )(place, got)


def final_kernel(own_ref, a_ref, b_ref, d_ref, gate_ref, up_ref, gate_grad_ref, up_grad_ref):
    packed = own_ref[...] + decode(a_ref[...]) + decode(b_ref[...]) + decode(d_ref[...])
    tail = packed[192:208]
    tails = jnp.concatenate([tail] + [pltpu.roll(tail, LANES - 32 * k, 1) for k in range(1, 4)], axis=0)
    width = gate_ref.shape[1]
    for k in range(4):
        cols = slice(LANES * k, min(LANES * (k + 1), width))
        grad = packed[64 * k : 64 * k + 64] if k < 3 else tails[:, : width - 3 * LANES]
        gate = gate_ref[:, cols].astype(jnp.float32)
        up = up_ref[:, cols].astype(jnp.float32)
        s = jax.nn.sigmoid(gate)
        gate_grad_ref[:, cols] = (grad * up * s * (1.0 + gate * (1.0 - s))).astype(gate_grad_ref.dtype)
        up_grad_ref[:, cols] = (grad * (gate * s)).astype(up_grad_ref.dtype)


def final(parts, gate_pre, up_pre):
    return pl.pallas_call(
        final_kernel,
        out_shape=(jax.ShapeDtypeStruct(gate_pre.shape, gate_pre.dtype),) * 2,
        in_specs=[whole] * 6,
        out_specs=(whole, whole),
        compiler_params=pltpu.CompilerParams(vmem_limit_bytes=VMEM_BYTES),
        cost_estimate=pl.CostEstimate(flops=1, bytes_accessed=1, transcendentals=0),
        name="finish_grads",
    )(*parts, gate_pre, up_pre)


def weight_kernel(place_ref, near_ref, up1_ref, down1_ref, up2_ref, down2_ref, mine_ref, other_ref, out_ref, tokens):
    c, z = place_ref[1], place_ref[3]
    for ref, shift, begin, count in (
        (near_ref, 0, 0, 4),
        (up1_ref, -1, 0, 4),
        (down1_ref, 1, 0, 4),
        (up2_ref, -2, 1, 2),
        (down2_ref, 2, 0, 2),
    ):
        for k in range(count):
            owner = lax.rem(z + shift - 4 * (begin + k - 1) + 32, 16)
            core = lax.rem(owner // 2, 2)
            for xl in range(2):
                start = pl.multiple_of(lax.rem(owner, 2) * 64, 64)
                tokens[xl, core, owner // 4, pl.ds(start, 64)] = ref[k, xl]
    hid = out_ref.shape[0]
    total = None
    for xl in range(2):
        for ref, core in ((mine_ref, c), (other_ref, 1 - c)):
            rows = ref[4 * xl : 4 * xl + 4].reshape(512, ref.shape[2])
            hidden = tokens[xl, core].reshape(512, tokens.shape[4])
            product = lax.dot_general(hidden, rows, (((0,), (0,)), ((), ())), preferred_element_type=jnp.float32)
            total = product if total is None else total + product
    out_ref[...] = total[:hid] * 2048 ** (-0.5)


def weight_part(place, blocks, mine, other, hid):
    return pl.pallas_call(
        weight_kernel,
        out_shape=jax.ShapeDtypeStruct((hid, mine.shape[2]), jnp.float32),
        in_specs=[scalars] + [whole] * 7,
        out_specs=whole,
        scratch_shapes=[pltpu.VMEM((2, 2, 4, 128, 512), mine.dtype)],
        compiler_params=pltpu.CompilerParams(vmem_limit_bytes=VMEM_BYTES),
        cost_estimate=pl.CostEstimate(flops=2 * 2048 * 512 * 512, bytes_accessed=5 << 20, transcendentals=0),
        name="weight_grad",
    )(place, *blocks, mine, other)


def shift(array, axes, step):
    size = 2 ** len(axes)
    return lax.ppermute(array, axes, [(i, (i + step) % size) for i in range(size)])


def shards(gate_pre, up_pre, out_grad, down_weight):
    xl = lax.axis_index("xl")
    place = jnp.stack([xl, lax.axis_index("c"), lax.axis_index(FAR), lax.axis_index(Z)]).astype(jnp.int32)
    hid = gate_pre.shape[1]
    gate_vals = gate_pre.astype(jnp.float32)
    hidden = (gate_vals * jax.nn.sigmoid(gate_vals) * up_pre.astype(jnp.float32)).astype(jnp.bfloat16)
    hidden = jnp.pad(hidden, ((0, 0), (0, 512 - hid)))

    theirs = lax.ppermute(hidden, "xl", SWAP)
    pair = jnp.where(xl == 0, jnp.stack([hidden, theirs]), jnp.stack([theirs, hidden]))
    steps = [shift(pair, FAR, k) for k in (3, 1, 2)]

    mine = lax.all_to_all(jnp.broadcast_to(out_grad[None], (8,) + out_grad.shape), YX, 0, 0)
    other = lax.ppermute(mine, "c", SWAP)

    sent = [send_part(place, rows, down_weight).astype(jnp.float16) for rows in (mine, other)]
    sent, pair, steps = lax.optimization_barrier((sent, pair, steps))
    got = [lax.ppermute(s, "xl", SWAP) for s in sent]

    near = jnp.stack([steps[0], pair, steps[1], steps[2]])
    blocks = [near, shift(near, Z, 1), shift(near, Z, -1), shift(near[1:3], Z, 2), shift(near[0:2], Z, -2)]
    got, blocks = lax.optimization_barrier((got, blocks))

    kept = keep_part(place, mine, other, down_weight, *[g.astype(jnp.float32) for g in got])
    kept = kept.astype(jnp.float16).reshape(4, 4, 224, LANES)
    merged = merge(place, lax.all_to_all(kept, ("z1", "z0"), 0, 0).astype(jnp.float32))
    far = [shift(merged[k].astype(jnp.float16), FAR, k).astype(jnp.float32) for k in range(1, 4)]
    gate_grad, up_grad = final([merged[0]] + far, gate_pre, up_pre)

    weight_grad = weight_part(place, blocks, mine, other, hid)
    return (gate_grad, up_grad, weight_grad)


def solution(mesh):
    bits = Mesh(np.asarray(mesh.devices).reshape((2,) * 9), DP + TENSOR)
    return jax.shard_map(
        shards,
        mesh=bits,
        in_specs=(P(DP, TENSOR), P(DP, TENSOR), P(TENSOR, DP), P(TENSOR, DP)),
        out_specs=(P(DP, TENSOR), P(DP, TENSOR), P(TENSOR, DP)),
        check_vma=False,
    )
```

time: 223 us -> 161 us (0.72)
  the two profiles are of different devices: /device:TPU:6 before, /device:TPU:1 now
where the time goes in v2:
time: 161 us
  starting transfers between devices  67.6 us (42%)
  blocking collectives  48.4 us (30%)
  waiting for transfers between devices  33.5 us (21%)
  Pallas kernels  8.35 us (5%)
    ppermute x10, starting transfers between devices, shift(): lax.ppermute(array, axes, [(i, (i + step) % size) for i in range(size)])  54.9 us
    ppermute x10, waiting for transfers between devices, shift(): lax.ppermute(array, axes, [(i, (i + step) % size) for i in range(size)])  28.4 us
    all_to_all x1, blocking collectives, shards(): lax.all_to_all(kept, ('z1', 'z0'), 0, 0).astype(jnp.float32)  26.2 us
    all_to_all x1, blocking collectives, shards(): lax.all_to_all(jnp.broadcast_to(out_grad[None], (8,) + out_grad.shape), Y...  22.2 us
    ppermute x2, starting transfers between devices, shards(): got = [lax.ppermute(s, 'xl', SWAP) for s in sent]  5.28 us
    ppermute x1, starting transfers between devices, shards(): other = lax.ppermute(mine, 'c', SWAP)  5.14 us
    ppermute x1, waiting for transfers between devices, shards(): theirs = lax.ppermute(hidden, 'xl', SWAP)  3.27 us
  transfers between devices with their start and end apart: 14, of which 6 were waited for; matrix products, arithmetic and copies ran while one was open for 0% of the time, Pallas kernels for 3%

profile of v2, /device:TPU:1, one launch (start us, length us, event | category | flops | bytes accessed | tf_op | source)
XLA Modules:
  0.0 160.8 jit_solution(16638976291303783413)
XLA Ops:
  0.7 1.0 broadcast_in_dim.2
  1.7 22.2 %all_to_all.10.rows_ref.mine_ref = bf16[8,128,512]{2,1,0:T(8,128)(2,1)S(1)} all-to-all(bf16[8,128,512]{2,1,0:T(8,128)(2,1)S(1)} %broadcast_in_dim.2), channel_id=1, replica_groups=mesh['xl'=2,'z3'=2,'z2'=2,'z1'=2,'z0'=2,'y1'=2,'y0'=2,'xh'=2,'c'=2] {'y1..., dimensions={0} | all-to-all | bytes 2097152 | tf_op jit(solution)/shard_map/all_to_all | solution.py:207
  23.9 5.1 %collective-permute-start = (bf16[8,128,512]{2,1,0:T(8,128)(2,1)S(1)}, bf16[8,128,512]{2,1,0:T(8,128)(2,1)S(1)}, u32[]{:S(2)}, u32[]{:S(2)}) collective-permute-start(bf16[8,128,512]{2,1,0:T(8,128)(2,1)S(1)} %all_to_all.10.rows_ref.mine_ref), channel_id=1, source_target_pairs={{0,1},{1,0},{2,3},{3,2},{4,5},{5,4},{6,7},{7,6},{8,9},{9,8},{10,11... | collective-permute-start | bytes 3145736 | tf_op jit(solution)/shard_map/ppermute | solution.py:208
  29.1 2.3 %collective-permute-start.1 = (bf16[64,512]{1,0:T(8,128)(2,1)S(1)}, bf16[64,512]{1,0:T(8,128)(2,1)S(1)}, u32[]{:S(2)}, u32[]{:S(2)}) collective-permute-start(bf16[64,512]{1,0:T(8,128)(2,1)S(1)} %get-tuple-element.44), channel_id=1, source_target_pairs={{0,256},{256,0},{1,257},{257,1},{2,258},{258,2},{3,259},{259,3},{4... | collective-permute-start | bytes 196616 | tf_op jit(solution)/shard_map/ppermute | solution.py:203
  31.5 3.3 %collective-permute-done.1 = bf16[64,512]{1,0:T(8,128)(2,1)S(1)} collective-permute-done((bf16[64,512]{1,0:T(8,128)(2,1)S(1)}, bf16[64,512]{1,0:T(8,128)(2,1)S(1)}, u32[]{:S(2)}, u32[]{:S(2)}) %collective-permute-start.1) | collective-permute-done | bytes 65568 | tf_op jit(solution)/shard_map/ppermute | solution.py:203
  34.8 15.4 %collective-permute-start.4 = (bf16[2,64,512]{2,1,0:T(8,128)(2,1)S(1)}, bf16[2,64,512]{2,1,0:T(8,128)(2,1)S(1)}, u32[]{:S(2)}, u32[]{:S(2)}) collective-permute-start(bf16[2,64,512]{2,1,0:T(8,128)(2,1)S(1)} %maximum_select_fusion), channel_id=1, source_target_pairs={{0,128},{64,192},{128,0},{192,64},{1,129},{65,193},{129,1},{193,65... | collective-permute-start | bytes 393224 | tf_op jit(solution)/shard_map/ppermute | solution.py:192
  50.2 4.0 %collective-permute-start.3 = (bf16[2,64,512]{2,1,0:T(8,128)(2,1)S(1)}, bf16[2,64,512]{2,1,0:T(8,128)(2,1)S(1)}, u32[]{:S(2)}, u32[]{:S(2)}) collective-permute-start(bf16[2,64,512]{2,1,0:T(8,128)(2,1)S(1)} %maximum_select_fusion), channel_id=1, source_target_pairs={{0,64},{64,128},{128,192},{192,0},{1,65},{65,129},{129,193},{193,1... | collective-permute-start | bytes 393224 | tf_op jit(solution)/shard_map/ppermute | solution.py:192
  54.2 5.2 %collective-permute-start.2 = (bf16[2,64,512]{2,1,0:T(8,128)(2,1)S(1)}, bf16[2,64,512]{2,1,0:T(8,128)(2,1)S(1)}, u32[]{:S(2)}, u32[]{:S(2)}) collective-permute-start(bf16[2,64,512]{2,1,0:T(8,128)(2,1)S(1)} %maximum_select_fusion), channel_id=1, source_target_pairs={{0,192},{64,0},{128,64},{192,128},{1,193},{65,1},{129,65},{193,129... | collective-permute-start | bytes 393224 | tf_op jit(solution)/shard_map/ppermute | solution.py:192
  59.4 0.1 pad_add_fusion.place_ref
  59.5 1.2 send_part.2
  60.8 1.2 send_part.3
  62.1 0.6 collective-permute-done.3
  62.7 11.5 %collective-permute-done.2 = bf16[2,64,512]{2,1,0:T(8,128)(2,1)S(1)} collective-permute-done((bf16[2,64,512]{2,1,0:T(8,128)(2,1)S(1)}, bf16[2,64,512]{2,1,0:T(8,128)(2,1)S(1)}, u32[]{:S(2)}, u32[]{:S(2)}) %collective-permute-start.2) | collective-permute-done | bytes 131104 | tf_op jit(solution)/shard_map/ppermute | solution.py:192
  74.3 5.0 %collective-permute-start.10 = (bf16[2,2,64,512]{3,2,1,0:T(8,128)(2,1)S(1)}, bf16[2,2,64,512]{3,2,1,0:T(8,128)(2,1)S(1)}, u32[]{:S(2)}, u32[]{:S(2)}) collective-permute-start(bf16[2,2,64,512]{3,2,1,0:T(8,128)(2,1)S(1)} %get-tuple-element.41), channel_id=1, source_target_pairs={{0,224},{16,240},{32,0},{48,16},{64,32},{80,48},{96,64},{112,80},{... | collective-permute-start | bytes 786440 | tf_op jit(solution)/shard_map/ppermute | solution.py:192
  79.3 1.9 %collective-permute-start.8 = (bf16[4,2,64,512]{3,2,1,0:T(8,128)(2,1)S(1)}, bf16[4,2,64,512]{3,2,1,0:T(8,128)(2,1)S(1)}, u32[]{:S(2)}, u32[]{:S(2)}) collective-permute-start(bf16[4,2,64,512]{3,2,1,0:T(8,128)(2,1)S(1)} %pad_maximum_fusion.near_ref), channel_id=1, source_target_pairs={{0,240},{16,0},{32,16},{48,32},{64,48},{80,64},{96,80},{112,96},{1... | collective-permute-start | bytes 1572872 | tf_op jit(solution)/shard_map/ppermute | solution.py:192
  81.2 3.4 %collective-permute-start.7 = (bf16[4,2,64,512]{3,2,1,0:T(8,128)(2,1)S(1)}, bf16[4,2,64,512]{3,2,1,0:T(8,128)(2,1)S(1)}, u32[]{:S(2)}, u32[]{:S(2)}) collective-permute-start(bf16[4,2,64,512]{3,2,1,0:T(8,128)(2,1)S(1)} %pad_maximum_fusion.near_ref), channel_id=1, source_target_pairs={{0,16},{16,32},{32,48},{48,64},{64,80},{80,96},{96,112},{112,128},... | collective-permute-start | bytes 1572872 | tf_op jit(solution)/shard_map/ppermute | solution.py:192
  84.6 2.3 %collective-permute-start.5 = (f16[2,4,224,128]{3,2,1,0:T(8,128)(2,1)S(1)}, f16[2,4,224,128]{3,2,1,0:T(8,128)(2,1)S(1)}, u32[]{:S(2)}, u32[]{:S(2)}) collective-permute-start(f16[2,4,224,128]{3,2,1,0:T(8,128)(2,1)S(1)} %convert_element_type.47), channel_id=1, source_target_pairs={{0,256},{256,0},{1,257},{257,1},{2,258},{258,2},{3,259},{259,3},{4... | collective-permute-start | bytes 1376264 | tf_op jit(solution)/shard_map/ppermute | solution.py:212
  86.9 3.0 %collective-permute-start.6 = (f16[2,4,224,128]{3,2,1,0:T(8,128)(2,1)S(1)}, f16[2,4,224,128]{3,2,1,0:T(8,128)(2,1)S(1)}, u32[]{:S(2)}, u32[]{:S(2)}) collective-permute-start(f16[2,4,224,128]{3,2,1,0:T(8,128)(2,1)S(1)} %convert_element_type.48), channel_id=1, source_target_pairs={{0,256},{256,0},{1,257},{257,1},{2,258},{258,2},{3,259},{259,3},{4... | collective-permute-start | bytes 1376264 | tf_op jit(solution)/shard_map/ppermute | solution.py:212
  89.9 2.5 %collective-permute-start.9 = (bf16[2,2,64,512]{3,2,1,0:T(8,128)(2,1)S(1)}, bf16[2,2,64,512]{3,2,1,0:T(8,128)(2,1)S(1)}, u32[]{:S(2)}, u32[]{:S(2)}) collective-permute-start(bf16[2,2,64,512]{3,2,1,0:T(8,128)(2,1)S(1)} %get-tuple-element.42), channel_id=1, source_target_pairs={{0,32},{16,48},{32,64},{48,80},{64,96},{80,112},{96,128},{112,144}... | collective-permute-start | bytes 786440 | tf_op jit(solution)/shard_map/ppermute | solution.py:192
  92.5 12.2 %collective-permute-done.9.up2_ref = bf16[2,2,64,512]{3,2,1,0:T(8,128)(2,1)S(1)} collective-permute-done((bf16[2,2,64,512]{3,2,1,0:T(8,128)(2,1)S(1)}, bf16[2,2,64,512]{3,2,1,0:T(8,128)(2,1)S(1)}, u32[]{:S(2)}, u32[]{:S(2)}) %collective-permute-start.9) | collective-permute-done | bytes 262176 | tf_op jit(solution)/shard_map/ppermute | solution.py:192
  104.6 1.8 %collective-permute-done.6 = f16[2,4,224,128]{3,2,1,0:T(8,128)(2,1)S(1)} collective-permute-done((f16[2,4,224,128]{3,2,1,0:T(8,128)(2,1)S(1)}, f16[2,4,224,128]{3,2,1,0:T(8,128)(2,1)S(1)}, u32[]{:S(2)}, u32[]{:S(2)}) %collective-permute-start.6) | collective-permute-done | bytes 458784 | tf_op jit(solution)/shard_map/ppermute | solution.py:212
  106.6 1.5 keep_part.1
  108.1 0.1 convert_element_type.54
  108.2 26.2 %all_to_all.11 = f16[4,4,224,128]{3,2,1,0:T(8,128)(2,1)S(1)} all-to-all(f16[4,4,224,128]{3,2,1,0:T(8,128)(2,1)S(1)} %bitcast.12), channel_id=1, replica_groups=mesh['xl'=2,'z3'=2,'z2'=2,'z1'=2,'z0'=2,'y1'=2,'y0'=2,'xh'=2,'c'=2] {'z1..., dimensions={0} | all-to-all | bytes 1835008 | tf_op jit(solution)/shard_map/all_to_all | solution.py:220
  134.4 0.2 convert_element_type.55.got_ref
  134.6 0.8 merge_parts.1
  135.4 5.3 %collective-permute-start.13 = (f16[224,128]{1,0:T(8,128)(2,1)S(1)}, f16[224,128]{1,0:T(8,128)(2,1)S(1)}, u32[]{:S(2)}, u32[]{:S(2)}) collective-permute-start(f16[224,128]{1,0:T(8,128)(2,1)S(1)} %convert_element_type.60), channel_id=1, source_target_pairs={{0,192},{64,0},{128,64},{192,128},{1,193},{65,1},{129,65},{193,129... | collective-permute-start | bytes 172040 | tf_op jit(solution)/shard_map/ppermute | solution.py:192
  140.8 5.5 %collective-permute-start.12 = (f16[224,128]{1,0:T(8,128)(2,1)S(1)}, f16[224,128]{1,0:T(8,128)(2,1)S(1)}, u32[]{:S(2)}, u32[]{:S(2)}) collective-permute-start(f16[224,128]{1,0:T(8,128)(2,1)S(1)} %convert_element_type.58), channel_id=1, source_target_pairs={{0,128},{64,192},{128,0},{192,64},{1,129},{65,193},{129,1},{193,65... | collective-permute-start | bytes 172040 | tf_op jit(solution)/shard_map/ppermute | solution.py:192
  146.3 6.6 %collective-permute-start.11 = (f16[224,128]{1,0:T(8,128)(2,1)S(1)}, f16[224,128]{1,0:T(8,128)(2,1)S(1)}, u32[]{:S(2)}, u32[]{:S(2)}) collective-permute-start(f16[224,128]{1,0:T(8,128)(2,1)S(1)} %convert_element_type.56), channel_id=1, source_target_pairs={{0,64},{64,128},{128,192},{192,0},{1,65},{65,129},{129,193},{193,1... | collective-permute-start | bytes 172040 | tf_op jit(solution)/shard_map/ppermute | solution.py:192
  152.9 2.9 %weight_grad.1 = f32[416,512]{1,0:T(8,128)} custom-call(s32[4]{0:T(128)S(1)} %pad_add_fusion.place_ref, bf16[4,2,64,512]{3,2,1,0:T(8,128)(2,1)S(1)} %pad_maximum_fusion.near_ref, bf16[4,2,64,512]{3,2,1,0:T(8,128)(2,1)S(1)} %collective-permute-done.7.up1_ref, bf16[4,2,64,512]{3,2,1,0:T(8,128)(2,1)S(1)} %collective-permute-done.8.down1_ref, ...), custom_call_target="tpu_custom_call" | custom-call | flops 1073741824 | bytes 5242880 | tf_op jit(solution)/shard_map/weight_grad/pallas_call | solution.py:178
  155.9 4.1 %collective-permute-done.11 = f16[224,128]{1,0:T(8,128)(2,1)S(1)} collective-permute-done((f16[224,128]{1,0:T(8,128)(2,1)S(1)}, f16[224,128]{1,0:T(8,128)(2,1)S(1)}, u32[]{:S(2)}, u32[]{:S(2)}) %collective-permute-start.11) | collective-permute-done | bytes 57376 | tf_op jit(solution)/shard_map/ppermute | solution.py:192
  160.0 0.7 finish_grads.1
  (29 shorter events, 0.5 us)
Async XLA Ops:
  0.6 28.4 %copy-start.2 = (bf16[64,416]{1,0:T(8,128)(2,1)S(1)}, bf16[64,416]{1,0:T(8,128)(2,1)}, u32[]{:S(2)}) copy-start(bf16[64,416]{1,0:T(8,128)(2,1)} %up_ref.1) | copy-start | bytes 159748
  0.6 28.4 %copy-start.1 = (bf16[64,416]{1,0:T(8,128)(2,1)S(1)}, bf16[64,416]{1,0:T(8,128)(2,1)}, u32[]{:S(2)}) copy-start(bf16[64,416]{1,0:T(8,128)(2,1)} %gate_ref.1) | copy-start | bytes 159748
  0.7 58.9 %copy-start = (bf16[416,512]{1,0:T(8,128)(2,1)S(1)}, bf16[416,512]{1,0:T(8,128)(2,1)}, u32[]{:S(2)}) copy-start(bf16[416,512]{1,0:T(8,128)(2,1)} %weight_ref.5) | copy-start | bytes 1277956
  23.9 36.9 %collective-permute-start = (bf16[8,128,512]{2,1,0:T(8,128)(2,1)S(1)}, bf16[8,128,512]{2,1,0:T(8,128)(2,1)S(1)}, u32[]{:S(2)}, u32[]{:S(2)}) collective-permute-start(bf16[8,128,512]{2,1,0:T(8,128)(2,1)S(1)} %all_to_all.10.rows_ref.mine_ref), channel_id=1, source_target_pairs={{0,1},{1,0},{2,3},{3,2},{4,5},{5,4},{6,7},{7,6},{8,9},{9,8},{10,11... | collective-permute-start | bytes 3145736 | tf_op jit(solution)/shard_map/ppermute | solution.py:208
  29.1 5.6 %collective-permute-start.1 = (bf16[64,512]{1,0:T(8,128)(2,1)S(1)}, bf16[64,512]{1,0:T(8,128)(2,1)S(1)}, u32[]{:S(2)}, u32[]{:S(2)}) collective-permute-start(bf16[64,512]{1,0:T(8,128)(2,1)S(1)} %get-tuple-element.44), channel_id=1, source_target_pairs={{0,256},{256,0},{1,257},{257,1},{2,258},{258,2},{3,259},{259,3},{4... | collective-permute-start | bytes 196616 | tf_op jit(solution)/shard_map/ppermute | solution.py:203
  34.8 27.3 %collective-permute-start.4 = (bf16[2,64,512]{2,1,0:T(8,128)(2,1)S(1)}, bf16[2,64,512]{2,1,0:T(8,128)(2,1)S(1)}, u32[]{:S(2)}, u32[]{:S(2)}) collective-permute-start(bf16[2,64,512]{2,1,0:T(8,128)(2,1)S(1)} %maximum_select_fusion), channel_id=1, source_target_pairs={{0,128},{64,192},{128,0},{192,64},{1,129},{65,193},{129,1},{193,65... | collective-permute-start | bytes 393224 | tf_op jit(solution)/shard_map/ppermute | solution.py:192
  50.2 12.5 %collective-permute-start.3 = (bf16[2,64,512]{2,1,0:T(8,128)(2,1)S(1)}, bf16[2,64,512]{2,1,0:T(8,128)(2,1)S(1)}, u32[]{:S(2)}, u32[]{:S(2)}) collective-permute-start(bf16[2,64,512]{2,1,0:T(8,128)(2,1)S(1)} %maximum_select_fusion), channel_id=1, source_target_pairs={{0,64},{64,128},{128,192},{192,0},{1,65},{65,129},{129,193},{193,1... | collective-permute-start | bytes 393224 | tf_op jit(solution)/shard_map/ppermute | solution.py:192
  54.2 20.0 %collective-permute-start.2 = (bf16[2,64,512]{2,1,0:T(8,128)(2,1)S(1)}, bf16[2,64,512]{2,1,0:T(8,128)(2,1)S(1)}, u32[]{:S(2)}, u32[]{:S(2)}) collective-permute-start(bf16[2,64,512]{2,1,0:T(8,128)(2,1)S(1)} %maximum_select_fusion), channel_id=1, source_target_pairs={{0,192},{64,0},{128,64},{192,128},{1,193},{65,1},{129,65},{193,129... | collective-permute-start | bytes 393224 | tf_op jit(solution)/shard_map/ppermute | solution.py:192
  74.3 15.7 %collective-permute-start.10 = (bf16[2,2,64,512]{3,2,1,0:T(8,128)(2,1)S(1)}, bf16[2,2,64,512]{3,2,1,0:T(8,128)(2,1)S(1)}, u32[]{:S(2)}, u32[]{:S(2)}) collective-permute-start(bf16[2,2,64,512]{3,2,1,0:T(8,128)(2,1)S(1)} %get-tuple-element.41), channel_id=1, source_target_pairs={{0,224},{16,240},{32,0},{48,16},{64,32},{80,48},{96,64},{112,80},{... | collective-permute-start | bytes 786440 | tf_op jit(solution)/shard_map/ppermute | solution.py:192
  79.3 27.1 %collective-permute-start.8 = (bf16[4,2,64,512]{3,2,1,0:T(8,128)(2,1)S(1)}, bf16[4,2,64,512]{3,2,1,0:T(8,128)(2,1)S(1)}, u32[]{:S(2)}, u32[]{:S(2)}) collective-permute-start(bf16[4,2,64,512]{3,2,1,0:T(8,128)(2,1)S(1)} %pad_maximum_fusion.near_ref), channel_id=1, source_target_pairs={{0,240},{16,0},{32,16},{48,32},{64,48},{80,64},{96,80},{112,96},{1... | collective-permute-start | bytes 1572872 | tf_op jit(solution)/shard_map/ppermute | solution.py:192
  81.2 25.2 %collective-permute-start.7 = (bf16[4,2,64,512]{3,2,1,0:T(8,128)(2,1)S(1)}, bf16[4,2,64,512]{3,2,1,0:T(8,128)(2,1)S(1)}, u32[]{:S(2)}, u32[]{:S(2)}) collective-permute-start(bf16[4,2,64,512]{3,2,1,0:T(8,128)(2,1)S(1)} %pad_maximum_fusion.near_ref), channel_id=1, source_target_pairs={{0,16},{16,32},{32,48},{48,64},{64,80},{80,96},{96,112},{112,128},... | collective-permute-start | bytes 1572872 | tf_op jit(solution)/shard_map/ppermute | solution.py:192
  84.6 20.0 %collective-permute-start.5 = (f16[2,4,224,128]{3,2,1,0:T(8,128)(2,1)S(1)}, f16[2,4,224,128]{3,2,1,0:T(8,128)(2,1)S(1)}, u32[]{:S(2)}, u32[]{:S(2)}) collective-permute-start(f16[2,4,224,128]{3,2,1,0:T(8,128)(2,1)S(1)} %convert_element_type.47), channel_id=1, source_target_pairs={{0,256},{256,0},{1,257},{257,1},{2,258},{258,2},{3,259},{259,3},{4... | collective-permute-start | bytes 1376264 | tf_op jit(solution)/shard_map/ppermute | solution.py:212
  86.9 19.5 %collective-permute-start.6 = (f16[2,4,224,128]{3,2,1,0:T(8,128)(2,1)S(1)}, f16[2,4,224,128]{3,2,1,0:T(8,128)(2,1)S(1)}, u32[]{:S(2)}, u32[]{:S(2)}) collective-permute-start(f16[2,4,224,128]{3,2,1,0:T(8,128)(2,1)S(1)} %convert_element_type.48), channel_id=1, source_target_pairs={{0,256},{256,0},{1,257},{257,1},{2,258},{258,2},{3,259},{259,3},{4... | collective-permute-start | bytes 1376264 | tf_op jit(solution)/shard_map/ppermute | solution.py:212
  89.9 14.7 %collective-permute-start.9 = (bf16[2,2,64,512]{3,2,1,0:T(8,128)(2,1)S(1)}, bf16[2,2,64,512]{3,2,1,0:T(8,128)(2,1)S(1)}, u32[]{:S(2)}, u32[]{:S(2)}) collective-permute-start(bf16[2,2,64,512]{3,2,1,0:T(8,128)(2,1)S(1)} %get-tuple-element.42), channel_id=1, source_target_pairs={{0,32},{16,48},{32,64},{48,80},{64,96},{80,112},{96,128},{112,144}... | collective-permute-start | bytes 786440 | tf_op jit(solution)/shard_map/ppermute | solution.py:192
  135.4 20.4 %collective-permute-start.13 = (f16[224,128]{1,0:T(8,128)(2,1)S(1)}, f16[224,128]{1,0:T(8,128)(2,1)S(1)}, u32[]{:S(2)}, u32[]{:S(2)}) collective-permute-start(f16[224,128]{1,0:T(8,128)(2,1)S(1)} %convert_element_type.60), channel_id=1, source_target_pairs={{0,192},{64,0},{128,64},{192,128},{1,193},{65,1},{129,65},{193,129... | collective-permute-start | bytes 172040 | tf_op jit(solution)/shard_map/ppermute | solution.py:192
  140.8 15.1 %collective-permute-start.12 = (f16[224,128]{1,0:T(8,128)(2,1)S(1)}, f16[224,128]{1,0:T(8,128)(2,1)S(1)}, u32[]{:S(2)}, u32[]{:S(2)}) collective-permute-start(f16[224,128]{1,0:T(8,128)(2,1)S(1)} %convert_element_type.58), channel_id=1, source_target_pairs={{0,128},{64,192},{128,0},{192,64},{1,129},{65,193},{129,1},{193,65... | collective-permute-start | bytes 172040 | tf_op jit(solution)/shard_map/ppermute | solution.py:192
  146.3 13.7 %collective-permute-start.11 = (f16[224,128]{1,0:T(8,128)(2,1)S(1)}, f16[224,128]{1,0:T(8,128)(2,1)S(1)}, u32[]{:S(2)}, u32[]{:S(2)}) collective-permute-start(f16[224,128]{1,0:T(8,128)(2,1)S(1)} %convert_element_type.56), channel_id=1, source_target_pairs={{0,64},{64,128},{128,192},{192,0},{1,65},{65,129},{129,193},{193,1... | collective-permute-start | bytes 172040 | tf_op jit(solution)/shard_map/ppermute | solution.py:192

commit v3 on v2

--- a/solution.py
+++ b/solution.py
@@ -148,9 +148,9 @@
     )(*parts, gate_pre, up_pre)
 
 
-def weight_kernel(place_ref, near_ref, up1_ref, down1_ref, up2_ref, down2_ref, mine_ref, other_ref, out_ref, tokens):
-    c, z = place_ref[1], place_ref[3]
-    for ref, shift, begin, count in (
+def collect_kernel(place_ref, near_ref, up1_ref, down1_ref, up2_ref, down2_ref, out_ref):
+    z = place_ref[3]
+    for ref, step, begin, count in (
         (near_ref, 0, 0, 4),
         (up1_ref, -1, 0, 4),
         (down1_ref, 1, 0, 4),
@@ -158,33 +158,50 @@
         (down2_ref, 2, 0, 2),
     ):
         for k in range(count):
-            owner = lax.rem(z + shift - 4 * (begin + k - 1) + 32, 16)
-            core = lax.rem(owner // 2, 2)
-            for xl in range(2):
-                start = pl.multiple_of(lax.rem(owner, 2) * 64, 64)
-                tokens[xl, core, owner // 4, pl.ds(start, 64)] = ref[k, xl]
+            owner = lax.rem(z + step - 4 * (begin + k - 1) + 32, 16)
+            start = pl.multiple_of(lax.rem(owner, 2) * 64, 64)
+            out_ref[lax.rem(owner // 2, 2), owner // 4, pl.ds(start, 64)] = ref[k]
+
+
+def collect(place, blocks):
+    near = blocks[0]
+    return pl.pallas_call(
+        collect_kernel,
+        out_shape=jax.ShapeDtypeStruct((2, 4, 128, near.shape[2]), near.dtype),
+        in_specs=[scalars] + [whole] * 5,
+        out_specs=whole,
+        compiler_params=pltpu.CompilerParams(vmem_limit_bytes=VMEM_BYTES),
+        cost_estimate=pl.CostEstimate(flops=1 << 20, bytes_accessed=2 << 20, transcendentals=0),
+        name="collect_hidden",
+    )(place, *blocks)
+
+
+def weight_kernel(last, place_ref, hidden_ref, mine_ref, other_ref, *refs):
+    before_ref, out_ref = refs if last else (None, refs[0])
+    xl, c = place_ref[0], place_ref[1]
+    first = ((1 - xl) if last else xl) * 4
     hid = out_ref.shape[0]
     total = None
-    for xl in range(2):
-        for ref, core in ((mine_ref, c), (other_ref, 1 - c)):
-            rows = ref[4 * xl : 4 * xl + 4].reshape(512, ref.shape[2])
-            hidden = tokens[xl, core].reshape(512, tokens.shape[4])
-            product = lax.dot_general(hidden, rows, (((0,), (0,)), ((), ())), preferred_element_type=jnp.float32)
-            total = product if total is None else total + product
-    out_ref[...] = total[:hid] * 2048 ** (-0.5)
-
-
-def weight_part(place, blocks, mine, other, hid):
-    return pl.pallas_call(
-        weight_kernel,
+    for ref, core in ((mine_ref, c), (other_ref, 1 - c)):
+        rows = ref[pl.ds(first, 4)].reshape(512, ref.shape[2])
+        tokens = hidden_ref[core].reshape(512, hidden_ref.shape[3])
+        product = lax.dot_general(tokens, rows, (((0,), (0,)), ((), ())), preferred_element_type=jnp.float32)
+        total = product if total is None else total + product
+    total = total[:hid]
+    out_ref[...] = (before_ref[...] + total) * 2048 ** (-0.5) if last else total
+
+
+def weight_part(place, hidden, mine, other, hid, before=None):
+    last = before is not None
+    return pl.pallas_call(
+        functools.partial(weight_kernel, last),
         out_shape=jax.ShapeDtypeStruct((hid, mine.shape[2]), jnp.float32),
-        in_specs=[scalars] + [whole] * 7,
-        out_specs=whole,
-        scratch_shapes=[pltpu.VMEM((2, 2, 4, 128, 512), mine.dtype)],
-        compiler_params=pltpu.CompilerParams(vmem_limit_bytes=VMEM_BYTES),
-        cost_estimate=pl.CostEstimate(flops=2 * 2048 * 512 * 512, bytes_accessed=5 << 20, transcendentals=0),
-        name="weight_grad",
-    )(place, *blocks, mine, other)
+        in_specs=[scalars] + [whole] * (4 if last else 3),
+        out_specs=whole,
+        compiler_params=pltpu.CompilerParams(vmem_limit_bytes=VMEM_BYTES),
+        cost_estimate=pl.CostEstimate(flops=2 * 1024 * 512 * 512, bytes_accessed=4 << 20, transcendentals=0),
+        name="weight_part",
+    )(place, hidden, mine, other, *([before] if last else []))
 
 
 def shift(array, axes, step):
@@ -193,35 +210,36 @@
 
 
 def shards(gate_pre, up_pre, out_grad, down_weight):
-    xl = lax.axis_index("xl")
-    place = jnp.stack([xl, lax.axis_index("c"), lax.axis_index(FAR), lax.axis_index(Z)]).astype(jnp.int32)
+    place = jnp.stack([lax.axis_index("xl"), lax.axis_index("c"), lax.axis_index(FAR), lax.axis_index(Z)]).astype(jnp.int32)
     hid = gate_pre.shape[1]
     gate_vals = gate_pre.astype(jnp.float32)
     hidden = (gate_vals * jax.nn.sigmoid(gate_vals) * up_pre.astype(jnp.float32)).astype(jnp.bfloat16)
     hidden = jnp.pad(hidden, ((0, 0), (0, 512 - hid)))
 
-    theirs = lax.ppermute(hidden, "xl", SWAP)
-    pair = jnp.where(xl == 0, jnp.stack([hidden, theirs]), jnp.stack([theirs, hidden]))
-    steps = [shift(pair, FAR, k) for k in (3, 1, 2)]
-
     mine = lax.all_to_all(jnp.broadcast_to(out_grad[None], (8,) + out_grad.shape), YX, 0, 0)
+    steps = [shift(hidden, FAR, k) for k in (3, 1, 2)]
+    mine, hidden, steps = lax.optimization_barrier((mine, hidden, steps))
     other = lax.ppermute(mine, "c", SWAP)
 
     sent = [send_part(place, rows, down_weight).astype(jnp.float16) for rows in (mine, other)]
-    sent, pair, steps = lax.optimization_barrier((sent, pair, steps))
+    near = jnp.stack([steps[0], hidden, steps[1], steps[2]])
+    sent, near = lax.optimization_barrier((sent, near))
     got = [lax.ppermute(s, "xl", SWAP) for s in sent]
-
-    near = jnp.stack([steps[0], pair, steps[1], steps[2]])
     blocks = [near, shift(near, Z, 1), shift(near, Z, -1), shift(near[1:3], Z, 2), shift(near[0:2], Z, -2)]
     got, blocks = lax.optimization_barrier((got, blocks))
 
     kept = keep_part(place, mine, other, down_weight, *[g.astype(jnp.float32) for g in got])
     kept = kept.astype(jnp.float16).reshape(4, 4, 224, LANES)
-    merged = merge(place, lax.all_to_all(kept, ("z1", "z0"), 0, 0).astype(jnp.float32))
+    tokens = collect(place, blocks)
+    theirs = lax.ppermute(tokens, "xl", SWAP)
+    summed, theirs = lax.optimization_barrier((lax.all_to_all(kept, ("z1", "z0"), 0, 0), theirs))
+
+    merged = merge(place, summed.astype(jnp.float32))
     far = [shift(merged[k].astype(jnp.float16), FAR, k).astype(jnp.float32) for k in range(1, 4)]
     gate_grad, up_grad = final([merged[0]] + far, gate_pre, up_pre)
 
-    weight_grad = weight_part(place, blocks, mine, other, hid)
+    begun = weight_part(place, tokens, mine, other, hid)
+    weight_grad = weight_part(place, theirs, mine, other, hid, begun)
     return (gate_grad, up_grad, weight_grad)
 
 

time: 161 us -> 142 us (0.88)
  the two profiles are of different devices: /device:TPU:1 before, /device:TPU:6 now
where the time goes in v3:
time: 142 us; the launch traced here: 140 us
  starting transfers between devices  78.7 us (55%)
  waiting for transfers between devices  40.2 us (28%)
  Pallas kernels  9.69 us (7%)
  local copies, waits for them, and re-layouts  8.05 us (6%)
  other arithmetic  2.88 us (2%)
    ppermute x10, starting transfers between devices, shift(): lax.ppermute(array, axes, [(i, (i + step) % size) for i in range(size)])  54.7 us
    ppermute x1, waiting for transfers between devices, shards(): theirs = lax.ppermute(tokens, 'xl', SWAP)  23.1 us
    ppermute x10, waiting for transfers between devices, shift(): lax.ppermute(array, axes, [(i, (i + step) % size) for i in range(size)])  15.9 us
    all_to_all x1, starting transfers between devices, shards(): lax.all_to_all(jnp.broadcast_to(out_grad[None], (8,) + out_grad.shape), Y...  7.43 us
    all_to_all x1, starting transfers between devices, shards(): lax.all_to_all(kept, ('z1', 'z0'), 0, 0)  6.08 us
    unnamed x26, local copies, waits for them, and re-layouts  6 us
    ppermute x2, starting transfers between devices, shards(): got = [lax.ppermute(s, 'xl', SWAP) for s in sent]  5.84 us
    pallas_call x2, Pallas kernels, weight_part(): pl.pallas_call(functools.partial(weight_kernel, last), out_shape=jax.Shap...  3.45 us
  transfers between devices with their start and end apart: 16, of which 7 were waited for; matrix products, arithmetic and copies ran while one was open for 0% of the time, Pallas kernels for 4%

profile of v3, /device:TPU:6, one launch (start us, length us, event | category | flops | bytes accessed | tf_op | source)
XLA Modules:
  0.0 140.5 jit_solution(1433598683381795915)
XLA Ops:
  0.7 2.0 %broadcast_in_dim.2 = bf16[8,128,512]{2,1,0:T(8,128)(2,1)} broadcast(bf16[128,512]{1,0:T(8,128)(2,1)} %param.6), dimensions={1,2} | broadcast | bytes 1179648 | tf_op jit(solution)/shard_map/broadcast_in_dim | solution.py:219
  2.7 7.4 %all-to-all-start = ((bf16[8,128,512]{2,1,0:T(8,128)(2,1)}), bf16[8,128,512]{2,1,0:T(8,128)(2,1)S(1)}, u32[]{:S(2)}, u32[]{:S(2)}) async-start(bf16[8,128,512]{2,1,0:T(8,128)(2,1)} %broadcast_in_dim.2), calls=%async_computation | async-start | bytes 2097152 | tf_op jit(solution)/shard_map/all_to_all | solution.py:219
  10.2 15.7 %collective-permute-start.2 = (bf16[64,512]{1,0:T(8,128)(2,1)S(1)}, bf16[64,512]{1,0:T(8,128)(2,1)S(1)}, u32[]{:S(2)}, u32[]{:S(2)}) collective-permute-start(bf16[64,512]{1,0:T(8,128)(2,1)S(1)} %pad.4), channel_id=1, source_target_pairs={{0,128},{64,192},{128,0},{192,64},{1,129},{65,193},{129,1},{193,65... | collective-permute-start | bytes 196616 | tf_op jit(solution)/shard_map/ppermute | solution.py:209
  25.9 4.3 %collective-permute-start.1 = (bf16[64,512]{1,0:T(8,128)(2,1)S(1)}, bf16[64,512]{1,0:T(8,128)(2,1)S(1)}, u32[]{:S(2)}, u32[]{:S(2)}) collective-permute-start(bf16[64,512]{1,0:T(8,128)(2,1)S(1)} %pad.4), channel_id=1, source_target_pairs={{0,64},{64,128},{128,192},{192,0},{1,65},{65,129},{129,193},{193,1... | collective-permute-start | bytes 196616 | tf_op jit(solution)/shard_map/ppermute | solution.py:209
  30.2 5.5 %collective-permute-start = (bf16[64,512]{1,0:T(8,128)(2,1)S(1)}, bf16[64,512]{1,0:T(8,128)(2,1)S(1)}, u32[]{:S(2)}, u32[]{:S(2)}) collective-permute-start(bf16[64,512]{1,0:T(8,128)(2,1)S(1)} %pad.4), channel_id=1, source_target_pairs={{0,192},{64,0},{128,64},{192,128},{1,193},{65,1},{129,65},{193,129... | collective-permute-start | bytes 196616 | tf_op jit(solution)/shard_map/ppermute | solution.py:209
  35.7 1.2 collective-permute-done.1
  36.9 6.1 %collective-permute-done = bf16[64,512]{1,0:T(8,128)(2,1)S(1)} collective-permute-done((bf16[64,512]{1,0:T(8,128)(2,1)S(1)}, bf16[64,512]{1,0:T(8,128)(2,1)S(1)}, u32[]{:S(2)}, u32[]{:S(2)}) %collective-permute-start) | collective-permute-done | bytes 65568 | tf_op jit(solution)/shard_map/ppermute | solution.py:209
  43.0 1.9 %collective-permute-start.3 = (bf16[8,128,512]{2,1,0:T(8,128)(2,1)S(1)}, bf16[8,128,512]{2,1,0:T(8,128)(2,1)S(1)}, u32[]{:S(2)}, u32[]{:S(2)}) collective-permute-start(bf16[8,128,512]{2,1,0:T(8,128)(2,1)S(1)} %all-to-all-done.rows_ref.mine_ref), channel_id=1, source_target_pairs={{0,1},{1,0},{2,3},{3,2},{4,5},{5,4},{6,7},{7,6},{8,9},{9,8},{10,11... | collective-permute-start | bytes 3145736 | tf_op jit(solution)/shard_map/ppermute | solution.py:222
  45.0 1.2 send_part.2
  46.3 1.2 collective-permute-done.3.rows_ref.other_ref
  47.5 1.2 send_part.3
  48.8 2.7 %collective-permute-start.4 = (f16[2,4,224,128]{3,2,1,0:T(8,128)(2,1)S(1)}, f16[2,4,224,128]{3,2,1,0:T(8,128)(2,1)S(1)}, u32[]{:S(2)}, u32[]{:S(2)}) collective-permute-start(f16[2,4,224,128]{3,2,1,0:T(8,128)(2,1)S(1)} %convert_element_type.50), channel_id=1, source_target_pairs={{0,256},{256,0},{1,257},{257,1},{2,258},{258,2},{3,259},{259,3},{4... | collective-permute-start | bytes 1376264 | tf_op jit(solution)/shard_map/ppermute | solution.py:227
  51.5 3.1 %collective-permute-start.5 = (f16[2,4,224,128]{3,2,1,0:T(8,128)(2,1)S(1)}, f16[2,4,224,128]{3,2,1,0:T(8,128)(2,1)S(1)}, u32[]{:S(2)}, u32[]{:S(2)}) collective-permute-start(f16[2,4,224,128]{3,2,1,0:T(8,128)(2,1)S(1)} %convert_element_type.51), channel_id=1, source_target_pairs={{0,256},{256,0},{1,257},{257,1},{2,258},{258,2},{3,259},{259,3},{4... | collective-permute-start | bytes 1376264 | tf_op jit(solution)/shard_map/ppermute | solution.py:227
  54.7 4.2 %collective-permute-start.9 = (bf16[2,64,512]{2,1,0:T(8,128)(2,1)S(1)}, bf16[2,64,512]{2,1,0:T(8,128)(2,1)S(1)}, u32[]{:S(2)}, u32[]{:S(2)}) collective-permute-start(bf16[2,64,512]{2,1,0:T(8,128)(2,1)S(1)} %get-tuple-element.49), channel_id=1, source_target_pairs={{0,224},{16,240},{32,0},{48,16},{64,32},{80,48},{96,64},{112,80},{... | collective-permute-start | bytes 393224 | tf_op jit(solution)/shard_map/ppermute | solution.py:209
  58.9 2.6 %collective-permute-start.7 = (bf16[4,64,512]{2,1,0:T(8,128)(2,1)S(1)}, bf16[4,64,512]{2,1,0:T(8,128)(2,1)S(1)}, u32[]{:S(2)}, u32[]{:S(2)}) collective-permute-start(bf16[4,64,512]{2,1,0:T(8,128)(2,1)S(1)} %pad_maximum_fusion.near_ref), channel_id=1, source_target_pairs={{0,240},{16,0},{32,16},{48,32},{64,48},{80,64},{96,80},{112,96},{1... | collective-permute-start | bytes 786440 | tf_op jit(solution)/shard_map/ppermute | solution.py:209
  61.5 3.2 %collective-permute-start.6 = (bf16[4,64,512]{2,1,0:T(8,128)(2,1)S(1)}, bf16[4,64,512]{2,1,0:T(8,128)(2,1)S(1)}, u32[]{:S(2)}, u32[]{:S(2)}) collective-permute-start(bf16[4,64,512]{2,1,0:T(8,128)(2,1)S(1)} %pad_maximum_fusion.near_ref), channel_id=1, source_target_pairs={{0,16},{16,32},{32,48},{48,64},{64,80},{80,96},{96,112},{112,128},... | collective-permute-start | bytes 786440 | tf_op jit(solution)/shard_map/ppermute | solution.py:209
  65.4 4.1 %collective-permute-start.8 = (bf16[2,64,512]{2,1,0:T(8,128)(2,1)S(1)}, bf16[2,64,512]{2,1,0:T(8,128)(2,1)S(1)}, u32[]{:S(2)}, u32[]{:S(2)}) collective-permute-start(bf16[2,64,512]{2,1,0:T(8,128)(2,1)S(1)} %get-tuple-element.50), channel_id=1, source_target_pairs={{0,32},{16,48},{32,64},{48,80},{64,96},{80,112},{96,128},{112,144}... | collective-permute-start | bytes 393224 | tf_op jit(solution)/shard_map/ppermute | solution.py:209
  69.6 4.9 %collective-permute-done.8.up2_ref = bf16[2,64,512]{2,1,0:T(8,128)(2,1)S(1)} collective-permute-done((bf16[2,64,512]{2,1,0:T(8,128)(2,1)S(1)}, bf16[2,64,512]{2,1,0:T(8,128)(2,1)S(1)}, u32[]{:S(2)}, u32[]{:S(2)}) %collective-permute-start.8) | collective-permute-done | bytes 131104 | tf_op jit(solution)/shard_map/ppermute | solution.py:209
  75.4 1.5 %keep_part.1 = f32[2,2,4,224,128]{4,3,2,1,0:T(8,128)S(1)} custom-call(s32[4]{0:T(128)S(1)} %pad_add_fusion.place_ref, bf16[8,128,512]{2,1,0:T(8,128)(2,1)S(1)} %all-to-all-done.rows_ref.mine_ref, bf16[8,128,512]{2,1,0:T(8,128)(2,1)S(1)} %collective-permute-done.3.rows_ref.other_ref, bf16[416,512]{1,0:T(8,128)(2,1)S(1)} %copy-done, ...), custom_call_target="tpu_custom_call" | custom-call | flops 536870912 | bytes 4194304 | tf_op jit(solution)/shard_map/keep_part/pallas_call | solution.py:87
  76.9 1.0 convert_element_type.54
  77.9 6.1 %all-to-all-start.1 = ((f16[4,4,224,128]{3,2,1,0:T(8,128)(2,1)}), f16[4,4,224,128]{3,2,1,0:T(8,128)(2,1)}, u32[]{:S(2)}, u32[]{:S(2)}) async-start(f16[4,4,224,128]{3,2,1,0:T(8,128)(2,1)} %bitcast.9), calls=%async_computation.1 | async-start | bytes 1835008 | tf_op jit(solution)/shard_map/all_to_all | solution.py:235
  84.0 0.9 copy-done.4
  88.5 2.7 %collective-permute-start.10 = (bf16[2,4,128,512]{3,2,1,0:T(8,128)(2,1)S(1)}, bf16[2,4,128,512]{3,2,1,0:T(8,128)(2,1)S(1)}, u32[]{:S(2)}, u32[]{:S(2)}) collective-permute-start(bf16[2,4,128,512]{3,2,1,0:T(8,128)(2,1)S(1)} %collect_hidden.1.hidden_ref), channel_id=1, source_target_pairs={{0,256},{256,0},{1,257},{257,1},{2,258},{258,2},{3,259},{259,3},{4... | collective-permute-start | bytes 3145736 | tf_op jit(solution)/shard_map/ppermute | solution.py:234
  91.3 23.1 %collective-permute-done.10.hidden_ref = bf16[2,4,128,512]{3,2,1,0:T(8,128)(2,1)S(1)} collective-permute-done((bf16[2,4,128,512]{3,2,1,0:T(8,128)(2,1)S(1)}, bf16[2,4,128,512]{3,2,1,0:T(8,128)(2,1)S(1)}, u32[]{:S(2)}, u32[]{:S(2)}) %collective-permute-start.10) | collective-permute-done | bytes 1048608 | tf_op jit(solution)/shard_map/ppermute | solution.py:234
  114.4 1.0 copy-done.1
  115.4 1.4 convert_element_type.55.got_ref
  117.6 5.5 %collective-permute-start.13 = (f16[224,128]{1,0:T(8,128)(2,1)S(1)}, f16[224,128]{1,0:T(8,128)(2,1)S(1)}, u32[]{:S(2)}, u32[]{:S(2)}) collective-permute-start(f16[224,128]{1,0:T(8,128)(2,1)S(1)} %convert_element_type.60), channel_id=1, source_target_pairs={{0,192},{64,0},{128,64},{192,128},{1,193},{65,1},{129,65},{193,129... | collective-permute-start | bytes 172040 | tf_op jit(solution)/shard_map/ppermute | solution.py:209
  123.1 4.3 %collective-permute-start.12 = (f16[224,128]{1,0:T(8,128)(2,1)S(1)}, f16[224,128]{1,0:T(8,128)(2,1)S(1)}, u32[]{:S(2)}, u32[]{:S(2)}) collective-permute-start(f16[224,128]{1,0:T(8,128)(2,1)S(1)} %convert_element_type.58), channel_id=1, source_target_pairs={{0,128},{64,192},{128,0},{192,64},{1,129},{65,193},{129,1},{193,65... | collective-permute-start | bytes 172040 | tf_op jit(solution)/shard_map/ppermute | solution.py:209
  127.5 5.1 %collective-permute-start.11 = (f16[224,128]{1,0:T(8,128)(2,1)S(1)}, f16[224,128]{1,0:T(8,128)(2,1)S(1)}, u32[]{:S(2)}, u32[]{:S(2)}) collective-permute-start(f16[224,128]{1,0:T(8,128)(2,1)S(1)} %convert_element_type.56), channel_id=1, source_target_pairs={{0,64},{64,128},{128,192},{192,0},{1,65},{65,129},{129,193},{193,1... | collective-permute-start | bytes 172040 | tf_op jit(solution)/shard_map/ppermute | solution.py:209
  132.6 1.3 weight_part.2.refs_0_
  133.9 2.2 %weight_part.3 = f32[416,512]{1,0:T(8,128)} custom-call(s32[4]{0:T(128)S(1)} %pad_add_fusion.place_ref, bf16[2,4,128,512]{3,2,1,0:T(8,128)(2,1)S(1)} %copy-done.2, bf16[8,128,512]{2,1,0:T(8,128)(2,1)S(1)} %all-to-all-done.rows_ref.mine_ref, bf16[8,128,512]{2,1,0:T(8,128)(2,1)S(1)} %collective-permute-done.3.rows_ref.other_ref, f32[416,512]{1,0:T(8,128)S(1)} %weight_part.2.refs_0_), custom_call_target="tpu_custom_call" | custom-call | flops 536870912 | bytes 4194304 | tf_op jit(solution)/shard_map/weight_part/pallas_call | solution.py:196
  136.1 3.6 %collective-permute-done.12 = f16[224,128]{1,0:T(8,128)(2,1)S(1)} collective-permute-done((f16[224,128]{1,0:T(8,128)(2,1)S(1)}, f16[224,128]{1,0:T(8,128)(2,1)S(1)}, u32[]{:S(2)}, u32[]{:S(2)}) %collective-permute-start.12) | collective-permute-done | bytes 57376 | tf_op jit(solution)/shard_map/ppermute | solution.py:209
  (52 shorter events, 7.0 us)
Async XLA Ops:
  0.6 9.5 %copy-start.8 = (bf16[64,416]{1,0:T(8,128)(2,1)S(1)}, bf16[64,416]{1,0:T(8,128)(2,1)}, u32[]{:S(2)}) copy-start(bf16[64,416]{1,0:T(8,128)(2,1)} %up_ref.1) | copy-start | bytes 159748
  0.6 9.5 %copy-start.7 = (bf16[64,416]{1,0:T(8,128)(2,1)S(1)}, bf16[64,416]{1,0:T(8,128)(2,1)}, u32[]{:S(2)}) copy-start(bf16[64,416]{1,0:T(8,128)(2,1)} %gate_ref.1) | copy-start | bytes 159748
  0.7 44.3 %copy-start = (bf16[416,512]{1,0:T(8,128)(2,1)S(1)}, bf16[416,512]{1,0:T(8,128)(2,1)}, u32[]{:S(2)}) copy-start(bf16[416,512]{1,0:T(8,128)(2,1)} %weight_ref.5) | copy-start | bytes 1277956
  2.7 40.3 %all-to-all-start = ((bf16[8,128,512]{2,1,0:T(8,128)(2,1)}), bf16[8,128,512]{2,1,0:T(8,128)(2,1)S(1)}, u32[]{:S(2)}, u32[]{:S(2)}) async-start(bf16[8,128,512]{2,1,0:T(8,128)(2,1)} %broadcast_in_dim.2), calls=%async_computation | async-start | bytes 2097152 | tf_op jit(solution)/shard_map/all_to_all | solution.py:219
  10.2 25.5 %collective-permute-start.2 = (bf16[64,512]{1,0:T(8,128)(2,1)S(1)}, bf16[64,512]{1,0:T(8,128)(2,1)S(1)}, u32[]{:S(2)}, u32[]{:S(2)}) collective-permute-start(bf16[64,512]{1,0:T(8,128)(2,1)S(1)} %pad.4), channel_id=1, source_target_pairs={{0,128},{64,192},{128,0},{192,64},{1,129},{65,193},{129,1},{193,65... | collective-permute-start | bytes 196616 | tf_op jit(solution)/shard_map/ppermute | solution.py:209
  25.9 10.9 %collective-permute-start.1 = (bf16[64,512]{1,0:T(8,128)(2,1)S(1)}, bf16[64,512]{1,0:T(8,128)(2,1)S(1)}, u32[]{:S(2)}, u32[]{:S(2)}) collective-permute-start(bf16[64,512]{1,0:T(8,128)(2,1)S(1)} %pad.4), channel_id=1, source_target_pairs={{0,64},{64,128},{128,192},{192,0},{1,65},{65,129},{129,193},{193,1... | collective-permute-start | bytes 196616 | tf_op jit(solution)/shard_map/ppermute | solution.py:209
  30.2 12.7 %collective-permute-start = (bf16[64,512]{1,0:T(8,128)(2,1)S(1)}, bf16[64,512]{1,0:T(8,128)(2,1)S(1)}, u32[]{:S(2)}, u32[]{:S(2)}) collective-permute-start(bf16[64,512]{1,0:T(8,128)(2,1)S(1)} %pad.4), channel_id=1, source_target_pairs={{0,192},{64,0},{128,64},{192,128},{1,193},{65,1},{129,65},{193,129... | collective-permute-start | bytes 196616 | tf_op jit(solution)/shard_map/ppermute | solution.py:209
  43.0 4.5 %collective-permute-start.3 = (bf16[8,128,512]{2,1,0:T(8,128)(2,1)S(1)}, bf16[8,128,512]{2,1,0:T(8,128)(2,1)S(1)}, u32[]{:S(2)}, u32[]{:S(2)}) collective-permute-start(bf16[8,128,512]{2,1,0:T(8,128)(2,1)S(1)} %all-to-all-done.rows_ref.mine_ref), channel_id=1, source_target_pairs={{0,1},{1,0},{2,3},{3,2},{4,5},{5,4},{6,7},{7,6},{8,9},{9,8},{10,11... | collective-permute-start | bytes 3145736 | tf_op jit(solution)/shard_map/ppermute | solution.py:222
  48.8 26.4 %collective-permute-start.4 = (f16[2,4,224,128]{3,2,1,0:T(8,128)(2,1)S(1)}, f16[2,4,224,128]{3,2,1,0:T(8,128)(2,1)S(1)}, u32[]{:S(2)}, u32[]{:S(2)}) collective-permute-start(f16[2,4,224,128]{3,2,1,0:T(8,128)(2,1)S(1)} %convert_element_type.50), channel_id=1, source_target_pairs={{0,256},{256,0},{1,257},{257,1},{2,258},{258,2},{3,259},{259,3},{4... | collective-permute-start | bytes 1376264 | tf_op jit(solution)/shard_map/ppermute | solution.py:227
  51.5 23.7 %collective-permute-start.5 = (f16[2,4,224,128]{3,2,1,0:T(8,128)(2,1)S(1)}, f16[2,4,224,128]{3,2,1,0:T(8,128)(2,1)S(1)}, u32[]{:S(2)}, u32[]{:S(2)}) collective-permute-start(f16[2,4,224,128]{3,2,1,0:T(8,128)(2,1)S(1)} %convert_element_type.51), channel_id=1, source_target_pairs={{0,256},{256,0},{1,257},{257,1},{2,258},{258,2},{3,259},{259,3},{4... | collective-permute-start | bytes 1376264 | tf_op jit(solution)/shard_map/ppermute | solution.py:227
  54.7 10.1 %collective-permute-start.9 = (bf16[2,64,512]{2,1,0:T(8,128)(2,1)S(1)}, bf16[2,64,512]{2,1,0:T(8,128)(2,1)S(1)}, u32[]{:S(2)}, u32[]{:S(2)}) collective-permute-start(bf16[2,64,512]{2,1,0:T(8,128)(2,1)S(1)} %get-tuple-element.49), channel_id=1, source_target_pairs={{0,224},{16,240},{32,0},{48,16},{64,32},{80,48},{96,64},{112,80},{... | collective-permute-start | bytes 393224 | tf_op jit(solution)/shard_map/ppermute | solution.py:209
  58.9 16.2 %collective-permute-start.7 = (bf16[4,64,512]{2,1,0:T(8,128)(2,1)S(1)}, bf16[4,64,512]{2,1,0:T(8,128)(2,1)S(1)}, u32[]{:S(2)}, u32[]{:S(2)}) collective-permute-start(bf16[4,64,512]{2,1,0:T(8,128)(2,1)S(1)} %pad_maximum_fusion.near_ref), channel_id=1, source_target_pairs={{0,240},{16,0},{32,16},{48,32},{64,48},{80,64},{96,80},{112,96},{1... | collective-permute-start | bytes 786440 | tf_op jit(solution)/shard_map/ppermute | solution.py:209
  61.5 13.7 %collective-permute-start.6 = (bf16[4,64,512]{2,1,0:T(8,128)(2,1)S(1)}, bf16[4,64,512]{2,1,0:T(8,128)(2,1)S(1)}, u32[]{:S(2)}, u32[]{:S(2)}) collective-permute-start(bf16[4,64,512]{2,1,0:T(8,128)(2,1)S(1)} %pad_maximum_fusion.near_ref), channel_id=1, source_target_pairs={{0,16},{16,32},{32,48},{48,64},{64,80},{80,96},{96,112},{112,128},... | collective-permute-start | bytes 786440 | tf_op jit(solution)/shard_map/ppermute | solution.py:209
  64.8 0.7 copy-start.9
  65.4 9.1 %collective-permute-start.8 = (bf16[2,64,512]{2,1,0:T(8,128)(2,1)S(1)}, bf16[2,64,512]{2,1,0:T(8,128)(2,1)S(1)}, u32[]{:S(2)}, u32[]{:S(2)}) collective-permute-start(bf16[2,64,512]{2,1,0:T(8,128)(2,1)S(1)} %get-tuple-element.50), channel_id=1, source_target_pairs={{0,32},{16,48},{32,64},{48,80},{64,96},{80,112},{96,128},{112,144}... | collective-permute-start | bytes 393224 | tf_op jit(solution)/shard_map/ppermute | solution.py:209
  74.5 0.7 copy-start.11
  75.1 1.7 %copy-start.3 = (bf16[4,64,512]{2,1,0:T(8,128)(2,1)}, bf16[4,64,512]{2,1,0:T(8,128)(2,1)S(1)}, u32[]{:S(2)}) copy-start(bf16[4,64,512]{2,1,0:T(8,128)(2,1)S(1)} %collective-permute-done.7.down1_ref) | copy-start | bytes 786436
  75.2 1.7 %copy-start.5 = (bf16[4,64,512]{2,1,0:T(8,128)(2,1)}, bf16[4,64,512]{2,1,0:T(8,128)(2,1)S(1)}, u32[]{:S(2)}) copy-start(bf16[4,64,512]{2,1,0:T(8,128)(2,1)S(1)} %collective-permute-done.6.up1_ref) | copy-start | bytes 786436
  77.9 37.4 %all-to-all-start.1 = ((f16[4,4,224,128]{3,2,1,0:T(8,128)(2,1)}), f16[4,4,224,128]{3,2,1,0:T(8,128)(2,1)}, u32[]{:S(2)}, u32[]{:S(2)}) async-start(f16[4,4,224,128]{3,2,1,0:T(8,128)(2,1)} %bitcast.9), calls=%async_computation.1 | async-start | bytes 1835008 | tf_op jit(solution)/shard_map/all_to_all | solution.py:235
  84.0 0.9 copy-start.4
  85.0 0.9 copy-start.6
  85.9 0.9 copy-start.10
  86.8 0.9 copy-start.12
  88.5 25.8 %collective-permute-start.10 = (bf16[2,4,128,512]{3,2,1,0:T(8,128)(2,1)S(1)}, bf16[2,4,128,512]{3,2,1,0:T(8,128)(2,1)S(1)}, u32[]{:S(2)}, u32[]{:S(2)}) collective-permute-start(bf16[2,4,128,512]{3,2,1,0:T(8,128)(2,1)S(1)} %collect_hidden.1.hidden_ref), channel_id=1, source_target_pairs={{0,256},{256,0},{1,257},{257,1},{2,258},{258,2},{3,259},{259,3},{4... | collective-permute-start | bytes 3145736 | tf_op jit(solution)/shard_map/ppermute | solution.py:234
  114.4 1.0 copy-start.1
  117.6 16.3 %copy-start.2 = (bf16[2,4,128,512]{3,2,1,0:T(8,128)(2,1)S(1)}, bf16[2,4,128,512]{3,2,1,0:T(8,128)(2,1)}, u32[]{:S(2)}) copy-start(bf16[2,4,128,512]{3,2,1,0:T(8,128)(2,1)} %copy-done.1) | copy-start | bytes 3145732
  117.6 18.5 %collective-permute-start.13 = (f16[224,128]{1,0:T(8,128)(2,1)S(1)}, f16[224,128]{1,0:T(8,128)(2,1)S(1)}, u32[]{:S(2)}, u32[]{:S(2)}) collective-permute-start(f16[224,128]{1,0:T(8,128)(2,1)S(1)} %convert_element_type.60), channel_id=1, source_target_pairs={{0,192},{64,0},{128,64},{192,128},{1,193},{65,1},{129,65},{193,129... | collective-permute-start | bytes 172040 | tf_op jit(solution)/shard_map/ppermute | solution.py:209
  123.1 16.6 %collective-permute-start.12 = (f16[224,128]{1,0:T(8,128)(2,1)S(1)}, f16[224,128]{1,0:T(8,128)(2,1)S(1)}, u32[]{:S(2)}, u32[]{:S(2)}) collective-permute-start(f16[224,128]{1,0:T(8,128)(2,1)S(1)} %convert_element_type.58), channel_id=1, source_target_pairs={{0,128},{64,192},{128,0},{192,64},{1,129},{65,193},{129,1},{193,65... | collective-permute-start | bytes 172040 | tf_op jit(solution)/shard_map/ppermute | solution.py:209
  127.5 12.2 %collective-permute-start.11 = (f16[224,128]{1,0:T(8,128)(2,1)S(1)}, f16[224,128]{1,0:T(8,128)(2,1)S(1)}, u32[]{:S(2)}, u32[]{:S(2)}) collective-permute-start(f16[224,128]{1,0:T(8,128)(2,1)S(1)} %convert_element_type.56), channel_id=1, source_target_pairs={{0,64},{64,128},{128,192},{192,0},{1,65},{65,129},{129,193},{193,1... | collective-permute-start | bytes 172040 | tf_op jit(solution)/shard_map/ppermute | solution.py:209

commit v4 on v2

--- a/solution.py
+++ b/solution.py
@@ -68,27 +68,53 @@
     )(place, rows, weight)
 
 
-def keep_kernel(place_ref, mine_ref, other_ref, weight_ref, got_mine_ref, got_other_ref, out_ref, padded):
+def keep_kernel(place_ref, mine_ref, other_ref, weight_ref, got_mine_ref, got_other_ref, *refs):
+    own_ref, up1_ref, down1_ref, up2_ref, down2_ref, padded = refs
     hid = weight_ref.shape[0]
     padded[hid:] = jnp.zeros_like(padded[hid:])
     padded[:hid] = weight_ref[...]
-    xl, c = place_ref[0], place_ref[1]
-    for ref, got_ref, core in ((mine_ref, got_mine_ref, c), (other_ref, got_other_ref, 1 - c)):
+    xl, c, low = place_ref[0], place_ref[1], lax.rem(place_ref[3], 4)
+    products = {}
+    for own_core in (True, False):
+        ref, got_ref = (mine_ref, got_mine_ref) if own_core else (other_ref, got_other_ref)
         rows = ref[pl.ds(xl * 4, 4)].reshape(512, ref.shape[2])
         product = times(rows, padded[...])
-        for far in range(4):
-            for half in range(2):
+        core = c if own_core else 1 - c
+        for half in range(2):
+            ahead = lax.rem(core * 2 + half - low + 4, 4)
+            for far in range(4):
                 start = far * 128 + half * 64
-                vals = pack(product[start : start + 64]) + decode(got_ref[half, far])
-                out_ref[core, half, far] = encode(vals)
+                products[own_core, half, far] = pack(product[start : start + 64]) + decode(got_ref[half, far])
+
+            @pl.when(ahead == 0)
+            def _(own_core=own_core, half=half):
+                for far in range(4):
+                    own_ref[far] = products[own_core, half, far]
+
+            @pl.when(ahead == 1)
+            def _(own_core=own_core, half=half):
+                for far in range(4):
+                    up1_ref[far] = encode(products[own_core, half, far])
+
+            @pl.when(ahead == 2)
+            def _(own_core=own_core, half=half):
+                for far in range(4):
+                    out_ref = up2_ref if far < 2 else down2_ref
+                    out_ref[far % 2] = encode(products[own_core, half, far])
+
+            @pl.when(ahead == 3)
+            def _(own_core=own_core, half=half):
+                for far in range(4):
+                    down1_ref[far] = encode(products[own_core, half, far])
 
 
 def keep_part(place, mine, other, weight, got_mine, got_other):
+    shapes = [(4, 208, LANES), (4, 224, LANES), (4, 224, LANES), (2, 224, LANES), (2, 224, LANES)]
     return pl.pallas_call(
         keep_kernel,
-        out_shape=jax.ShapeDtypeStruct((2, 2, 4, 224, LANES), jnp.float32),
+        out_shape=tuple(jax.ShapeDtypeStruct(s, jnp.float32) for s in shapes),
         in_specs=[scalars] + [whole] * 5,
-        out_specs=whole,
+        out_specs=(whole,) * 5,
         scratch_shapes=[pltpu.VMEM((512, weight.shape[1]), weight.dtype)],
         compiler_params=pltpu.CompilerParams(vmem_limit_bytes=VMEM_BYTES),
         cost_estimate=pl.CostEstimate(flops=2 * 1024 * 512 * 512, bytes_accessed=4 << 20, transcendentals=0),
@@ -96,29 +122,34 @@
     )(place, mine, other, weight, got_mine, got_other)
 
 
-def merge_kernel(place_ref, got_ref, own_ref, *out_refs):
-    for k in range(4):
-        far = lax.rem(place_ref[2] + k, 4)
-        vals = decode(got_ref[0, far])
-        for near in range(1, 4):
-            vals += decode(got_ref[near, far])
-        if k == 0:
-            own_ref[...] = vals
-        else:
-            out_refs[k - 1][...] = encode(vals)
-
-
-def merge(place, got):
+def merge_kernel(place_ref, own_ref, up1_ref, down1_ref, up2_ref, down2_ref, total_ref, *out_refs):
+    for far in range(4):
+        twice_ref = up2_ref if far < 2 else down2_ref
+        vals = own_ref[far] + decode(up1_ref[far]) + decode(down1_ref[far]) + decode(twice_ref[far % 2])
+        ahead = lax.rem(far - place_ref[2] + 4, 4)
+
+        @pl.when(ahead == 0)
+        def _(vals=vals):
+            total_ref[...] = vals
+
+        for k in range(1, 4):
+
+            @pl.when(ahead == k)
+            def _(vals=vals, k=k):
+                out_refs[k - 1][...] = encode(vals)
+
+
+def merge(place, parts):
     return pl.pallas_call(
         merge_kernel,
         out_shape=(jax.ShapeDtypeStruct((208, LANES), jnp.float32),)
         + (jax.ShapeDtypeStruct((224, LANES), jnp.float32),) * 3,
-        in_specs=[scalars, whole],
+        in_specs=[scalars] + [whole] * 5,
         out_specs=(whole,) * 4,
         compiler_params=pltpu.CompilerParams(vmem_limit_bytes=VMEM_BYTES),
         cost_estimate=pl.CostEstimate(flops=1 << 20, bytes_accessed=1 << 20, transcendentals=0),
         name="merge_parts",
-    )(place, got)
+    )(place, *parts)
 
 
 def final_kernel(own_ref, a_ref, b_ref, d_ref, gate_ref, up_ref, gate_grad_ref, up_grad_ref):
@@ -148,43 +179,28 @@
     )(*parts, gate_pre, up_pre)
 
 
-def weight_kernel(place_ref, near_ref, up1_ref, down1_ref, up2_ref, down2_ref, mine_ref, other_ref, out_ref, tokens):
-    c, z = place_ref[1], place_ref[3]
-    for ref, shift, begin, count in (
-        (near_ref, 0, 0, 4),
-        (up1_ref, -1, 0, 4),
-        (down1_ref, 1, 0, 4),
-        (up2_ref, -2, 1, 2),
-        (down2_ref, 2, 0, 2),
-    ):
-        for k in range(count):
-            owner = lax.rem(z + shift - 4 * (begin + k - 1) + 32, 16)
-            core = lax.rem(owner // 2, 2)
-            for xl in range(2):
-                start = pl.multiple_of(lax.rem(owner, 2) * 64, 64)
-                tokens[xl, core, owner // 4, pl.ds(start, 64)] = ref[k, xl]
-    hid = out_ref.shape[0]
+def weight_kernel(place_ref, own_ref, partner_ref, mine_ref, other_ref, out_ref):
+    xl, c = place_ref[0], place_ref[1]
     total = None
-    for xl in range(2):
+    for hidden_ref, owner in ((own_ref, xl), (partner_ref, 1 - xl)):
         for ref, core in ((mine_ref, c), (other_ref, 1 - c)):
-            rows = ref[4 * xl : 4 * xl + 4].reshape(512, ref.shape[2])
-            hidden = tokens[xl, core].reshape(512, tokens.shape[4])
-            product = lax.dot_general(hidden, rows, (((0,), (0,)), ((), ())), preferred_element_type=jnp.float32)
+            rows = ref[pl.ds(owner * 4, 4)].reshape(512, ref.shape[2])
+            tokens = jnp.concatenate([hidden_ref[far, core] for far in range(4)], axis=1)
+            product = jnp.dot(tokens, rows, preferred_element_type=jnp.float32)
             total = product if total is None else total + product
-    out_ref[...] = total[:hid] * 2048 ** (-0.5)
-
-
-def weight_part(place, blocks, mine, other, hid):
+    out_ref[...] = total * 2048 ** (-0.5)
+
+
+def weight_part(place, own, partner, mine, other):
     return pl.pallas_call(
         weight_kernel,
-        out_shape=jax.ShapeDtypeStruct((hid, mine.shape[2]), jnp.float32),
-        in_specs=[scalars] + [whole] * 7,
+        out_shape=jax.ShapeDtypeStruct((own.shape[2], mine.shape[2]), jnp.float32),
+        in_specs=[scalars] + [whole] * 4,
         out_specs=whole,
-        scratch_shapes=[pltpu.VMEM((2, 2, 4, 128, 512), mine.dtype)],
         compiler_params=pltpu.CompilerParams(vmem_limit_bytes=VMEM_BYTES),
         cost_estimate=pl.CostEstimate(flops=2 * 2048 * 512 * 512, bytes_accessed=5 << 20, transcendentals=0),
         name="weight_grad",
-    )(place, *blocks, mine, other)
+    )(place, own, partner, mine, other)
 
 
 def shift(array, axes, step):
@@ -193,35 +209,31 @@
 
 
 def shards(gate_pre, up_pre, out_grad, down_weight):
-    xl = lax.axis_index("xl")
-    place = jnp.stack([xl, lax.axis_index("c"), lax.axis_index(FAR), lax.axis_index(Z)]).astype(jnp.int32)
+    place = jnp.stack([lax.axis_index("xl"), lax.axis_index("c"), lax.axis_index(FAR), lax.axis_index(Z)]).astype(jnp.int32)
     hid = gate_pre.shape[1]
     gate_vals = gate_pre.astype(jnp.float32)
     hidden = (gate_vals * jax.nn.sigmoid(gate_vals) * up_pre.astype(jnp.float32)).astype(jnp.bfloat16)
-    hidden = jnp.pad(hidden, ((0, 0), (0, 512 - hid)))
-
-    theirs = lax.ppermute(hidden, "xl", SWAP)
-    pair = jnp.where(xl == 0, jnp.stack([hidden, theirs]), jnp.stack([theirs, hidden]))
-    steps = [shift(pair, FAR, k) for k in (3, 1, 2)]
 
     mine = lax.all_to_all(jnp.broadcast_to(out_grad[None], (8,) + out_grad.shape), YX, 0, 0)
     other = lax.ppermute(mine, "c", SWAP)
 
     sent = [send_part(place, rows, down_weight).astype(jnp.float16) for rows in (mine, other)]
-    sent, pair, steps = lax.optimization_barrier((sent, pair, steps))
+    sent, hidden = lax.optimization_barrier((sent, hidden))
     got = [lax.ppermute(s, "xl", SWAP) for s in sent]
-
-    near = jnp.stack([steps[0], pair, steps[1], steps[2]])
-    blocks = [near, shift(near, Z, 1), shift(near, Z, -1), shift(near[1:3], Z, 2), shift(near[0:2], Z, -2)]
-    got, blocks = lax.optimization_barrier((got, blocks))
+    tokens = lax.all_gather(hidden, Z, axis=0, tiled=True)
+    got, tokens = lax.optimization_barrier((got, tokens))
+    tokens = tokens.reshape(4, 2, 128, hid).transpose(0, 1, 3, 2)
+    theirs = lax.ppermute(tokens, "xl", SWAP)
 
     kept = keep_part(place, mine, other, down_weight, *[g.astype(jnp.float32) for g in got])
-    kept = kept.astype(jnp.float16).reshape(4, 4, 224, LANES)
-    merged = merge(place, lax.all_to_all(kept, ("z1", "z0"), 0, 0).astype(jnp.float32))
+    halves = [k.astype(jnp.float16) for k in kept[1:]]
+    near = [shift(h, Z, step) for h, step in zip(halves, (1, -1, 2, -2), strict=True)]
+    near, theirs = lax.optimization_barrier((near, theirs))
+    merged = merge(place, [kept[0]] + [n.astype(jnp.float32) for n in near])
     far = [shift(merged[k].astype(jnp.float16), FAR, k).astype(jnp.float32) for k in range(1, 4)]
     gate_grad, up_grad = final([merged[0]] + far, gate_pre, up_pre)
 
-    weight_grad = weight_part(place, blocks, mine, other, hid)
+    weight_grad = weight_part(place, tokens, theirs, mine, other)
     return (gate_grad, up_grad, weight_grad)
 
 

time: 161 us -> 134 us (0.83)
  the two profiles are of different devices: /device:TPU:1 before, /device:TPU:6 now
where the time goes in v4:
time: 134 us; the launch traced here: 132 us
  blocking collectives  65.8 us (49%)
  starting transfers between devices  43.4 us (32%)
  Pallas kernels  8.88 us (7%)
  waiting for transfers between devices  6.84 us (5%)
  local copies, waits for them, and re-layouts  4.19 us (3%)
  other arithmetic  1.67 us (1%)
    all_gather x1, blocking collectives, shards(): tokens = lax.all_gather(hidden, Z, axis=0, tiled=True)  43.9 us
    ppermute x7, starting transfers between devices, shift(): lax.ppermute(array, axes, [(i, (i + step) % size) for i in range(size)])  32.8 us
    all_to_all x1, blocking collectives, shards(): lax.all_to_all(jnp.broadcast_to(out_grad[None], (8,) + out_grad.shape), Y...  21.9 us
    ppermute x2, starting transfers between devices, shards(): got = [lax.ppermute(s, 'xl', SWAP) for s in sent]  5.84 us
    ppermute x7, waiting for transfers between devices, shift(): lax.ppermute(array, axes, [(i, (i + step) % size) for i in range(size)])  5.65 us
    ppermute x1, starting transfers between devices, shards(): theirs = lax.ppermute(tokens, 'xl', SWAP)  2.87 us
  transfers between devices with their start and end apart: 11, of which 4 were waited for; matrix products, arithmetic and copies ran while one was open for 1% of the time, Pallas kernels for 4%

profile of v4, /device:TPU:6, one launch (start us, length us, event | category | flops | bytes accessed | tf_op | source)
XLA Modules:
  0.0 131.7 jit_solution(8676218212088902955)
XLA Ops:
  0.6 1.0 broadcast_in_dim.2
  1.7 21.9 %all_to_all.5.rows_ref.mine_ref = bf16[8,128,512]{2,1,0:T(8,128)(2,1)S(1)} all-to-all(bf16[8,128,512]{2,1,0:T(8,128)(2,1)S(1)} %broadcast_in_dim.2), channel_id=1, replica_groups=mesh['xl'=2,'z3'=2,'z2'=2,'z1'=2,'z0'=2,'y1'=2,'y0'=2,'xh'=2,'c'=2] {'y1..., dimensions={0} | all-to-all | bytes 2097152 | tf_op jit(solution)/shard_map/all_to_all | solution.py:217
  23.6 1.9 %collective-permute-start = (bf16[8,128,512]{2,1,0:T(8,128)(2,1)S(1)}, bf16[8,128,512]{2,1,0:T(8,128)(2,1)S(1)}, u32[]{:S(2)}, u32[]{:S(2)}) collective-permute-start(bf16[8,128,512]{2,1,0:T(8,128)(2,1)S(1)} %all_to_all.5.rows_ref.mine_ref), channel_id=1, source_target_pairs={{0,1},{1,0},{2,3},{3,2},{4,5},{5,4},{6,7},{7,6},{8,9},{9,8},{10,11... | collective-permute-start | bytes 3145736 | tf_op jit(solution)/shard_map/ppermute | solution.py:218
  25.5 0.1 pad_add_fusion.place_ref
  25.6 1.2 send_part.2
  26.8 0.1 convert_element_type.63
  26.9 1.2 collective-permute-done.rows_ref.other_ref
  28.1 1.2 send_part.3
  29.3 0.1 convert_element_type.64
  29.4 2.7 %collective-permute-start.1 = (f16[2,4,224,128]{3,2,1,0:T(8,128)(2,1)S(1)}, f16[2,4,224,128]{3,2,1,0:T(8,128)(2,1)S(1)}, u32[]{:S(2)}, u32[]{:S(2)}) collective-permute-start(f16[2,4,224,128]{3,2,1,0:T(8,128)(2,1)S(1)} %convert_element_type.63), channel_id=1, source_target_pairs={{0,256},{256,0},{1,257},{257,1},{2,258},{258,2},{3,259},{259,3},{4... | collective-permute-start | bytes 1376264 | tf_op jit(solution)/shard_map/ppermute | solution.py:222
  32.1 3.1 %collective-permute-start.2 = (f16[2,4,224,128]{3,2,1,0:T(8,128)(2,1)S(1)}, f16[2,4,224,128]{3,2,1,0:T(8,128)(2,1)S(1)}, u32[]{:S(2)}, u32[]{:S(2)}) collective-permute-start(f16[2,4,224,128]{3,2,1,0:T(8,128)(2,1)S(1)} %convert_element_type.64), channel_id=1, source_target_pairs={{0,256},{256,0},{1,257},{257,1},{2,258},{258,2},{3,259},{259,3},{4... | collective-permute-start | bytes 1376264 | tf_op jit(solution)/shard_map/ppermute | solution.py:222
  35.2 43.9 %all_gather.3 = bf16[1024,416]{1,0:T(8,128)(2,1)} all-gather(bf16[64,416]{1,0:T(8,128)(2,1)S(1)} %fusion.4), channel_id=1, replica_groups=mesh['xl'=2,'z3'=2,'z2'=2,'z1'=2,'z0'=2,'y1'=2,'y0'=2,'xh'=2,'c'=2] {'z3..., dimensions={0}, use_global_device_ids=true | all-gather | bytes 905216 | tf_op jit(solution)/shard_map/all_gather | solution.py:223
  79.1 0.8 copy-done.3
  79.9 0.8 copy-done.4
  80.7 1.6 %copy.8 = bf16[4,2,128,416]{2,3,1,0:T(8,128)(2,1)S(1)} copy(bf16[4,2,128,416]{3,2,1,0:T(8,128)(2,1)} %bitcast.8) | data formatting | bytes 1703936 | tf_op jit(solution)/shard_map/reshape | solution.py:225
  82.3 2.9 %collective-permute-start.7 = (bf16[4,2,416,128]{3,2,1,0:T(8,128)(2,1)S(1)}, bf16[4,2,416,128]{3,2,1,0:T(8,128)(2,1)S(1)}, u32[]{:S(2)}, u32[]{:S(2)}) collective-permute-start(bf16[4,2,416,128]{3,2,1,0:T(8,128)(2,1)S(1)} %bitcast.6), channel_id=1, source_target_pairs={{0,256},{256,0},{1,257},{257,1},{2,258},{258,2},{3,259},{259,3},{4... | collective-permute-start | bytes 2555912 | tf_op jit(solution)/shard_map/ppermute | solution.py:226
  85.2 1.1 convert_element_type.68.got_mine_ref
  86.3 0.1 convert_element_type.69.got_other_ref
  86.3 2.2 %keep_part.1 = (f32[4,208,128]{2,1,0:T(8,128)S(1)}, f32[4,224,128]{2,1,0:T(8,128)S(1)}, f32[4,224,128]{2,1,0:T(8,128)S(1)}, f32[2,224,128]{2,1,0:T(8,128)S(1)}, f32[2,224,128]{2,1,0:T(8,128)S(1)}) custom-call(s32[4]{0:T(128)S(1)} %pad_add_fusion.place_ref, bf16[8,128,512]{2,1,0:T(8,128)(2,1)S(1)} %all_to_all.5.rows_ref.mine_ref, ...), custom_call_target="tpu_custom_call" | custom-call | flops 536870912 | bytes 4194304 | tf_op jit(solution)/shard_map/keep_part/pallas_call | solution.py:113
  88.6 1.9 %collective-permute-start.3 = (f16[4,224,128]{2,1,0:T(8,128)(2,1)S(1)}, f16[4,224,128]{2,1,0:T(8,128)(2,1)S(1)}, u32[]{:S(2)}, u32[]{:S(2)}) collective-permute-start(f16[4,224,128]{2,1,0:T(8,128)(2,1)S(1)} %convert_element_type.70), channel_id=1, source_target_pairs={{0,16},{16,32},{32,48},{48,64},{64,80},{80,96},{96,112},{112,128},... | collective-permute-start | bytes 688136 | tf_op jit(solution)/shard_map/ppermute | solution.py:208
  90.6 5.1 %collective-permute-start.4 = (f16[4,224,128]{2,1,0:T(8,128)(2,1)S(1)}, f16[4,224,128]{2,1,0:T(8,128)(2,1)S(1)}, u32[]{:S(2)}, u32[]{:S(2)}) collective-permute-start(f16[4,224,128]{2,1,0:T(8,128)(2,1)S(1)} %convert_element_type.71), channel_id=1, source_target_pairs={{0,240},{16,0},{32,16},{48,32},{64,48},{80,64},{96,80},{112,96},{1... | collective-permute-start | bytes 688136 | tf_op jit(solution)/shard_map/ppermute | solution.py:208
  95.7 1.9 %collective-permute-start.5 = (f16[2,224,128]{2,1,0:T(8,128)(2,1)S(1)}, f16[2,224,128]{2,1,0:T(8,128)(2,1)S(1)}, u32[]{:S(2)}, u32[]{:S(2)}) collective-permute-start(f16[2,224,128]{2,1,0:T(8,128)(2,1)S(1)} %convert_element_type.72), channel_id=1, source_target_pairs={{0,32},{16,48},{32,64},{48,80},{64,96},{80,112},{96,128},{112,144}... | collective-permute-start | bytes 344072 | tf_op jit(solution)/shard_map/ppermute | solution.py:208
  97.7 6.0 %collective-permute-start.6 = (f16[2,224,128]{2,1,0:T(8,128)(2,1)S(1)}, f16[2,224,128]{2,1,0:T(8,128)(2,1)S(1)}, u32[]{:S(2)}, u32[]{:S(2)}) collective-permute-start(f16[2,224,128]{2,1,0:T(8,128)(2,1)S(1)} %convert_element_type.73), channel_id=1, source_target_pairs={{0,224},{16,240},{32,0},{48,16},{64,32},{80,48},{96,64},{112,80},{... | collective-permute-start | bytes 344072 | tf_op jit(solution)/shard_map/ppermute | solution.py:208
  103.7 0.8 collective-permute-done.5
  104.5 2.2 %collective-permute-done.6 = f16[2,224,128]{2,1,0:T(8,128)(2,1)S(1)} collective-permute-done((f16[2,224,128]{2,1,0:T(8,128)(2,1)S(1)}, f16[2,224,128]{2,1,0:T(8,128)(2,1)S(1)}, u32[]{:S(2)}, u32[]{:S(2)}) %collective-permute-start.6) | collective-permute-done | bytes 114720 | tf_op jit(solution)/shard_map/ppermute | solution.py:208
  106.9 1.0 merge_parts.1
  108.0 5.0 %collective-permute-start.8 = (f16[224,128]{1,0:T(8,128)(2,1)S(1)}, f16[224,128]{1,0:T(8,128)(2,1)S(1)}, u32[]{:S(2)}, u32[]{:S(2)}) collective-permute-start(f16[224,128]{1,0:T(8,128)(2,1)S(1)} %convert_element_type.78), channel_id=1, source_target_pairs={{0,64},{64,128},{128,192},{192,0},{1,65},{65,129},{129,193},{193,1... | collective-permute-start | bytes 172040 | tf_op jit(solution)/shard_map/ppermute | solution.py:208
  113.0 7.3 %collective-permute-start.9 = (f16[224,128]{1,0:T(8,128)(2,1)S(1)}, f16[224,128]{1,0:T(8,128)(2,1)S(1)}, u32[]{:S(2)}, u32[]{:S(2)}) collective-permute-start(f16[224,128]{1,0:T(8,128)(2,1)S(1)} %convert_element_type.80), channel_id=1, source_target_pairs={{0,128},{64,192},{128,0},{192,64},{1,129},{65,193},{129,1},{193,65... | collective-permute-start | bytes 172040 | tf_op jit(solution)/shard_map/ppermute | solution.py:208
  120.3 5.5 %collective-permute-start.10 = (f16[224,128]{1,0:T(8,128)(2,1)S(1)}, f16[224,128]{1,0:T(8,128)(2,1)S(1)}, u32[]{:S(2)}, u32[]{:S(2)}) collective-permute-start(f16[224,128]{1,0:T(8,128)(2,1)S(1)} %convert_element_type.82), channel_id=1, source_target_pairs={{0,192},{64,0},{128,64},{192,128},{1,193},{65,1},{129,65},{193,129... | collective-permute-start | bytes 172040 | tf_op jit(solution)/shard_map/ppermute | solution.py:208
  125.8 2.5 %weight_grad.1 = f32[416,512]{1,0:T(8,128)} custom-call(s32[4]{0:T(128)S(1)} %pad_add_fusion.place_ref, bf16[4,2,416,128]{3,2,1,0:T(8,128)(2,1)S(1)} %bitcast.7, bf16[4,2,416,128]{3,2,1,0:T(8,128)(2,1)S(1)} %collective-permute-done.7.partner_ref, bf16[8,128,512]{2,1,0:T(8,128)(2,1)S(1)} %all_to_all.5.rows_ref.mine_ref, ...), custom_call_target="tpu_custom_call" | custom-call | flops 1073741824 | bytes 5242880 | tf_op jit(solution)/shard_map/weight_grad/pallas_call | solution.py:195
  128.3 2.6 %collective-permute-done.10 = f16[224,128]{1,0:T(8,128)(2,1)S(1)} collective-permute-done((f16[224,128]{1,0:T(8,128)(2,1)S(1)}, f16[224,128]{1,0:T(8,128)(2,1)S(1)}, u32[]{:S(2)}, u32[]{:S(2)}) %collective-permute-start.10) | collective-permute-done | bytes 57376 | tf_op jit(solution)/shard_map/ppermute | solution.py:208
  131.0 0.7 finish_grads.1
  (32 shorter events, 0.4 us)
Async XLA Ops:
  1.6 23.9 %copy-start.1 = (bf16[64,416]{1,0:T(8,128)(2,1)S(1)}, bf16[64,416]{1,0:T(8,128)(2,1)}, u32[]{:S(2)}) copy-start(bf16[64,416]{1,0:T(8,128)(2,1)} %gate_ref.1) | copy-start | bytes 159748
  1.6 23.9 %copy-start.2 = (bf16[64,416]{1,0:T(8,128)(2,1)S(1)}, bf16[64,416]{1,0:T(8,128)(2,1)}, u32[]{:S(2)}) copy-start(bf16[64,416]{1,0:T(8,128)(2,1)} %up_ref.1) | copy-start | bytes 159748
  1.6 24.0 %copy-start = (bf16[416,512]{1,0:T(8,128)(2,1)S(1)}, bf16[416,512]{1,0:T(8,128)(2,1)}, u32[]{:S(2)}) copy-start(bf16[416,512]{1,0:T(8,128)(2,1)} %weight_ref.5) | copy-start | bytes 1277956
  23.6 4.5 %collective-permute-start = (bf16[8,128,512]{2,1,0:T(8,128)(2,1)S(1)}, bf16[8,128,512]{2,1,0:T(8,128)(2,1)S(1)}, u32[]{:S(2)}, u32[]{:S(2)}) collective-permute-start(bf16[8,128,512]{2,1,0:T(8,128)(2,1)S(1)} %all_to_all.5.rows_ref.mine_ref), channel_id=1, source_target_pairs={{0,1},{1,0},{2,3},{3,2},{4,5},{5,4},{6,7},{7,6},{8,9},{9,8},{10,11... | collective-permute-start | bytes 3145736 | tf_op jit(solution)/shard_map/ppermute | solution.py:218
  29.4 49.7 %collective-permute-start.1 = (f16[2,4,224,128]{3,2,1,0:T(8,128)(2,1)S(1)}, f16[2,4,224,128]{3,2,1,0:T(8,128)(2,1)S(1)}, u32[]{:S(2)}, u32[]{:S(2)}) collective-permute-start(f16[2,4,224,128]{3,2,1,0:T(8,128)(2,1)S(1)} %convert_element_type.63), channel_id=1, source_target_pairs={{0,256},{256,0},{1,257},{257,1},{2,258},{258,2},{3,259},{259,3},{4... | collective-permute-start | bytes 1376264 | tf_op jit(solution)/shard_map/ppermute | solution.py:222
  32.1 47.0 %collective-permute-start.2 = (f16[2,4,224,128]{3,2,1,0:T(8,128)(2,1)S(1)}, f16[2,4,224,128]{3,2,1,0:T(8,128)(2,1)S(1)}, u32[]{:S(2)}, u32[]{:S(2)}) collective-permute-start(f16[2,4,224,128]{3,2,1,0:T(8,128)(2,1)S(1)} %convert_element_type.64), channel_id=1, source_target_pairs={{0,256},{256,0},{1,257},{257,1},{2,258},{258,2},{3,259},{259,3},{4... | collective-permute-start | bytes 1376264 | tf_op jit(solution)/shard_map/ppermute | solution.py:222
  79.1 0.8 copy-start.3
  79.9 0.8 copy-start.4
  82.3 4.0 %copy-start.5 = (f16[2,4,224,128]{3,2,1,0:T(8,128)(2,1)S(1)}, f16[2,4,224,128]{3,2,1,0:T(8,128)(2,1)}, u32[]{:S(2)}) copy-start(f16[2,4,224,128]{3,2,1,0:T(8,128)(2,1)} %copy-done.4) | copy-start | bytes 1376260
  82.3 24.5 %collective-permute-start.7 = (bf16[4,2,416,128]{3,2,1,0:T(8,128)(2,1)S(1)}, bf16[4,2,416,128]{3,2,1,0:T(8,128)(2,1)S(1)}, u32[]{:S(2)}, u32[]{:S(2)}) collective-permute-start(bf16[4,2,416,128]{3,2,1,0:T(8,128)(2,1)S(1)} %bitcast.6), channel_id=1, source_target_pairs={{0,256},{256,0},{1,257},{257,1},{2,258},{258,2},{3,259},{259,3},{4... | collective-permute-start | bytes 2555912 | tf_op jit(solution)/shard_map/ppermute | solution.py:226
  88.6 18.2 %collective-permute-start.3 = (f16[4,224,128]{2,1,0:T(8,128)(2,1)S(1)}, f16[4,224,128]{2,1,0:T(8,128)(2,1)S(1)}, u32[]{:S(2)}, u32[]{:S(2)}) collective-permute-start(f16[4,224,128]{2,1,0:T(8,128)(2,1)S(1)} %convert_element_type.70), channel_id=1, source_target_pairs={{0,16},{16,32},{32,48},{48,64},{64,80},{80,96},{96,112},{112,128},... | collective-permute-start | bytes 688136 | tf_op jit(solution)/shard_map/ppermute | solution.py:208
  90.6 16.2 %collective-permute-start.4 = (f16[4,224,128]{2,1,0:T(8,128)(2,1)S(1)}, f16[4,224,128]{2,1,0:T(8,128)(2,1)S(1)}, u32[]{:S(2)}, u32[]{:S(2)}) collective-permute-start(f16[4,224,128]{2,1,0:T(8,128)(2,1)S(1)} %convert_element_type.71), channel_id=1, source_target_pairs={{0,240},{16,0},{32,16},{48,32},{64,48},{80,64},{96,80},{112,96},{1... | collective-permute-start | bytes 688136 | tf_op jit(solution)/shard_map/ppermute | solution.py:208
  95.7 8.8 %collective-permute-start.5 = (f16[2,224,128]{2,1,0:T(8,128)(2,1)S(1)}, f16[2,224,128]{2,1,0:T(8,128)(2,1)S(1)}, u32[]{:S(2)}, u32[]{:S(2)}) collective-permute-start(f16[2,224,128]{2,1,0:T(8,128)(2,1)S(1)} %convert_element_type.72), channel_id=1, source_target_pairs={{0,32},{16,48},{32,64},{48,80},{64,96},{80,112},{96,128},{112,144}... | collective-permute-start | bytes 344072 | tf_op jit(solution)/shard_map/ppermute | solution.py:208
  97.7 9.1 %collective-permute-start.6 = (f16[2,224,128]{2,1,0:T(8,128)(2,1)S(1)}, f16[2,224,128]{2,1,0:T(8,128)(2,1)S(1)}, u32[]{:S(2)}, u32[]{:S(2)}) collective-permute-start(f16[2,224,128]{2,1,0:T(8,128)(2,1)S(1)} %convert_element_type.73), channel_id=1, source_target_pairs={{0,224},{16,240},{32,0},{48,16},{64,32},{80,48},{96,64},{112,80},{... | collective-permute-start | bytes 344072 | tf_op jit(solution)/shard_map/ppermute | solution.py:208
  108.0 20.3 %collective-permute-start.8 = (f16[224,128]{1,0:T(8,128)(2,1)S(1)}, f16[224,128]{1,0:T(8,128)(2,1)S(1)}, u32[]{:S(2)}, u32[]{:S(2)}) collective-permute-start(f16[224,128]{1,0:T(8,128)(2,1)S(1)} %convert_element_type.78), channel_id=1, source_target_pairs={{0,64},{64,128},{128,192},{192,0},{1,65},{65,129},{129,193},{193,1... | collective-permute-start | bytes 172040 | tf_op jit(solution)/shard_map/ppermute | solution.py:208
  113.0 15.3 %collective-permute-start.9 = (f16[224,128]{1,0:T(8,128)(2,1)S(1)}, f16[224,128]{1,0:T(8,128)(2,1)S(1)}, u32[]{:S(2)}, u32[]{:S(2)}) collective-permute-start(f16[224,128]{1,0:T(8,128)(2,1)S(1)} %convert_element_type.80), channel_id=1, source_target_pairs={{0,128},{64,192},{128,0},{192,64},{1,129},{65,193},{129,1},{193,65... | collective-permute-start | bytes 172040 | tf_op jit(solution)/shard_map/ppermute | solution.py:208
  120.3 10.6 %collective-permute-start.10 = (f16[224,128]{1,0:T(8,128)(2,1)S(1)}, f16[224,128]{1,0:T(8,128)(2,1)S(1)}, u32[]{:S(2)}, u32[]{:S(2)}) collective-permute-start(f16[224,128]{1,0:T(8,128)(2,1)S(1)} %convert_element_type.82), channel_id=1, source_target_pairs={{0,192},{64,0},{128,64},{192,128},{1,193},{65,1},{129,65},{193,129... | collective-permute-start | bytes 172040 | tf_op jit(solution)/shard_map/ppermute | solution.py:208

commit v5 on v4

v5 whole, which is shorter than its diff:
```python
import functools

import jax
import jax.numpy as jnp
import numpy as np
from jax import lax
from jax.experimental import pallas as pl
from jax.experimental.pallas import tpu as pltpu
from jax.sharding import Mesh, PartitionSpec as P

Z = ("z3", "z2", "z1", "z0")
FAR = Z[:2]
DP = ("xl",) + Z
YX = ("y1", "y0", "xh")
TENSOR = YX + ("c",)
SWAP = [(0, 1), (1, 0)]
TURN = [(0, 0), (1, 2), (2, 1), (3, 3)]
LANES = 128
VMEM_BYTES = 32 * 1024 * 1024
whole = pl.BlockSpec(memory_space=pltpu.VMEM)
scalars = pl.BlockSpec(memory_space=pltpu.SMEM)


def pack(block):
    tail = block[:, 3 * LANES :]
    packed = tail[0:16]
    for k in range(1, 4):
        packed += pltpu.roll(tail[16 * k : 16 * k + 16], 32 * k, 1)
    return jnp.concatenate([block[:, LANES * k : LANES * (k + 1)] for k in range(3)] + [packed], axis=0)


def encode(packed):
    top = jnp.max(jnp.max(jnp.abs(packed), axis=0, keepdims=True), axis=1, keepdims=True)
    exponent = jnp.floor(jnp.log2(jnp.maximum(top, 1e-37)))
    scaled = packed * jnp.exp2(-exponent)
    return jnp.concatenate([scaled, jnp.broadcast_to(exponent, (16, LANES))], axis=0)


def decode(coded):
    return coded[:208] * jnp.exp2(coded[208:209])


def times(rows, weight):
    return lax.dot_general(rows, weight, (((1,), (1,)), ((), ())), preferred_element_type=jnp.float32)


def keep_kernel(place_ref, grad_ref, own_weight_ref, their_weight_ref, *refs):
    own_ref, up1_ref, down1_ref, up2_ref, down2_ref, padded = refs
    hid, feats = own_weight_ref.shape
    xl, low = place_ref[0], place_ref[1]
    padded[:, hid:] = jnp.zeros_like(padded[:, hid:])
    padded[xl, :hid] = own_weight_ref[...]
    padded[1 - xl, :hid] = their_weight_ref[...]
    for y1 in range(2):
        product = sum(times(grad_ref[y1 * 4 : y1 * 4 + 4, k].reshape(512, feats), padded[k]) for k in range(2))
        for half in range(2):
            ahead = lax.rem(y1 * 2 + half - low + 4, 4)
            vals = [pack(product[far * 128 + half * 64 :][:64]) for far in range(4)]

            @pl.when(ahead == 0)
            def _(vals=vals):
                for far in range(4):
                    own_ref[far] = vals[far]

            @pl.when(ahead == 1)
            def _(vals=vals):
                for far in range(4):
                    up1_ref[far] = encode(vals[far])

            @pl.when(ahead == 2)
            def _(vals=vals):
                for far in range(4):
                    out_ref = up2_ref if far < 2 else down2_ref
                    out_ref[far % 2] = encode(vals[far])

            @pl.when(ahead == 3)
            def _(vals=vals):
                for far in range(4):
                    down1_ref[far] = encode(vals[far])


def keep_part(place, grad, own_weight, their_weight):
    shapes = [(4, 208, LANES), (4, 224, LANES), (4, 224, LANES), (2, 224, LANES), (2, 224, LANES)]
    return pl.pallas_call(
        keep_kernel,
        out_shape=tuple(jax.ShapeDtypeStruct(s, jnp.float32) for s in shapes),
        in_specs=[scalars] + [whole] * 3,
        out_specs=(whole,) * 5,
        scratch_shapes=[pltpu.VMEM((2, 512, own_weight.shape[1]), own_weight.dtype)],
        compiler_params=pltpu.CompilerParams(vmem_limit_bytes=VMEM_BYTES),
        cost_estimate=pl.CostEstimate(flops=2 * 1024 * 1024 * 512, bytes_accessed=4 << 20, transcendentals=0),
        name="keep_part",
    )(place, grad, own_weight, their_weight)


def merge_kernel(place_ref, own_ref, up1_ref, down1_ref, up2_ref, down2_ref, *out_refs):
    for far in range(4):
        twice_ref = up2_ref if far < 2 else down2_ref
        vals = own_ref[far] + decode(up1_ref[far]) + decode(down1_ref[far]) + decode(twice_ref[far % 2])
        ahead = lax.rem(far - place_ref[2] + 4, 4)
        for k in range(4):

            @pl.when(ahead == k)
            def _(vals=vals, k=k):
                out_refs[k][...] = encode(vals)


def merge(place, parts):
    return pl.pallas_call(
        merge_kernel,
        out_shape=(jax.ShapeDtypeStruct((224, LANES), jnp.float32),) * 4,
        in_specs=[scalars] + [whole] * 5,
        out_specs=(whole,) * 4,
        compiler_params=pltpu.CompilerParams(vmem_limit_bytes=VMEM_BYTES),
        cost_estimate=pl.CostEstimate(flops=1 << 20, bytes_accessed=1 << 20, transcendentals=0),
        name="merge_parts",
    )(place, *parts)


def final_kernel(a_ref, b_ref, d_ref, e_ref, gate_ref, up_ref, gate_grad_ref, up_grad_ref):
    packed = decode(a_ref[...]) + decode(b_ref[...]) + decode(d_ref[...]) + decode(e_ref[...])
    tail = packed[192:208]
    tails = jnp.concatenate([tail] + [pltpu.roll(tail, LANES - 32 * k, 1) for k in range(1, 4)], axis=0)
    width = gate_ref.shape[1]
    for k in range(4):
        cols = slice(LANES * k, min(LANES * (k + 1), width))
        grad = packed[64 * k : 64 * k + 64] if k < 3 else tails[:, : width - 3 * LANES]
        gate = gate_ref[:, cols].astype(jnp.float32)
        up = up_ref[:, cols].astype(jnp.float32)
        s = jax.nn.sigmoid(gate)
        gate_grad_ref[:, cols] = (grad * up * s * (1.0 + gate * (1.0 - s))).astype(gate_grad_ref.dtype)
        up_grad_ref[:, cols] = (grad * (gate * s)).astype(up_grad_ref.dtype)


def final(parts, gate_pre, up_pre):
    return pl.pallas_call(
        final_kernel,
        out_shape=(jax.ShapeDtypeStruct(gate_pre.shape, gate_pre.dtype),) * 2,
        in_specs=[whole] * 6,
        out_specs=(whole, whole),
        compiler_params=pltpu.CompilerParams(vmem_limit_bytes=VMEM_BYTES),
        cost_estimate=pl.CostEstimate(flops=1, bytes_accessed=1, transcendentals=0),
        name="finish_grads",
    )(*parts, gate_pre, up_pre)


def weight_kernel(place_ref, hidden_ref, grad_ref, own_ref, their_ref):
    xl = place_ref[0]
    feats = own_ref.shape[1]
    tokens = [hidden_ref[:, y1].reshape(512, hidden_ref.shape[3]) for y1 in range(2)]
    for out_ref, k in ((their_ref, 1 - xl), (own_ref, xl)):
        out_ref[...] = sum(
            lax.dot_general(
                tokens[y1],
                grad_ref[y1 * 4 : y1 * 4 + 4, k].reshape(512, feats),
                (((0,), (0,)), ((), ())),
                preferred_element_type=jnp.float32,
            )
            for y1 in range(2)
        )


def weight_part(place, hidden, grad):
    return pl.pallas_call(
        weight_kernel,
        out_shape=(jax.ShapeDtypeStruct((hidden.shape[3], grad.shape[3]), jnp.float32),) * 2,
        in_specs=[scalars] + [whole] * 2,
        out_specs=(whole, whole),
        compiler_params=pltpu.CompilerParams(vmem_limit_bytes=VMEM_BYTES),
        cost_estimate=pl.CostEstimate(flops=2 * 2048 * 512 * 512, bytes_accessed=5 << 20, transcendentals=0),
        name="weight_part",
    )(place, hidden, grad)


def shift(array, axes, step):
    size = 2 ** len(axes)
    return lax.ppermute(array, axes, [(i, (i + step) % size) for i in range(size)])


def to_owner(array, step):
    pairs = [
        (a * 8 + far * 2 + b, b * 8 + (far + step) % 4 * 2 + a) for a in range(2) for far in range(4) for b in range(2)
    ]
    return lax.ppermute(array, ("xl",) + FAR + ("z1",), pairs)


def shards(gate_pre, up_pre, out_grad, down_weight):
    place = jnp.stack([lax.axis_index("xl"), lax.axis_index(Z[2:]), lax.axis_index(FAR)]).astype(jnp.int32)
    hid, feats = down_weight.shape
    gate_vals = gate_pre.astype(jnp.float32)
    hidden = (gate_vals * jax.nn.sigmoid(gate_vals) * up_pre.astype(jnp.float32)).astype(jnp.bfloat16)

    hidden = lax.ppermute(hidden, ("xl", "z1"), TURN)
    turned = lax.ppermute(out_grad, ("xl", "c"), TURN)
    their_weight = lax.ppermute(down_weight, "xl", SWAP)
    hidden, turned = lax.optimization_barrier((hidden, turned))
    grad = lax.all_to_all(jnp.broadcast_to(turned[None], (16,) + turned.shape), TENSOR, 0, 0)
    tokens = lax.all_gather(hidden, Z, axis=0, tiled=True)
    grad, tokens, their_weight = lax.optimization_barrier((grad, tokens, their_weight))
    grad = grad.reshape(8, 2, 128, feats)

    kept = keep_part(place, grad, down_weight, their_weight)
    halves = [k.astype(jnp.float16) for k in kept[1:]]
    near = [shift(h, Z, step) for h, step in zip(halves, (1, -1, 2, -2), strict=True)]
    own, theirs = weight_part(place, tokens.reshape(4, 2, 128, hid), grad)
    near, theirs = lax.optimization_barrier((near, theirs))
    merged = merge(place, [kept[0]] + [n.astype(jnp.float32) for n in near])
    got = lax.ppermute(theirs, "xl", SWAP)
    far = [to_owner(m.astype(jnp.float16), k).astype(jnp.float32) for k, m in enumerate(merged)]
    gate_grad, up_grad = final(far, gate_pre, up_pre)
    weight_grad = (own + got) * 2048 ** (-0.5)
    return (gate_grad, up_grad, weight_grad)


def solution(mesh):
    bits = Mesh(np.asarray(mesh.devices).reshape((2,) * 9), DP + TENSOR)
    return jax.shard_map(
        shards,
        mesh=bits,
        in_specs=(P(DP, TENSOR), P(DP, TENSOR), P(TENSOR, DP), P(TENSOR, DP)),
        out_specs=(P(DP, TENSOR), P(DP, TENSOR), P(TENSOR, DP)),
        check_vma=False,
    )
```

time: 134 us -> 126 us (0.940); the launches traced: 132 us -> 126 us
  blocking collectives: 65.8 us -> 43 us
  starting transfers between devices: 43.4 us -> 56.1 us
  waiting for transfers between devices: 6.84 us -> 14.7 us
  local copies, waits for them, and re-layouts: 4.19 us -> 1.56 us
  Pallas kernels: 8.88 us -> 6.91 us
    ppermute x4 -> x8, starting transfers between devices: 10.6 us -> 33.6 us  [the longest x4 22.8 us: to_owner(): return lax.ppermute(array, ('xl',) + FAR + ('z1',), pairs)]
    all_to_all x1 -> x0, blocking collectives: 21.9 us -> none  [shards(): lax.all_to_all(jnp.broadcast_to(out_grad[None], (8,) + out_grad.shape), Y...]
    ppermute x7 -> x4, starting transfers between devices: 32.8 us -> 15 us  [shift(): lax.ppermute(array, axes, [(i, (i + step) % size) for i in range(size)])]
    ppermute x4 -> x8, waiting for transfers between devices: 1.19 us -> 13.3 us  [the longest x4 9.56 us: to_owner(): return lax.ppermute(array, ('xl',) + FAR + ('z1',), pairs)]
    all_to_all x0 -> x1, starting transfers between devices: none -> 7.45 us  [shards(): lax.all_to_all(jnp.broadcast_to(turned[None], (16,) + turned.shape), TENS...]
    ppermute x7 -> x4, waiting for transfers between devices: 5.65 us -> 1.39 us  [shift(): lax.ppermute(array, axes, [(i, (i + step) % size) for i in range(size)])]
    pallas_call x4 -> x2, Pallas kernels: 5.92 us -> 2.74 us  [the longest x1 1.62 us: weight_part(): pl.pallas_call(weight_kernel, out_shape=(jax.ShapeDtypeStruct((hidden.sha...]
    reshape x1 -> x0, local copies, waits for them, and re-layouts: 1.62 us -> none  [shards(): tokens = tokens.reshape(4, 2, 128, hid).transpose(0, 1, 3, 2)]
  transfers between devices with their start and end apart: 11 -> 13, of which waited for: 4 -> 4; matrix products, arithmetic and copies ran while one was open for 1% -> 1% of each run, Pallas kernels for 4% -> 3%
where the time goes in v5:
time: 126 us
  starting transfers between devices  56.1 us (45%)
  blocking collectives  43 us (34%)
  waiting for transfers between devices  14.7 us (12%)
  Pallas kernels  6.91 us (5%)
  other arithmetic  2.37 us (2%)
  local copies, waits for them, and re-layouts  1.56 us (1%)
    all_gather x1, blocking collectives, shards(): tokens = lax.all_gather(hidden, Z, axis=0, tiled=True)  43 us
    ppermute x4, starting transfers between devices, to_owner(): return lax.ppermute(array, ('xl',) + FAR + ('z1',), pairs)  22.8 us
    ppermute x4, starting transfers between devices, shift(): lax.ppermute(array, axes, [(i, (i + step) % size) for i in range(size)])  15 us
    ppermute x4, waiting for transfers between devices, to_owner(): return lax.ppermute(array, ('xl',) + FAR + ('z1',), pairs)  9.56 us
    all_to_all x1, starting transfers between devices, shards(): lax.all_to_all(jnp.broadcast_to(turned[None], (16,) + turned.shape), TENS...  7.45 us
    ppermute x1, starting transfers between devices, shards(): hidden = lax.ppermute(hidden, ('xl', 'z1'), TURN)  4.82 us
    ppermute x1, waiting for transfers between devices, shards(): hidden = lax.ppermute(hidden, ('xl', 'z1'), TURN)  3.75 us
    pallas_call x1, Pallas kernels, keep_part(): pl.pallas_call(keep_kernel, out_shape=tuple((jax.ShapeDtypeStruct(s, jnp....  3.42 us
  transfers between devices with their start and end apart: 13, of which 4 were waited for; matrix products, arithmetic and copies ran while one was open for 1% of the time, Pallas kernels for 3%

profile of v5, /device:TPU:6, one launch (start us, length us, event | category | flops | bytes accessed | tf_op | source)
XLA Modules:
  0.0 125.6 jit_solution(16690228848692411162)
XLA Ops:
  0.6 2.2 %collective-permute-start.1 = (bf16[128,512]{1,0:T(8,128)(2,1)}, bf16[128,512]{1,0:T(8,128)(2,1)S(1)}, u32[]{:S(2)}, u32[]{:S(2)}) collective-permute-start(bf16[128,512]{1,0:T(8,128)(2,1)} %param.6), channel_id=1, source_target_pairs={{0,0},{1,256},{256,1},{257,257},{2,2},{3,258},{258,3},{259,259},{4... | collective-permute-start | bytes 393224 | tf_op jit(solution)/shard_map/ppermute | solution.py:194
  2.8 0.9 fusion.4
  3.7 4.8 %collective-permute-start = (bf16[64,416]{1,0:T(8,128)(2,1)S(1)}, bf16[64,416]{1,0:T(8,128)(2,1)S(1)}, u32[]{:S(2)}, u32[]{:S(2)}) collective-permute-start(bf16[64,416]{1,0:T(8,128)(2,1)S(1)} %fusion.4), channel_id=1, source_target_pairs={{0,0},{32,256},{256,32},{288,288},{1,1},{33,257},{257,33},{289,289... | collective-permute-start | bytes 159752 | tf_op jit(solution)/shard_map/ppermute | solution.py:193
  8.6 3.7 %collective-permute-done = bf16[64,416]{1,0:T(8,128)(2,1)S(1)} collective-permute-done((bf16[64,416]{1,0:T(8,128)(2,1)S(1)}, bf16[64,416]{1,0:T(8,128)(2,1)S(1)}, u32[]{:S(2)}, u32[]{:S(2)}) %collective-permute-start) | collective-permute-done | bytes 53280 | tf_op jit(solution)/shard_map/ppermute | solution.py:193
  12.3 0.0 collective-permute-done.1
  12.3 1.5 %broadcast_in_dim.2 = bf16[16,128,512]{2,1,0:T(8,128)(2,1)} broadcast(bf16[128,512]{1,0:T(8,128)(2,1)S(1)} %collective-permute-done.1), dimensions={1,2} | broadcast | bytes 2228224 | tf_op jit(solution)/shard_map/broadcast_in_dim | solution.py:197
  13.9 7.4 %all-to-all-start = ((bf16[16,128,512]{2,1,0:T(8,128)(2,1)}), bf16[16,128,512]{2,1,0:T(8,128)(2,1)S(1)}, u32[]{:S(2)}, u32[]{:S(2)}) async-start(bf16[16,128,512]{2,1,0:T(8,128)(2,1)} %broadcast_in_dim.2), calls=%async_computation | async-start | bytes 4194304 | tf_op jit(solution)/shard_map/all_to_all | solution.py:197
  21.3 1.9 %collective-permute-start.2 = (bf16[416,512]{1,0:T(8,128)(2,1)}, bf16[416,512]{1,0:T(8,128)(2,1)}, u32[]{:S(2)}, u32[]{:S(2)}) collective-permute-start(bf16[416,512]{1,0:T(8,128)(2,1)} %own_weight_ref.1), channel_id=1, source_target_pairs={{0,256},{256,0},{1,257},{257,1},{2,258},{258,2},{3,259},{259,3},{4... | collective-permute-start | bytes 1277960 | tf_op jit(solution)/shard_map/ppermute | solution.py:195
  23.2 0.1 pad_add_fusion.place_ref
  23.3 43.0 %all_gather.3 = bf16[1024,416]{1,0:T(8,128)(2,1)S(1)} all-gather(bf16[64,416]{1,0:T(8,128)(2,1)S(1)} %collective-permute-done), channel_id=1, replica_groups=mesh['xl'=2,'z3'=2,'z2'=2,'z1'=2,'z0'=2,'y1'=2,'y0'=2,'xh'=2,'c'=2] {'z3..., dimensions={0}, use_global_device_ids=true | all-gather | bytes 905216 | tf_op jit(solution)/shard_map/all_gather | solution.py:198
  66.3 0.0 collective-permute-done.2.their_weight_ref
  66.3 0.0 all-to-all-done
  66.3 3.4 %keep_part.1 = (f32[4,208,128]{2,1,0:T(8,128)S(1)}, f32[4,224,128]{2,1,0:T(8,128)S(1)}, f32[4,224,128]{2,1,0:T(8,128)S(1)}, f32[2,224,128]{2,1,0:T(8,128)S(1)}, f32[2,224,128]{2,1,0:T(8,128)S(1)}) custom-call(s32[3]{0:T(128)S(1)} %pad_add_fusion.place_ref, bf16[8,2,128,512]{3,2,1,0:T(8,128)(2,1)S(1)} %bitcast.5, bf16[416,512]{1,0:T(8,128)(2,1)} %own_weight_ref.1, ...), custom_call_target="tpu_custom_call" | custom-call | flops 1073741824 | bytes 4194304 | tf_op jit(solution)/shard_map/keep_part/pallas_call | solution.py:84
  69.8 1.9 %collective-permute-start.3 = (f16[4,224,128]{2,1,0:T(8,128)(2,1)S(1)}, f16[4,224,128]{2,1,0:T(8,128)(2,1)S(1)}, u32[]{:S(2)}, u32[]{:S(2)}) collective-permute-start(f16[4,224,128]{2,1,0:T(8,128)(2,1)S(1)} %convert_element_type.60), channel_id=1, source_target_pairs={{0,16},{16,32},{32,48},{48,64},{64,80},{80,96},{96,112},{112,128},... | collective-permute-start | bytes 688136 | tf_op jit(solution)/shard_map/ppermute | solution.py:177
  71.8 5.1 %collective-permute-start.4 = (f16[4,224,128]{2,1,0:T(8,128)(2,1)S(1)}, f16[4,224,128]{2,1,0:T(8,128)(2,1)S(1)}, u32[]{:S(2)}, u32[]{:S(2)}) collective-permute-start(f16[4,224,128]{2,1,0:T(8,128)(2,1)S(1)} %convert_element_type.61), channel_id=1, source_target_pairs={{0,240},{16,0},{32,16},{48,32},{64,48},{80,64},{96,80},{112,96},{1... | collective-permute-start | bytes 688136 | tf_op jit(solution)/shard_map/ppermute | solution.py:177
  76.9 1.9 %collective-permute-start.5 = (f16[2,224,128]{2,1,0:T(8,128)(2,1)S(1)}, f16[2,224,128]{2,1,0:T(8,128)(2,1)S(1)}, u32[]{:S(2)}, u32[]{:S(2)}) collective-permute-start(f16[2,224,128]{2,1,0:T(8,128)(2,1)S(1)} %convert_element_type.62), channel_id=1, source_target_pairs={{0,32},{16,48},{32,64},{48,80},{64,96},{80,112},{96,128},{112,144}... | collective-permute-start | bytes 344072 | tf_op jit(solution)/shard_map/ppermute | solution.py:177
  78.9 6.0 %collective-permute-start.6 = (f16[2,224,128]{2,1,0:T(8,128)(2,1)S(1)}, f16[2,224,128]{2,1,0:T(8,128)(2,1)S(1)}, u32[]{:S(2)}, u32[]{:S(2)}) collective-permute-start(f16[2,224,128]{2,1,0:T(8,128)(2,1)S(1)} %convert_element_type.63), channel_id=1, source_target_pairs={{0,224},{16,240},{32,0},{48,16},{64,32},{80,48},{96,64},{112,80},{... | collective-permute-start | bytes 344072 | tf_op jit(solution)/shard_map/ppermute | solution.py:177
  84.9 1.6 %weight_part.1 = (f32[416,512]{1,0:T(8,128)S(1)}, f32[416,512]{1,0:T(8,128)S(1)}) custom-call(s32[3]{0:T(128)S(1)} %pad_add_fusion.place_ref, bf16[4,2,128,416]{3,2,1,0:T(8,128)(2,1)S(1)} %bitcast.7, bf16[8,2,128,512]{3,2,1,0:T(8,128)(2,1)S(1)} %bitcast.6), custom_call_target="tpu_custom_call" | custom-call | flops 1073741824 | bytes 5242880 | tf_op jit(solution)/shard_map/weight_part/pallas_call | solution.py:164
  86.6 0.0 collective-permute-done.5
  86.6 1.4 %collective-permute-done.6 = f16[2,224,128]{2,1,0:T(8,128)(2,1)S(1)} collective-permute-done((f16[2,224,128]{2,1,0:T(8,128)(2,1)S(1)}, f16[2,224,128]{2,1,0:T(8,128)(2,1)S(1)}, u32[]{:S(2)}, u32[]{:S(2)}) %collective-permute-start.6) | collective-permute-done | bytes 114720 | tf_op jit(solution)/shard_map/ppermute | solution.py:177
  88.0 1.9 %collective-permute-start.11 = (f32[416,512]{1,0:T(8,128)S(1)}, f32[416,512]{1,0:T(8,128)S(1)}, u32[]{:S(2)}, u32[]{:S(2)}) collective-permute-start(f32[416,512]{1,0:T(8,128)S(1)} %get-tuple-element.48), channel_id=1, source_target_pairs={{0,256},{256,0},{1,257},{257,1},{2,258},{258,2},{3,259},{259,3},{4... | collective-permute-start | bytes 2555912 | tf_op jit(solution)/shard_map/ppermute | solution.py:208
  90.0 0.0 copy-start
  90.0 0.0 copy-start.1
  90.0 1.1 merge_parts.1
  91.2 4.9 %collective-permute-start.7 = (f16[224,128]{1,0:T(8,128)(2,1)S(1)}, f16[224,128]{1,0:T(8,128)(2,1)S(1)}, u32[]{:S(2)}, u32[]{:S(2)}) collective-permute-start(f16[224,128]{1,0:T(8,128)(2,1)S(1)} %convert_element_type.68), channel_id=1, source_target_pairs={{0,0},{32,256},{64,64},{96,320},{128,128},{160,384},{192,192},{224... | collective-permute-start | bytes 172040 | tf_op jit(solution)/shard_map/ppermute | solution.py:184
  96.1 5.8 %collective-permute-start.8 = (f16[224,128]{1,0:T(8,128)(2,1)S(1)}, f16[224,128]{1,0:T(8,128)(2,1)S(1)}, u32[]{:S(2)}, u32[]{:S(2)}) collective-permute-start(f16[224,128]{1,0:T(8,128)(2,1)S(1)} %convert_element_type.70), channel_id=1, source_target_pairs={{0,64},{32,320},{64,128},{96,384},{128,192},{160,448},{192,0},{224... | collective-permute-start | bytes 172040 | tf_op jit(solution)/shard_map/ppermute | solution.py:184
  101.9 7.9 %collective-permute-start.9 = (f16[224,128]{1,0:T(8,128)(2,1)S(1)}, f16[224,128]{1,0:T(8,128)(2,1)S(1)}, u32[]{:S(2)}, u32[]{:S(2)}) collective-permute-start(f16[224,128]{1,0:T(8,128)(2,1)S(1)} %convert_element_type.72), channel_id=1, source_target_pairs={{0,128},{32,384},{64,192},{96,448},{128,0},{160,256},{192,64},{224... | collective-permute-start | bytes 172040 | tf_op jit(solution)/shard_map/ppermute | solution.py:184
  109.8 4.2 %collective-permute-start.10 = (f16[224,128]{1,0:T(8,128)(2,1)S(1)}, f16[224,128]{1,0:T(8,128)(2,1)S(1)}, u32[]{:S(2)}, u32[]{:S(2)}) collective-permute-start(f16[224,128]{1,0:T(8,128)(2,1)S(1)} %convert_element_type.74), channel_id=1, source_target_pairs={{0,192},{32,448},{64,0},{96,256},{128,64},{160,320},{192,128},{224... | collective-permute-start | bytes 172040 | tf_op jit(solution)/shard_map/ppermute | solution.py:184
  114.1 1.7 %collective-permute-done.9 = f16[224,128]{1,0:T(8,128)(2,1)S(1)} collective-permute-done((f16[224,128]{1,0:T(8,128)(2,1)S(1)}, f16[224,128]{1,0:T(8,128)(2,1)S(1)}, u32[]{:S(2)}, u32[]{:S(2)}) %collective-permute-start.9) | collective-permute-done | bytes 57376 | tf_op jit(solution)/shard_map/ppermute | solution.py:184
  115.8 7.9 %collective-permute-done.10 = f16[224,128]{1,0:T(8,128)(2,1)S(1)} collective-permute-done((f16[224,128]{1,0:T(8,128)(2,1)S(1)}, f16[224,128]{1,0:T(8,128)(2,1)S(1)}, u32[]{:S(2)}, u32[]{:S(2)}) %collective-permute-start.10) | collective-permute-done | bytes 57376 | tf_op jit(solution)/shard_map/ppermute | solution.py:184
  123.7 0.7 finish_grads.1
  124.5 1.1 add_multiply_fusion
  (23 shorter events, 0.3 us)
Async XLA Ops:
  0.6 11.7 %collective-permute-start.1 = (bf16[128,512]{1,0:T(8,128)(2,1)}, bf16[128,512]{1,0:T(8,128)(2,1)S(1)}, u32[]{:S(2)}, u32[]{:S(2)}) collective-permute-start(bf16[128,512]{1,0:T(8,128)(2,1)} %param.6), channel_id=1, source_target_pairs={{0,0},{1,256},{256,1},{257,257},{2,2},{3,258},{258,3},{259,259},{4... | collective-permute-start | bytes 393224 | tf_op jit(solution)/shard_map/ppermute | solution.py:194
  3.7 8.6 %collective-permute-start = (bf16[64,416]{1,0:T(8,128)(2,1)S(1)}, bf16[64,416]{1,0:T(8,128)(2,1)S(1)}, u32[]{:S(2)}, u32[]{:S(2)}) collective-permute-start(bf16[64,416]{1,0:T(8,128)(2,1)S(1)} %fusion.4), channel_id=1, source_target_pairs={{0,0},{32,256},{256,32},{288,288},{1,1},{33,257},{257,33},{289,289... | collective-permute-start | bytes 159752 | tf_op jit(solution)/shard_map/ppermute | solution.py:193
  13.9 52.5 %all-to-all-start = ((bf16[16,128,512]{2,1,0:T(8,128)(2,1)}), bf16[16,128,512]{2,1,0:T(8,128)(2,1)S(1)}, u32[]{:S(2)}, u32[]{:S(2)}) async-start(bf16[16,128,512]{2,1,0:T(8,128)(2,1)} %broadcast_in_dim.2), calls=%async_computation | async-start | bytes 4194304 | tf_op jit(solution)/shard_map/all_to_all | solution.py:197
  21.3 45.0 %collective-permute-start.2 = (bf16[416,512]{1,0:T(8,128)(2,1)}, bf16[416,512]{1,0:T(8,128)(2,1)}, u32[]{:S(2)}, u32[]{:S(2)}) collective-permute-start(bf16[416,512]{1,0:T(8,128)(2,1)} %own_weight_ref.1), channel_id=1, source_target_pairs={{0,256},{256,0},{1,257},{257,1},{2,258},{258,2},{3,259},{259,3},{4... | collective-permute-start | bytes 1277960 | tf_op jit(solution)/shard_map/ppermute | solution.py:195
  69.8 18.2 %collective-permute-start.3 = (f16[4,224,128]{2,1,0:T(8,128)(2,1)S(1)}, f16[4,224,128]{2,1,0:T(8,128)(2,1)S(1)}, u32[]{:S(2)}, u32[]{:S(2)}) collective-permute-start(f16[4,224,128]{2,1,0:T(8,128)(2,1)S(1)} %convert_element_type.60), channel_id=1, source_target_pairs={{0,16},{16,32},{32,48},{48,64},{64,80},{80,96},{96,112},{112,128},... | collective-permute-start | bytes 688136 | tf_op jit(solution)/shard_map/ppermute | solution.py:177
  71.8 16.2 %collective-permute-start.4 = (f16[4,224,128]{2,1,0:T(8,128)(2,1)S(1)}, f16[4,224,128]{2,1,0:T(8,128)(2,1)S(1)}, u32[]{:S(2)}, u32[]{:S(2)}) collective-permute-start(f16[4,224,128]{2,1,0:T(8,128)(2,1)S(1)} %convert_element_type.61), channel_id=1, source_target_pairs={{0,240},{16,0},{32,16},{48,32},{64,48},{80,64},{96,80},{112,96},{1... | collective-permute-start | bytes 688136 | tf_op jit(solution)/shard_map/ppermute | solution.py:177
  76.9 9.6 %collective-permute-start.5 = (f16[2,224,128]{2,1,0:T(8,128)(2,1)S(1)}, f16[2,224,128]{2,1,0:T(8,128)(2,1)S(1)}, u32[]{:S(2)}, u32[]{:S(2)}) collective-permute-start(f16[2,224,128]{2,1,0:T(8,128)(2,1)S(1)} %convert_element_type.62), channel_id=1, source_target_pairs={{0,32},{16,48},{32,64},{48,80},{64,96},{80,112},{96,128},{112,144}... | collective-permute-start | bytes 344072 | tf_op jit(solution)/shard_map/ppermute | solution.py:177
  78.9 9.1 %collective-permute-start.6 = (f16[2,224,128]{2,1,0:T(8,128)(2,1)S(1)}, f16[2,224,128]{2,1,0:T(8,128)(2,1)S(1)}, u32[]{:S(2)}, u32[]{:S(2)}) collective-permute-start(f16[2,224,128]{2,1,0:T(8,128)(2,1)S(1)} %convert_element_type.63), channel_id=1, source_target_pairs={{0,224},{16,240},{32,0},{48,16},{64,32},{80,48},{96,64},{112,80},{... | collective-permute-start | bytes 344072 | tf_op jit(solution)/shard_map/ppermute | solution.py:177
  88.0 36.5 %collective-permute-start.11 = (f32[416,512]{1,0:T(8,128)S(1)}, f32[416,512]{1,0:T(8,128)S(1)}, u32[]{:S(2)}, u32[]{:S(2)}) collective-permute-start(f32[416,512]{1,0:T(8,128)S(1)} %get-tuple-element.48), channel_id=1, source_target_pairs={{0,256},{256,0},{1,257},{257,1},{2,258},{258,2},{3,259},{259,3},{4... | collective-permute-start | bytes 2555912 | tf_op jit(solution)/shard_map/ppermute | solution.py:208
  90.0 33.8 %copy-start = (bf16[64,416]{1,0:T(8,128)(2,1)S(1)}, bf16[64,416]{1,0:T(8,128)(2,1)}, u32[]{:S(2)}) copy-start(bf16[64,416]{1,0:T(8,128)(2,1)} %gate_ref.1) | copy-start | bytes 159748
  90.0 33.8 %copy-start.1 = (bf16[64,416]{1,0:T(8,128)(2,1)S(1)}, bf16[64,416]{1,0:T(8,128)(2,1)}, u32[]{:S(2)}) copy-start(bf16[64,416]{1,0:T(8,128)(2,1)} %up_ref.1) | copy-start | bytes 159748
  91.2 22.9 %collective-permute-start.7 = (f16[224,128]{1,0:T(8,128)(2,1)S(1)}, f16[224,128]{1,0:T(8,128)(2,1)S(1)}, u32[]{:S(2)}, u32[]{:S(2)}) collective-permute-start(f16[224,128]{1,0:T(8,128)(2,1)S(1)} %convert_element_type.68), channel_id=1, source_target_pairs={{0,0},{32,256},{64,64},{96,320},{128,128},{160,384},{192,192},{224... | collective-permute-start | bytes 172040 | tf_op jit(solution)/shard_map/ppermute | solution.py:184
  96.1 18.0 %collective-permute-start.8 = (f16[224,128]{1,0:T(8,128)(2,1)S(1)}, f16[224,128]{1,0:T(8,128)(2,1)S(1)}, u32[]{:S(2)}, u32[]{:S(2)}) collective-permute-start(f16[224,128]{1,0:T(8,128)(2,1)S(1)} %convert_element_type.70), channel_id=1, source_target_pairs={{0,64},{32,320},{64,128},{96,384},{128,192},{160,448},{192,0},{224... | collective-permute-start | bytes 172040 | tf_op jit(solution)/shard_map/ppermute | solution.py:184
  101.9 13.9 %collective-permute-start.9 = (f16[224,128]{1,0:T(8,128)(2,1)S(1)}, f16[224,128]{1,0:T(8,128)(2,1)S(1)}, u32[]{:S(2)}, u32[]{:S(2)}) collective-permute-start(f16[224,128]{1,0:T(8,128)(2,1)S(1)} %convert_element_type.72), channel_id=1, source_target_pairs={{0,128},{32,384},{64,192},{96,448},{128,0},{160,256},{192,64},{224... | collective-permute-start | bytes 172040 | tf_op jit(solution)/shard_map/ppermute | solution.py:184
  109.8 13.9 %collective-permute-start.10 = (f16[224,128]{1,0:T(8,128)(2,1)S(1)}, f16[224,128]{1,0:T(8,128)(2,1)S(1)}, u32[]{:S(2)}, u32[]{:S(2)}) collective-permute-start(f16[224,128]{1,0:T(8,128)(2,1)S(1)} %convert_element_type.74), channel_id=1, source_target_pairs={{0,192},{32,448},{64,0},{96,256},{128,64},{160,320},{192,128},{224... | collective-permute-start | bytes 172040 | tf_op jit(solution)/shard_map/ppermute | solution.py:184

commit v6 on v5

--- a/solution.py
+++ b/solution.py
@@ -46,16 +46,16 @@
 
 def keep_kernel(place_ref, grad_ref, own_weight_ref, their_weight_ref, *refs):
     own_ref, up1_ref, down1_ref, up2_ref, down2_ref, padded = refs
-    hid, feats = own_weight_ref.shape
+    hid = own_weight_ref.shape[0]
     xl, low = place_ref[0], place_ref[1]
     padded[:, hid:] = jnp.zeros_like(padded[:, hid:])
     padded[xl, :hid] = own_weight_ref[...]
     padded[1 - xl, :hid] = their_weight_ref[...]
     for y1 in range(2):
-        product = sum(times(grad_ref[y1 * 4 : y1 * 4 + 4, k].reshape(512, feats), padded[k]) for k in range(2))
-        for half in range(2):
-            ahead = lax.rem(y1 * 2 + half - low + 4, 4)
-            vals = [pack(product[far * 128 + half * 64 :][:64]) for far in range(4)]
+        product = sum(times(grad_ref[k, y1], padded[k]) for k in range(2))
+        for core in range(2):
+            ahead = lax.rem(core * 2 + y1 - low + 4, 4)
+            vals = [pack(product[far * 128 + core * 64 :][:64]) for far in range(4)]
 
             @pl.when(ahead == 0)
             def _(vals=vals):
@@ -146,13 +146,12 @@
 
 def weight_kernel(place_ref, hidden_ref, grad_ref, own_ref, their_ref):
     xl = place_ref[0]
-    feats = own_ref.shape[1]
     tokens = [hidden_ref[:, y1].reshape(512, hidden_ref.shape[3]) for y1 in range(2)]
     for out_ref, k in ((their_ref, 1 - xl), (own_ref, xl)):
         out_ref[...] = sum(
             lax.dot_general(
                 tokens[y1],
-                grad_ref[y1 * 4 : y1 * 4 + 4, k].reshape(512, feats),
+                grad_ref[k, y1],
                 (((0,), (0,)), ((), ())),
                 preferred_element_type=jnp.float32,
             )
@@ -181,7 +180,7 @@
     pairs = [
         (a * 8 + far * 2 + b, b * 8 + (far + step) % 4 * 2 + a) for a in range(2) for far in range(4) for b in range(2)
     ]
-    return lax.ppermute(array, ("xl",) + FAR + ("z1",), pairs)
+    return lax.ppermute(array, ("xl",) + FAR + ("z0",), pairs)
 
 
 def shards(gate_pre, up_pre, out_grad, down_weight):
@@ -190,25 +189,25 @@
     gate_vals = gate_pre.astype(jnp.float32)
     hidden = (gate_vals * jax.nn.sigmoid(gate_vals) * up_pre.astype(jnp.float32)).astype(jnp.bfloat16)
 
-    hidden = lax.ppermute(hidden, ("xl", "z1"), TURN)
-    turned = lax.ppermute(out_grad, ("xl", "c"), TURN)
+    hidden = lax.ppermute(hidden, ("xl", "z0"), TURN)
     their_weight = lax.ppermute(down_weight, "xl", SWAP)
-    hidden, turned = lax.optimization_barrier((hidden, turned))
-    grad = lax.all_to_all(jnp.broadcast_to(turned[None], (16,) + turned.shape), TENSOR, 0, 0)
+    copies = jnp.broadcast_to(out_grad.reshape(2, 1, 64, feats), (2, 16, 64, feats)).reshape(32, 64, feats)
+    grad = lax.all_to_all(copies, ("xl",) + TENSOR, 0, 0)
     tokens = lax.all_gather(hidden, Z, axis=0, tiled=True)
     grad, tokens, their_weight = lax.optimization_barrier((grad, tokens, their_weight))
-    grad = grad.reshape(8, 2, 128, feats)
+    grad = grad.reshape(2, 2, 512, feats)
 
     kept = keep_part(place, grad, down_weight, their_weight)
     halves = [k.astype(jnp.float16) for k in kept[1:]]
     near = [shift(h, Z, step) for h, step in zip(halves, (1, -1, 2, -2), strict=True)]
-    own, theirs = weight_part(place, tokens.reshape(4, 2, 128, hid), grad)
+    own, theirs = weight_part(place, tokens.reshape(8, 2, 64, hid), grad)
     near, theirs = lax.optimization_barrier((near, theirs))
     merged = merge(place, [kept[0]] + [n.astype(jnp.float32) for n in near])
     got = lax.ppermute(theirs, "xl", SWAP)
-    far = [to_owner(m.astype(jnp.float16), k).astype(jnp.float32) for k, m in enumerate(merged)]
-    gate_grad, up_grad = final(far, gate_pre, up_pre)
+    far = [to_owner(m.astype(jnp.float16), k) for k, m in enumerate(merged)]
     weight_grad = (own + got) * 2048 ** (-0.5)
+    far, weight_grad = lax.optimization_barrier((far, weight_grad))
+    gate_grad, up_grad = final([f.astype(jnp.float32) for f in far], gate_pre, up_pre)
     return (gate_grad, up_grad, weight_grad)
 
 

time: 126 us -> 114 us (0.905)
  waiting for transfers between devices: 14.7 us -> 8.31 us
  blocking collectives: 43 us -> 38.8 us
  starting transfers between devices: 56.1 us -> 54.2 us
    ppermute x6 -> x5, waiting for transfers between devices: 13.3 us -> 6.61 us  [the longest x4 3.62 us: to_owner(): return lax.ppermute(array, ('xl',) + FAR + ('z0',), pairs)]
    ppermute x6 -> x5, starting transfers between devices: 29.8 us -> 24.1 us  [the longest x4 22 us: to_owner(): return lax.ppermute(array, ('xl',) + FAR + ('z0',), pairs)]
    all_gather x1, blocking collectives: 43 us -> 38.8 us  [shards(): tokens = lax.all_gather(hidden, Z, axis=0, tiled=True)]
    all_to_all x1, starting transfers between devices: 7.45 us -> 9.76 us  [shards(): grad = lax.all_to_all(copies, ('xl',) + TENSOR, 0, 0)]
    ppermute x1, starting transfers between devices: 1.91 us -> 3.41 us  [shards(): got = lax.ppermute(theirs, 'xl', SWAP)]
  transfers between devices with their start and end apart: 13 -> 12, of which waited for: 4 -> 4; matrix products, arithmetic and copies ran while one was open for 1% -> 1% of each run, Pallas kernels for 3% -> 2%
where the time goes in v6:
time: 114 us; the launch traced here: 113 us
  starting transfers between devices  54.2 us (48%)
  blocking collectives  38.8 us (34%)
  waiting for transfers between devices  8.31 us (7%)
  Pallas kernels  6.9 us (6%)
  local copies, waits for them, and re-layouts  2.49 us (2%)
  other arithmetic  1.5 us (1%)
    all_gather x1, blocking collectives, shards(): tokens = lax.all_gather(hidden, Z, axis=0, tiled=True)  38.8 us
    ppermute x4, starting transfers between devices, to_owner(): return lax.ppermute(array, ('xl',) + FAR + ('z0',), pairs)  22 us
    ppermute x4, starting transfers between devices, shift(): lax.ppermute(array, axes, [(i, (i + step) % size) for i in range(size)])  15 us
    all_to_all x1, starting transfers between devices, shards(): grad = lax.all_to_all(copies, ('xl',) + TENSOR, 0, 0)  9.76 us
    ppermute x4, waiting for transfers between devices, to_owner(): return lax.ppermute(array, ('xl',) + FAR + ('z0',), pairs)  3.62 us
    pallas_call x1, Pallas kernels, keep_part(): pl.pallas_call(keep_kernel, out_shape=tuple((jax.ShapeDtypeStruct(s, jnp....  3.42 us
    ppermute x1, starting transfers between devices, shards(): got = lax.ppermute(theirs, 'xl', SWAP)  3.41 us
    ppermute x1, waiting for transfers between devices, shards(): hidden = lax.ppermute(hidden, ('xl', 'z0'), TURN)  2.98 us
  transfers between devices with their start and end apart: 12, of which 4 were waited for; matrix products, arithmetic and copies ran while one was open for 1% of the time, Pallas kernels for 2%

profile of v6, /device:TPU:6, one launch (start us, length us, event | category | flops | bytes accessed | tf_op | source)
XLA Modules:
  0.0 113.1 jit_solution(8036977824050150205)
XLA Ops:
  0.6 2.5 %broadcast_in_dim.8 = bf16[2,16,64,512]{3,2,1,0:T(8,128)(2,1)} broadcast(bf16[2,64,512]{2,1,0:T(8,128)(2,1)} %bitcast.11), dimensions={0,2,3} | broadcast | bytes 2228224 | tf_op jit(solution)/shard_map/broadcast_in_dim | solution.py:194
  3.1 9.8 %all-to-all-start = ((bf16[32,64,512]{2,1,0:T(8,128)(2,1)}), bf16[32,64,512]{2,1,0:T(8,128)(2,1)S(1)}, u32[]{:S(2)}, u32[]{:S(2)}) async-start(bf16[32,64,512]{2,1,0:T(8,128)(2,1)} %bitcast.10), calls=%async_computation | async-start | bytes 4194304 | tf_op jit(solution)/shard_map/all_to_all | solution.py:195
  13.0 2.1 %collective-permute-start = (bf16[64,416]{1,0:T(8,128)(2,1)S(1)}, bf16[64,416]{1,0:T(8,128)(2,1)S(1)}, u32[]{:S(2)}, u32[]{:S(2)}) collective-permute-start(bf16[64,416]{1,0:T(8,128)(2,1)S(1)} %fusion.4), channel_id=1, source_target_pairs={{0,0},{16,256},{256,16},{272,272},{1,1},{17,257},{257,17},{273,273... | collective-permute-start | bytes 159752 | tf_op jit(solution)/shard_map/ppermute | solution.py:192
  15.0 1.9 %collective-permute-start.1 = (bf16[416,512]{1,0:T(8,128)(2,1)}, bf16[416,512]{1,0:T(8,128)(2,1)}, u32[]{:S(2)}, u32[]{:S(2)}) collective-permute-start(bf16[416,512]{1,0:T(8,128)(2,1)} %own_weight_ref.1), channel_id=1, source_target_pairs={{0,256},{256,0},{1,257},{257,1},{2,258},{258,2},{3,259},{259,3},{4... | collective-permute-start | bytes 1277960 | tf_op jit(solution)/shard_map/ppermute | solution.py:193
  17.0 0.1 pad_add_fusion.place_ref
  17.0 3.0 %collective-permute-done = bf16[64,416]{1,0:T(8,128)(2,1)S(1)} collective-permute-done((bf16[64,416]{1,0:T(8,128)(2,1)S(1)}, bf16[64,416]{1,0:T(8,128)(2,1)S(1)}, u32[]{:S(2)}, u32[]{:S(2)}) %collective-permute-start) | collective-permute-done | bytes 53280 | tf_op jit(solution)/shard_map/ppermute | solution.py:192
  20.0 38.8 %all_gather.3 = bf16[1024,416]{1,0:T(8,128)(2,1)S(1)} all-gather(bf16[64,416]{1,0:T(8,128)(2,1)S(1)} %collective-permute-done), channel_id=1, replica_groups=mesh['xl'=2,'z3'=2,'z2'=2,'z1'=2,'z0'=2,'y1'=2,'y0'=2,'xh'=2,'c'=2] {'z3..., dimensions={0}, use_global_device_ids=true | all-gather | bytes 905216 | tf_op jit(solution)/shard_map/all_gather | solution.py:196
  58.8 0.0 collective-permute-done.1.their_weight_ref
  58.8 0.0 all-to-all-done
  58.8 3.4 %keep_part.1 = (f32[4,208,128]{2,1,0:T(8,128)S(1)}, f32[4,224,128]{2,1,0:T(8,128)S(1)}, f32[4,224,128]{2,1,0:T(8,128)S(1)}, f32[2,224,128]{2,1,0:T(8,128)S(1)}, f32[2,224,128]{2,1,0:T(8,128)S(1)}) custom-call(s32[3]{0:T(128)S(1)} %pad_add_fusion.place_ref, bf16[2,2,512,512]{3,2,1,0:T(8,128)(2,1)S(1)} %bitcast.7, bf16[416,512]{1,0:T(8,128)(2,1)} %own_weight_ref.1, ...), custom_call_target="tpu_custom_call" | custom-call | flops 1073741824 | bytes 4194304 | tf_op jit(solution)/shard_map/keep_part/pallas_call | solution.py:84
  62.3 2.4 %collective-permute-start.2 = (f16[4,224,128]{2,1,0:T(8,128)(2,1)S(1)}, f16[4,224,128]{2,1,0:T(8,128)(2,1)S(1)}, u32[]{:S(2)}, u32[]{:S(2)}) collective-permute-start(f16[4,224,128]{2,1,0:T(8,128)(2,1)S(1)} %convert_element_type.60), channel_id=1, source_target_pairs={{0,16},{16,32},{32,48},{48,64},{64,80},{80,96},{96,112},{112,128},... | collective-permute-start | bytes 688136 | tf_op jit(solution)/shard_map/ppermute | solution.py:176
  64.7 4.7 %collective-permute-start.3 = (f16[4,224,128]{2,1,0:T(8,128)(2,1)S(1)}, f16[4,224,128]{2,1,0:T(8,128)(2,1)S(1)}, u32[]{:S(2)}, u32[]{:S(2)}) collective-permute-start(f16[4,224,128]{2,1,0:T(8,128)(2,1)S(1)} %convert_element_type.61), channel_id=1, source_target_pairs={{0,240},{16,0},{32,16},{48,32},{64,48},{80,64},{96,80},{112,96},{1... | collective-permute-start | bytes 688136 | tf_op jit(solution)/shard_map/ppermute | solution.py:176
  69.4 1.9 %collective-permute-start.4 = (f16[2,224,128]{2,1,0:T(8,128)(2,1)S(1)}, f16[2,224,128]{2,1,0:T(8,128)(2,1)S(1)}, u32[]{:S(2)}, u32[]{:S(2)}) collective-permute-start(f16[2,224,128]{2,1,0:T(8,128)(2,1)S(1)} %convert_element_type.62), channel_id=1, source_target_pairs={{0,32},{16,48},{32,64},{48,80},{64,96},{80,112},{96,128},{112,144}... | collective-permute-start | bytes 344072 | tf_op jit(solution)/shard_map/ppermute | solution.py:176
  71.4 6.0 %collective-permute-start.5 = (f16[2,224,128]{2,1,0:T(8,128)(2,1)S(1)}, f16[2,224,128]{2,1,0:T(8,128)(2,1)S(1)}, u32[]{:S(2)}, u32[]{:S(2)}) collective-permute-start(f16[2,224,128]{2,1,0:T(8,128)(2,1)S(1)} %convert_element_type.63), channel_id=1, source_target_pairs={{0,224},{16,240},{32,0},{48,16},{64,32},{80,48},{96,64},{112,80},{... | collective-permute-start | bytes 344072 | tf_op jit(solution)/shard_map/ppermute | solution.py:176
  77.4 1.6 %weight_part.1 = (f32[416,512]{1,0:T(8,128)S(1)}, f32[416,512]{1,0:T(8,128)S(1)}) custom-call(s32[3]{0:T(128)S(1)} %pad_add_fusion.place_ref, bf16[8,2,64,416]{3,2,1,0:T(8,128)(2,1)S(1)} %bitcast.9, bf16[2,2,512,512]{3,2,1,0:T(8,128)(2,1)S(1)} %bitcast.8), custom_call_target="tpu_custom_call" | custom-call | flops 1073741824 | bytes 5242880 | tf_op jit(solution)/shard_map/weight_part/pallas_call | solution.py:163
  79.1 0.0 collective-permute-done.4
  79.1 1.7 %collective-permute-done.5 = f16[2,224,128]{2,1,0:T(8,128)(2,1)S(1)} collective-permute-done((f16[2,224,128]{2,1,0:T(8,128)(2,1)S(1)}, f16[2,224,128]{2,1,0:T(8,128)(2,1)S(1)}, u32[]{:S(2)}, u32[]{:S(2)}) %collective-permute-start.5) | collective-permute-done | bytes 114720 | tf_op jit(solution)/shard_map/ppermute | solution.py:176
  80.8 0.0 collective-permute-done.2
  80.8 0.0 collective-permute-done.3
  80.8 3.4 %collective-permute-start.10 = (f32[416,512]{1,0:T(8,128)S(1)}, f32[416,512]{1,0:T(8,128)S(1)}, u32[]{:S(2)}, u32[]{:S(2)}) collective-permute-start(f32[416,512]{1,0:T(8,128)S(1)} %get-tuple-element.47), channel_id=1, source_target_pairs={{0,256},{256,0},{1,257},{257,1},{2,258},{258,2},{3,259},{259,3},{4... | collective-permute-start | bytes 2555912 | tf_op jit(solution)/shard_map/ppermute | solution.py:206
  84.3 1.1 merge_parts.1
  85.5 1.9 %collective-permute-start.6 = (f16[224,128]{1,0:T(8,128)(2,1)S(1)}, f16[224,128]{1,0:T(8,128)(2,1)S(1)}, u32[]{:S(2)}, u32[]{:S(2)}) collective-permute-start(f16[224,128]{1,0:T(8,128)(2,1)S(1)} %convert_element_type.68), channel_id=1, source_target_pairs={{0,0},{16,256},{64,64},{80,320},{128,128},{144,384},{192,192},{208... | collective-permute-start | bytes 172040 | tf_op jit(solution)/shard_map/ppermute | solution.py:183
  87.4 7.3 %collective-permute-start.7 = (f16[224,128]{1,0:T(8,128)(2,1)S(1)}, f16[224,128]{1,0:T(8,128)(2,1)S(1)}, u32[]{:S(2)}, u32[]{:S(2)}) collective-permute-start(f16[224,128]{1,0:T(8,128)(2,1)S(1)} %convert_element_type.69), channel_id=1, source_target_pairs={{0,64},{16,320},{64,128},{80,384},{128,192},{144,448},{192,0},{208... | collective-permute-start | bytes 172040 | tf_op jit(solution)/shard_map/ppermute | solution.py:183
  94.7 5.1 %collective-permute-start.8 = (f16[224,128]{1,0:T(8,128)(2,1)S(1)}, f16[224,128]{1,0:T(8,128)(2,1)S(1)}, u32[]{:S(2)}, u32[]{:S(2)}) collective-permute-start(f16[224,128]{1,0:T(8,128)(2,1)S(1)} %convert_element_type.70), channel_id=1, source_target_pairs={{0,128},{16,384},{64,192},{80,448},{128,0},{144,256},{192,64},{208... | collective-permute-start | bytes 172040 | tf_op jit(solution)/shard_map/ppermute | solution.py:183
  99.9 7.7 %collective-permute-start.9 = (f16[224,128]{1,0:T(8,128)(2,1)S(1)}, f16[224,128]{1,0:T(8,128)(2,1)S(1)}, u32[]{:S(2)}, u32[]{:S(2)}) collective-permute-start(f16[224,128]{1,0:T(8,128)(2,1)S(1)} %convert_element_type.71), channel_id=1, source_target_pairs={{0,192},{16,448},{64,0},{80,256},{128,64},{144,320},{192,128},{208... | collective-permute-start | bytes 172040 | tf_op jit(solution)/shard_map/ppermute | solution.py:183
  107.6 0.0 collective-permute-done.10
  107.6 1.1 add_multiply_fusion
  108.7 0.0 collective-permute-done.6
  108.7 0.0 collective-permute-done.7
  108.7 1.3 %collective-permute-done.8 = f16[224,128]{1,0:T(8,128)(2,1)S(1)} collective-permute-done((f16[224,128]{1,0:T(8,128)(2,1)S(1)}, f16[224,128]{1,0:T(8,128)(2,1)S(1)}, u32[]{:S(2)}, u32[]{:S(2)}) %collective-permute-start.8) | collective-permute-done | bytes 57376 | tf_op jit(solution)/shard_map/ppermute | solution.py:183
  110.0 2.3 %collective-permute-done.9 = f16[224,128]{1,0:T(8,128)(2,1)S(1)} collective-permute-done((f16[224,128]{1,0:T(8,128)(2,1)S(1)}, f16[224,128]{1,0:T(8,128)(2,1)S(1)}, u32[]{:S(2)}, u32[]{:S(2)}) %collective-permute-start.9) | collective-permute-done | bytes 57376 | tf_op jit(solution)/shard_map/ppermute | solution.py:183
  112.4 0.7 finish_grads.1
  (21 shorter events, 0.3 us)
Async XLA Ops:
  3.1 9.8 %copy-start = (bf16[64,416]{1,0:T(8,128)(2,1)S(1)}, bf16[64,416]{1,0:T(8,128)(2,1)}, u32[]{:S(2)}) copy-start(bf16[64,416]{1,0:T(8,128)(2,1)} %gate_ref.1) | copy-start | bytes 159748
  3.1 9.8 %copy-start.1 = (bf16[64,416]{1,0:T(8,128)(2,1)S(1)}, bf16[64,416]{1,0:T(8,128)(2,1)}, u32[]{:S(2)}) copy-start(bf16[64,416]{1,0:T(8,128)(2,1)} %up_ref.1) | copy-start | bytes 159748
  3.1 55.7 %all-to-all-start = ((bf16[32,64,512]{2,1,0:T(8,128)(2,1)}), bf16[32,64,512]{2,1,0:T(8,128)(2,1)S(1)}, u32[]{:S(2)}, u32[]{:S(2)}) async-start(bf16[32,64,512]{2,1,0:T(8,128)(2,1)} %bitcast.10), calls=%async_computation | async-start | bytes 4194304 | tf_op jit(solution)/shard_map/all_to_all | solution.py:195
  13.0 7.1 %collective-permute-start = (bf16[64,416]{1,0:T(8,128)(2,1)S(1)}, bf16[64,416]{1,0:T(8,128)(2,1)S(1)}, u32[]{:S(2)}, u32[]{:S(2)}) collective-permute-start(bf16[64,416]{1,0:T(8,128)(2,1)S(1)} %fusion.4), channel_id=1, source_target_pairs={{0,0},{16,256},{256,16},{272,272},{1,1},{17,257},{257,17},{273,273... | collective-permute-start | bytes 159752 | tf_op jit(solution)/shard_map/ppermute | solution.py:192
  15.0 43.8 %collective-permute-start.1 = (bf16[416,512]{1,0:T(8,128)(2,1)}, bf16[416,512]{1,0:T(8,128)(2,1)}, u32[]{:S(2)}, u32[]{:S(2)}) collective-permute-start(bf16[416,512]{1,0:T(8,128)(2,1)} %own_weight_ref.1), channel_id=1, source_target_pairs={{0,256},{256,0},{1,257},{257,1},{2,258},{258,2},{3,259},{259,3},{4... | collective-permute-start | bytes 1277960 | tf_op jit(solution)/shard_map/ppermute | solution.py:193
  62.3 18.5 %collective-permute-start.2 = (f16[4,224,128]{2,1,0:T(8,128)(2,1)S(1)}, f16[4,224,128]{2,1,0:T(8,128)(2,1)S(1)}, u32[]{:S(2)}, u32[]{:S(2)}) collective-permute-start(f16[4,224,128]{2,1,0:T(8,128)(2,1)S(1)} %convert_element_type.60), channel_id=1, source_target_pairs={{0,16},{16,32},{32,48},{48,64},{64,80},{80,96},{96,112},{112,128},... | collective-permute-start | bytes 688136 | tf_op jit(solution)/shard_map/ppermute | solution.py:176
  64.7 16.0 %collective-permute-start.3 = (f16[4,224,128]{2,1,0:T(8,128)(2,1)S(1)}, f16[4,224,128]{2,1,0:T(8,128)(2,1)S(1)}, u32[]{:S(2)}, u32[]{:S(2)}) collective-permute-start(f16[4,224,128]{2,1,0:T(8,128)(2,1)S(1)} %convert_element_type.61), channel_id=1, source_target_pairs={{0,240},{16,0},{32,16},{48,32},{64,48},{80,64},{96,80},{112,96},{1... | collective-permute-start | bytes 688136 | tf_op jit(solution)/shard_map/ppermute | solution.py:176
  69.4 9.6 %collective-permute-start.4 = (f16[2,224,128]{2,1,0:T(8,128)(2,1)S(1)}, f16[2,224,128]{2,1,0:T(8,128)(2,1)S(1)}, u32[]{:S(2)}, u32[]{:S(2)}) collective-permute-start(f16[2,224,128]{2,1,0:T(8,128)(2,1)S(1)} %convert_element_type.62), channel_id=1, source_target_pairs={{0,32},{16,48},{32,64},{48,80},{64,96},{80,112},{96,128},{112,144}... | collective-permute-start | bytes 344072 | tf_op jit(solution)/shard_map/ppermute | solution.py:176
  71.4 9.4 %collective-permute-start.5 = (f16[2,224,128]{2,1,0:T(8,128)(2,1)S(1)}, f16[2,224,128]{2,1,0:T(8,128)(2,1)S(1)}, u32[]{:S(2)}, u32[]{:S(2)}) collective-permute-start(f16[2,224,128]{2,1,0:T(8,128)(2,1)S(1)} %convert_element_type.63), channel_id=1, source_target_pairs={{0,224},{16,240},{32,0},{48,16},{64,32},{80,48},{96,64},{112,80},{... | collective-permute-start | bytes 344072 | tf_op jit(solution)/shard_map/ppermute | solution.py:176
  80.8 26.8 %collective-permute-start.10 = (f32[416,512]{1,0:T(8,128)S(1)}, f32[416,512]{1,0:T(8,128)S(1)}, u32[]{:S(2)}, u32[]{:S(2)}) collective-permute-start(f32[416,512]{1,0:T(8,128)S(1)} %get-tuple-element.47), channel_id=1, source_target_pairs={{0,256},{256,0},{1,257},{257,1},{2,258},{258,2},{3,259},{259,3},{4... | collective-permute-start | bytes 2555912 | tf_op jit(solution)/shard_map/ppermute | solution.py:206
  85.5 23.2 %collective-permute-start.6 = (f16[224,128]{1,0:T(8,128)(2,1)S(1)}, f16[224,128]{1,0:T(8,128)(2,1)S(1)}, u32[]{:S(2)}, u32[]{:S(2)}) collective-permute-start(f16[224,128]{1,0:T(8,128)(2,1)S(1)} %convert_element_type.68), channel_id=1, source_target_pairs={{0,0},{16,256},{64,64},{80,320},{128,128},{144,384},{192,192},{208... | collective-permute-start | bytes 172040 | tf_op jit(solution)/shard_map/ppermute | solution.py:183
  87.4 21.3 %collective-permute-start.7 = (f16[224,128]{1,0:T(8,128)(2,1)S(1)}, f16[224,128]{1,0:T(8,128)(2,1)S(1)}, u32[]{:S(2)}, u32[]{:S(2)}) collective-permute-start(f16[224,128]{1,0:T(8,128)(2,1)S(1)} %convert_element_type.69), channel_id=1, source_target_pairs={{0,64},{16,320},{64,128},{80,384},{128,192},{144,448},{192,0},{208... | collective-permute-start | bytes 172040 | tf_op jit(solution)/shard_map/ppermute | solution.py:183
  94.7 15.3 %collective-permute-start.8 = (f16[224,128]{1,0:T(8,128)(2,1)S(1)}, f16[224,128]{1,0:T(8,128)(2,1)S(1)}, u32[]{:S(2)}, u32[]{:S(2)}) collective-permute-start(f16[224,128]{1,0:T(8,128)(2,1)S(1)} %convert_element_type.70), channel_id=1, source_target_pairs={{0,128},{16,384},{64,192},{80,448},{128,0},{144,256},{192,64},{208... | collective-permute-start | bytes 172040 | tf_op jit(solution)/shard_map/ppermute | solution.py:183
  99.9 12.4 %collective-permute-start.9 = (f16[224,128]{1,0:T(8,128)(2,1)S(1)}, f16[224,128]{1,0:T(8,128)(2,1)S(1)}, u32[]{:S(2)}, u32[]{:S(2)}) collective-permute-start(f16[224,128]{1,0:T(8,128)(2,1)S(1)} %convert_element_type.71), channel_id=1, source_target_pairs={{0,192},{16,448},{64,0},{80,256},{128,64},{144,320},{192,128},{208... | collective-permute-start | bytes 172040 | tf_op jit(solution)/shard_map/ppermute | solution.py:183

commit v7 on v6

--- a/solution.py
+++ b/solution.py
@@ -16,7 +16,7 @@
 SWAP = [(0, 1), (1, 0)]
 TURN = [(0, 0), (1, 2), (2, 1), (3, 3)]
 LANES = 128
-VMEM_BYTES = 32 * 1024 * 1024
+VMEM_BYTES = 16 * 1024 * 1024
 whole = pl.BlockSpec(memory_space=pltpu.VMEM)
 scalars = pl.BlockSpec(memory_space=pltpu.SMEM)
 
@@ -44,53 +44,42 @@
     return lax.dot_general(rows, weight, (((1,), (1,)), ((), ())), preferred_element_type=jnp.float32)
 
 
-def keep_kernel(place_ref, grad_ref, own_weight_ref, their_weight_ref, *refs):
-    own_ref, up1_ref, down1_ref, up2_ref, down2_ref, padded = refs
-    hid = own_weight_ref.shape[0]
+def keep_kernel(for_others, place_ref, grad_ref, own_weight_ref, their_weight_ref, tokens_ref, *refs):
+    del tokens_ref
+    out_refs, padded = refs[:-1], refs[-1]
+    hid, feats = own_weight_ref.shape
     xl, low = place_ref[0], place_ref[1]
     padded[:, hid:] = jnp.zeros_like(padded[:, hid:])
     padded[xl, :hid] = own_weight_ref[...]
     padded[1 - xl, :hid] = their_weight_ref[...]
-    for y1 in range(2):
-        product = sum(times(grad_ref[k, y1], padded[k]) for k in range(2))
-        for core in range(2):
-            ahead = lax.rem(core * 2 + y1 - low + 4, 4)
-            vals = [pack(product[far * 128 + core * 64 :][:64]) for far in range(4)]
-
-            @pl.when(ahead == 0)
-            def _(vals=vals):
-                for far in range(4):
-                    own_ref[far] = vals[far]
-
-            @pl.when(ahead == 1)
-            def _(vals=vals):
-                for far in range(4):
-                    up1_ref[far] = encode(vals[far])
-
-            @pl.when(ahead == 2)
-            def _(vals=vals):
-                for far in range(4):
-                    out_ref = up2_ref if far < 2 else down2_ref
-                    out_ref[far % 2] = encode(vals[far])
-
-            @pl.when(ahead == 3)
-            def _(vals=vals):
-                for far in range(4):
-                    down1_ref[far] = encode(vals[far])
-
-
-def keep_part(place, grad, own_weight, their_weight):
-    shapes = [(4, 208, LANES), (4, 224, LANES), (4, 224, LANES), (2, 224, LANES), (2, 224, LANES)]
-    return pl.pallas_call(
-        keep_kernel,
+    for ahead in (1, 3, 2) if for_others else (0,):
+        place = lax.rem(low + ahead, 4)
+        y1, core = lax.rem(place, 2), place // 2
+        product = sum(times(grad_ref[k, y1, :, core].reshape(256, feats), padded[k]) for k in range(2))
+        for far in range(4):
+            vals = pack(product[64 * far : 64 * far + 64])
+            if ahead == 0:
+                out_refs[0][far] = vals
+            elif ahead == 1:
+                out_refs[0][far] = encode(vals)
+            elif ahead == 3:
+                out_refs[1][far] = encode(vals)
+            else:
+                out_refs[2 + far // 2][far % 2] = encode(vals)
+
+
+def keep_part(for_others, place, grad, own_weight, their_weight, tokens):
+    shapes = [(4, 224, LANES), (4, 224, LANES), (2, 224, LANES), (2, 224, LANES)] if for_others else [(4, 208, LANES)]
+    return pl.pallas_call(
+        functools.partial(keep_kernel, for_others),
         out_shape=tuple(jax.ShapeDtypeStruct(s, jnp.float32) for s in shapes),
-        in_specs=[scalars] + [whole] * 3,
-        out_specs=(whole,) * 5,
+        in_specs=[scalars] + [whole] * 4,
+        out_specs=(whole,) * len(shapes),
         scratch_shapes=[pltpu.VMEM((2, 512, own_weight.shape[1]), own_weight.dtype)],
         compiler_params=pltpu.CompilerParams(vmem_limit_bytes=VMEM_BYTES),
-        cost_estimate=pl.CostEstimate(flops=2 * 1024 * 1024 * 512, bytes_accessed=4 << 20, transcendentals=0),
-        name="keep_part",
-    )(place, grad, own_weight, their_weight)
+        cost_estimate=pl.CostEstimate(flops=2 * 256 * 1024 * 512, bytes_accessed=3 << 20, transcendentals=0),
+        name="keep_others" if for_others else "keep_own",
+    )(place, grad, own_weight, their_weight, tokens)
 
 
 def merge_kernel(place_ref, own_ref, up1_ref, down1_ref, up2_ref, down2_ref, *out_refs):
@@ -195,16 +184,16 @@
     grad = lax.all_to_all(copies, ("xl",) + TENSOR, 0, 0)
     tokens = lax.all_gather(hidden, Z, axis=0, tiled=True)
     grad, tokens, their_weight = lax.optimization_barrier((grad, tokens, their_weight))
-    grad = grad.reshape(2, 2, 512, feats)
-
-    kept = keep_part(place, grad, down_weight, their_weight)
-    halves = [k.astype(jnp.float16) for k in kept[1:]]
+    blocks = grad.reshape(2, 2, 4, 2, 64, feats)
+
+    halves = [k.astype(jnp.float16) for k in keep_part(True, place, blocks, down_weight, their_weight, tokens)]
     near = [shift(h, Z, step) for h, step in zip(halves, (1, -1, 2, -2), strict=True)]
-    own, theirs = weight_part(place, tokens.reshape(8, 2, 64, hid), grad)
-    near, theirs = lax.optimization_barrier((near, theirs))
-    merged = merge(place, [kept[0]] + [n.astype(jnp.float32) for n in near])
+    (kept,) = keep_part(False, place, blocks, down_weight, their_weight, tokens)
+    own, theirs = weight_part(place, tokens.reshape(8, 2, 64, hid), grad.reshape(2, 2, 512, feats))
+    near, kept, theirs = lax.optimization_barrier((near, kept, theirs))
+    merged = merge(place, [kept] + [n.astype(jnp.float32) for n in near])
     got = lax.ppermute(theirs, "xl", SWAP)
-    far = [to_owner(m.astype(jnp.float16), k) for k, m in enumerate(merged)]
+    far = [to_owner(merged[k].astype(jnp.float16), k) for k in (2, 1, 3, 0)]
     weight_grad = (own + got) * 2048 ** (-0.5)
     far, weight_grad = lax.optimization_barrier((far, weight_grad))
     gate_grad, up_grad = final([f.astype(jnp.float32) for f in far], gate_pre, up_pre)

time: 114 us -> 112 us (0.982)
  waiting for transfers between devices: 8.31 us -> 5.12 us
    ppermute x4, waiting for transfers between devices: 1.69 us -> 0.01 us  [shift(): lax.ppermute(array, axes, [(i, (i + step) % size) for i in range(size)])]
    ppermute x4, waiting for transfers between devices: 3.62 us -> 2.11 us  [to_owner(): return lax.ppermute(array, ('xl',) + FAR + ('z0',), pairs)]
    pallas_call x1 -> x2, Pallas kernels: 3.42 us -> 4.14 us  [keep_part(): pl.pallas_call(functools.partial(keep_kernel, for_others), out_shape=tupl...]
  transfers between devices with their start and end apart: 12 -> 12, of which waited for: 4 -> 2; matrix products, arithmetic and copies ran while one was open for 1% -> 1% of each run, Pallas kernels for 2% -> 4%
where the time goes in v7:
time: 112 us; the launch traced here: 111 us
  starting transfers between devices  55 us (49%)
  blocking collectives  38.8 us (35%)
  Pallas kernels  7.64 us (7%)
  waiting for transfers between devices  5.12 us (5%)
  local copies, waits for them, and re-layouts  2.49 us (2%)
  other arithmetic  1.49 us (1%)
    all_gather x1, blocking collectives, shards(): tokens = lax.all_gather(hidden, Z, axis=0, tiled=True)  38.8 us
    ppermute x4, starting transfers between devices, to_owner(): return lax.ppermute(array, ('xl',) + FAR + ('z0',), pairs)  22.5 us
    ppermute x4, starting transfers between devices, shift(): lax.ppermute(array, axes, [(i, (i + step) % size) for i in range(size)])  15 us
    all_to_all x1, starting transfers between devices, shards(): grad = lax.all_to_all(copies, ('xl',) + TENSOR, 0, 0)  9.76 us
    pallas_call x2, Pallas kernels, keep_part(): pl.pallas_call(functools.partial(keep_kernel, for_others), out_shape=tupl...  4.14 us
    ppermute x1, starting transfers between devices, shards(): got = lax.ppermute(theirs, 'xl', SWAP)  3.71 us
    ppermute x1, waiting for transfers between devices, shards(): hidden = lax.ppermute(hidden, ('xl', 'z0'), TURN)  2.99 us
    broadcast_in_dim x1, local copies, waits for them, and re-layouts, shards(): jnp.broadcast_to(out_grad.reshape(2, 1, 64, feats), (2, 16, 64, feats))  2.48 us
  transfers between devices with their start and end apart: 12, of which 2 were waited for; matrix products, arithmetic and copies ran while one was open for 1% of the time, Pallas kernels for 4%

profile of v7, /device:TPU:6, one launch (start us, length us, event | category | flops | bytes accessed | tf_op | source)
XLA Modules:
  0.0 111.5 jit_solution(77437989845515121)
XLA Ops:
  0.6 2.5 %broadcast_in_dim.8 = bf16[2,16,64,512]{3,2,1,0:T(8,128)(2,1)} broadcast(bf16[2,64,512]{2,1,0:T(8,128)(2,1)} %bitcast.13), dimensions={0,2,3} | broadcast | bytes 2228224 | tf_op jit(solution)/shard_map/broadcast_in_dim | solution.py:183
  3.1 9.8 %all-to-all-start = ((bf16[32,64,512]{2,1,0:T(8,128)(2,1)}), bf16[32,64,512]{2,1,0:T(8,128)(2,1)S(1)}, u32[]{:S(2)}, u32[]{:S(2)}) async-start(bf16[32,64,512]{2,1,0:T(8,128)(2,1)} %bitcast.12), calls=%async_computation | async-start | bytes 4194304 | tf_op jit(solution)/shard_map/all_to_all | solution.py:184
  13.0 2.1 %collective-permute-start = (bf16[64,416]{1,0:T(8,128)(2,1)S(1)}, bf16[64,416]{1,0:T(8,128)(2,1)S(1)}, u32[]{:S(2)}, u32[]{:S(2)}) collective-permute-start(bf16[64,416]{1,0:T(8,128)(2,1)S(1)} %fusion.4), channel_id=1, source_target_pairs={{0,0},{16,256},{256,16},{272,272},{1,1},{17,257},{257,17},{273,273... | collective-permute-start | bytes 159752 | tf_op jit(solution)/shard_map/ppermute | solution.py:181
  15.0 1.9 %collective-permute-start.1 = (bf16[416,512]{1,0:T(8,128)(2,1)}, bf16[416,512]{1,0:T(8,128)(2,1)}, u32[]{:S(2)}, u32[]{:S(2)}) collective-permute-start(bf16[416,512]{1,0:T(8,128)(2,1)} %own_weight_ref.3), channel_id=1, source_target_pairs={{0,256},{256,0},{1,257},{257,1},{2,258},{258,2},{3,259},{259,3},{4... | collective-permute-start | bytes 1277960 | tf_op jit(solution)/shard_map/ppermute | solution.py:182
  17.0 0.1 pad_add_fusion.place_ref
  17.0 3.0 %collective-permute-done = bf16[64,416]{1,0:T(8,128)(2,1)S(1)} collective-permute-done((bf16[64,416]{1,0:T(8,128)(2,1)S(1)}, bf16[64,416]{1,0:T(8,128)(2,1)S(1)}, u32[]{:S(2)}, u32[]{:S(2)}) %collective-permute-start) | collective-permute-done | bytes 53280 | tf_op jit(solution)/shard_map/ppermute | solution.py:181
  20.0 38.8 %all_gather.3.tokens_ref = bf16[1024,416]{1,0:T(8,128)(2,1)S(1)} all-gather(bf16[64,416]{1,0:T(8,128)(2,1)S(1)} %collective-permute-done), channel_id=1, replica_groups=mesh['xl'=2,'z3'=2,'z2'=2,'z1'=2,'z0'=2,'y1'=2,'y0'=2,'xh'=2,'c'=2] {'z3..., dimensions={0}, use_global_device_ids=true | all-gather | bytes 905216 | tf_op jit(solution)/shard_map/all_gather | solution.py:185
  58.8 0.0 collective-permute-done.1.their_weight_ref
  58.8 0.0 all-to-all-done
  58.8 2.4 %keep_others.1 = (f32[4,224,128]{2,1,0:T(8,128)S(1)}, f32[4,224,128]{2,1,0:T(8,128)S(1)}, f32[2,224,128]{2,1,0:T(8,128)S(1)}, f32[2,224,128]{2,1,0:T(8,128)S(1)}) custom-call(s32[3]{0:T(128)S(1)} %pad_add_fusion.place_ref, bf16[2,2,4,2,64,512]{5,4,3,2,1,0:T(8,128)(2,1)S(1)} %bitcast.8, bf16[416,512]{1,0:T(8,128)(2,1)} %own_weight_ref.3, ...), custom_call_target="tpu_custom_call" | custom-call | flops 268435456 | bytes 3145728 | tf_op jit(solution)/shard_map/keep_others/pallas_call | solution.py:73
  61.3 2.4 %collective-permute-start.2 = (f16[4,224,128]{2,1,0:T(8,128)(2,1)S(1)}, f16[4,224,128]{2,1,0:T(8,128)(2,1)S(1)}, u32[]{:S(2)}, u32[]{:S(2)}) collective-permute-start(f16[4,224,128]{2,1,0:T(8,128)(2,1)S(1)} %convert_element_type.60), channel_id=1, source_target_pairs={{0,16},{16,32},{32,48},{48,64},{64,80},{80,96},{96,112},{112,128},... | collective-permute-start | bytes 688136 | tf_op jit(solution)/shard_map/ppermute | solution.py:165
  63.7 4.7 %collective-permute-start.3 = (f16[4,224,128]{2,1,0:T(8,128)(2,1)S(1)}, f16[4,224,128]{2,1,0:T(8,128)(2,1)S(1)}, u32[]{:S(2)}, u32[]{:S(2)}) collective-permute-start(f16[4,224,128]{2,1,0:T(8,128)(2,1)S(1)} %convert_element_type.61), channel_id=1, source_target_pairs={{0,240},{16,0},{32,16},{48,32},{64,48},{80,64},{96,80},{112,96},{1... | collective-permute-start | bytes 688136 | tf_op jit(solution)/shard_map/ppermute | solution.py:165
  68.4 1.9 %collective-permute-start.4 = (f16[2,224,128]{2,1,0:T(8,128)(2,1)S(1)}, f16[2,224,128]{2,1,0:T(8,128)(2,1)S(1)}, u32[]{:S(2)}, u32[]{:S(2)}) collective-permute-start(f16[2,224,128]{2,1,0:T(8,128)(2,1)S(1)} %convert_element_type.62), channel_id=1, source_target_pairs={{0,32},{16,48},{32,64},{48,80},{64,96},{80,112},{96,128},{112,144}... | collective-permute-start | bytes 344072 | tf_op jit(solution)/shard_map/ppermute | solution.py:165
  70.4 6.0 %collective-permute-start.5 = (f16[2,224,128]{2,1,0:T(8,128)(2,1)S(1)}, f16[2,224,128]{2,1,0:T(8,128)(2,1)S(1)}, u32[]{:S(2)}, u32[]{:S(2)}) collective-permute-start(f16[2,224,128]{2,1,0:T(8,128)(2,1)S(1)} %convert_element_type.63), channel_id=1, source_target_pairs={{0,224},{16,240},{32,0},{48,16},{64,32},{80,48},{96,64},{112,80},{... | collective-permute-start | bytes 344072 | tf_op jit(solution)/shard_map/ppermute | solution.py:165
  76.4 1.7 %keep_own.1.own_ref = f32[4,208,128]{2,1,0:T(8,128)S(1)} custom-call(s32[3]{0:T(128)S(1)} %pad_add_fusion.place_ref, bf16[2,2,4,2,64,512]{5,4,3,2,1,0:T(8,128)(2,1)S(1)} %bitcast.9, bf16[416,512]{1,0:T(8,128)(2,1)} %own_weight_ref.3, bf16[416,512]{1,0:T(8,128)(2,1)} %collective-permute-done.1.their_weight_ref, bf16[1024,416]{1,0:T(8,128)(2,1)S(1)} %all_gather.3.tokens_ref), custom_call_target="tpu_custom_call" | custom-call | flops 268435456 | bytes 3145728 | tf_op jit(solution)/shard_map/keep_own/pallas_call | solution.py:73
  78.2 1.6 %weight_part.1 = (f32[416,512]{1,0:T(8,128)S(1)}, f32[416,512]{1,0:T(8,128)S(1)}) custom-call(s32[3]{0:T(128)S(1)} %pad_add_fusion.place_ref, bf16[8,2,64,416]{3,2,1,0:T(8,128)(2,1)S(1)} %bitcast.11, bf16[2,2,512,512]{3,2,1,0:T(8,128)(2,1)S(1)} %bitcast.10), custom_call_target="tpu_custom_call" | custom-call | flops 1073741824 | bytes 5242880 | tf_op jit(solution)/shard_map/weight_part/pallas_call | solution.py:152
  79.8 0.0 collective-permute-done.4
  79.8 0.0 collective-permute-done.5
  79.8 0.0 collective-permute-done.2
  79.8 0.0 collective-permute-done.3
  79.8 3.7 %collective-permute-start.10 = (f32[416,512]{1,0:T(8,128)S(1)}, f32[416,512]{1,0:T(8,128)S(1)}, u32[]{:S(2)}, u32[]{:S(2)}) collective-permute-start(f32[416,512]{1,0:T(8,128)S(1)} %get-tuple-element.47), channel_id=1, source_target_pairs={{0,256},{256,0},{1,257},{257,1},{2,258},{258,2},{3,259},{259,3},{4... | collective-permute-start | bytes 2555912 | tf_op jit(solution)/shard_map/ppermute | solution.py:195
  83.7 1.1 %merge_parts.1 = (f32[224,128]{1,0:T(8,128)S(1)}, f32[224,128]{1,0:T(8,128)S(1)}, f32[224,128]{1,0:T(8,128)S(1)}, f32[224,128]{1,0:T(8,128)S(1)}) custom-call(s32[3]{0:T(128)S(1)} %pad_add_fusion.place_ref, f32[4,208,128]{2,1,0:T(8,128)S(1)} %keep_own.1.own_ref, f32[4,224,128]{2,1,0:T(8,128)S(1)} %convert_element_type.64.up1_ref, ...), custom_call_target="tpu_custom_call" | custom-call | flops 1048576 | bytes 1048576 | tf_op jit(solution)/shard_map/merge_parts/pallas_call | solution.py:98
  84.8 6.3 %collective-permute-start.6 = (f16[224,128]{1,0:T(8,128)(2,1)S(1)}, f16[224,128]{1,0:T(8,128)(2,1)S(1)}, u32[]{:S(2)}, u32[]{:S(2)}) collective-permute-start(f16[224,128]{1,0:T(8,128)(2,1)S(1)} %convert_element_type.68), channel_id=1, source_target_pairs={{0,128},{16,384},{64,192},{80,448},{128,0},{144,256},{192,64},{208... | collective-permute-start | bytes 172040 | tf_op jit(solution)/shard_map/ppermute | solution.py:172
  91.2 7.4 %collective-permute-start.7 = (f16[224,128]{1,0:T(8,128)(2,1)S(1)}, f16[224,128]{1,0:T(8,128)(2,1)S(1)}, u32[]{:S(2)}, u32[]{:S(2)}) collective-permute-start(f16[224,128]{1,0:T(8,128)(2,1)S(1)} %convert_element_type.69), channel_id=1, source_target_pairs={{0,64},{16,320},{64,128},{80,384},{128,192},{144,448},{192,0},{208... | collective-permute-start | bytes 172040 | tf_op jit(solution)/shard_map/ppermute | solution.py:172
  98.6 2.3 %collective-permute-start.8 = (f16[224,128]{1,0:T(8,128)(2,1)S(1)}, f16[224,128]{1,0:T(8,128)(2,1)S(1)}, u32[]{:S(2)}, u32[]{:S(2)}) collective-permute-start(f16[224,128]{1,0:T(8,128)(2,1)S(1)} %convert_element_type.70), channel_id=1, source_target_pairs={{0,192},{16,448},{64,0},{80,256},{128,64},{144,320},{192,128},{208... | collective-permute-start | bytes 172040 | tf_op jit(solution)/shard_map/ppermute | solution.py:172
  101.0 6.4 %collective-permute-start.9 = (f16[224,128]{1,0:T(8,128)(2,1)S(1)}, f16[224,128]{1,0:T(8,128)(2,1)S(1)}, u32[]{:S(2)}, u32[]{:S(2)}) collective-permute-start(f16[224,128]{1,0:T(8,128)(2,1)S(1)} %convert_element_type.71), channel_id=1, source_target_pairs={{0,0},{16,256},{64,64},{80,320},{128,128},{144,384},{192,192},{208... | collective-permute-start | bytes 172040 | tf_op jit(solution)/shard_map/ppermute | solution.py:172
  107.5 1.1 add_multiply_fusion
  108.5 0.0 collective-permute-done.6
  108.5 0.0 collective-permute-done.7
  108.6 2.1 %collective-permute-done.8 = f16[224,128]{1,0:T(8,128)(2,1)S(1)} collective-permute-done((f16[224,128]{1,0:T(8,128)(2,1)S(1)}, f16[224,128]{1,0:T(8,128)(2,1)S(1)}, u32[]{:S(2)}, u32[]{:S(2)}) %collective-permute-start.8) | collective-permute-done | bytes 57376 | tf_op jit(solution)/shard_map/ppermute | solution.py:172
  110.7 0.0 collective-permute-done.9
  110.7 0.7 finish_grads.1
  (22 shorter events, 0.4 us)
Async XLA Ops:
  3.1 9.8 %copy-start = (bf16[64,416]{1,0:T(8,128)(2,1)S(1)}, bf16[64,416]{1,0:T(8,128)(2,1)}, u32[]{:S(2)}) copy-start(bf16[64,416]{1,0:T(8,128)(2,1)} %up_ref.1) | copy-start | bytes 159748
  3.1 9.8 %copy-start.1 = (bf16[64,416]{1,0:T(8,128)(2,1)S(1)}, bf16[64,416]{1,0:T(8,128)(2,1)}, u32[]{:S(2)}) copy-start(bf16[64,416]{1,0:T(8,128)(2,1)} %gate_ref.1) | copy-start | bytes 159748
  3.1 55.7 %all-to-all-start = ((bf16[32,64,512]{2,1,0:T(8,128)(2,1)}), bf16[32,64,512]{2,1,0:T(8,128)(2,1)S(1)}, u32[]{:S(2)}, u32[]{:S(2)}) async-start(bf16[32,64,512]{2,1,0:T(8,128)(2,1)} %bitcast.12), calls=%async_computation | async-start | bytes 4194304 | tf_op jit(solution)/shard_map/all_to_all | solution.py:184
  13.0 7.1 %collective-permute-start = (bf16[64,416]{1,0:T(8,128)(2,1)S(1)}, bf16[64,416]{1,0:T(8,128)(2,1)S(1)}, u32[]{:S(2)}, u32[]{:S(2)}) collective-permute-start(bf16[64,416]{1,0:T(8,128)(2,1)S(1)} %fusion.4), channel_id=1, source_target_pairs={{0,0},{16,256},{256,16},{272,272},{1,1},{17,257},{257,17},{273,273... | collective-permute-start | bytes 159752 | tf_op jit(solution)/shard_map/ppermute | solution.py:181
  15.0 43.8 %collective-permute-start.1 = (bf16[416,512]{1,0:T(8,128)(2,1)}, bf16[416,512]{1,0:T(8,128)(2,1)}, u32[]{:S(2)}, u32[]{:S(2)}) collective-permute-start(bf16[416,512]{1,0:T(8,128)(2,1)} %own_weight_ref.3), channel_id=1, source_target_pairs={{0,256},{256,0},{1,257},{257,1},{2,258},{258,2},{3,259},{259,3},{4... | collective-permute-start | bytes 1277960 | tf_op jit(solution)/shard_map/ppermute | solution.py:182
  61.3 18.5 %collective-permute-start.2 = (f16[4,224,128]{2,1,0:T(8,128)(2,1)S(1)}, f16[4,224,128]{2,1,0:T(8,128)(2,1)S(1)}, u32[]{:S(2)}, u32[]{:S(2)}) collective-permute-start(f16[4,224,128]{2,1,0:T(8,128)(2,1)S(1)} %convert_element_type.60), channel_id=1, source_target_pairs={{0,16},{16,32},{32,48},{48,64},{64,80},{80,96},{96,112},{112,128},... | collective-permute-start | bytes 688136 | tf_op jit(solution)/shard_map/ppermute | solution.py:165
  63.7 16.1 %collective-permute-start.3 = (f16[4,224,128]{2,1,0:T(8,128)(2,1)S(1)}, f16[4,224,128]{2,1,0:T(8,128)(2,1)S(1)}, u32[]{:S(2)}, u32[]{:S(2)}) collective-permute-start(f16[4,224,128]{2,1,0:T(8,128)(2,1)S(1)} %convert_element_type.61), channel_id=1, source_target_pairs={{0,240},{16,0},{32,16},{48,32},{64,48},{80,64},{96,80},{112,96},{1... | collective-permute-start | bytes 688136 | tf_op jit(solution)/shard_map/ppermute | solution.py:165
  68.4 11.4 %collective-permute-start.4 = (f16[2,224,128]{2,1,0:T(8,128)(2,1)S(1)}, f16[2,224,128]{2,1,0:T(8,128)(2,1)S(1)}, u32[]{:S(2)}, u32[]{:S(2)}) collective-permute-start(f16[2,224,128]{2,1,0:T(8,128)(2,1)S(1)} %convert_element_type.62), channel_id=1, source_target_pairs={{0,32},{16,48},{32,64},{48,80},{64,96},{80,112},{96,128},{112,144}... | collective-permute-start | bytes 344072 | tf_op jit(solution)/shard_map/ppermute | solution.py:165
  70.4 9.4 %collective-permute-start.5 = (f16[2,224,128]{2,1,0:T(8,128)(2,1)S(1)}, f16[2,224,128]{2,1,0:T(8,128)(2,1)S(1)}, u32[]{:S(2)}, u32[]{:S(2)}) collective-permute-start(f16[2,224,128]{2,1,0:T(8,128)(2,1)S(1)} %convert_element_type.63), channel_id=1, source_target_pairs={{0,224},{16,240},{32,0},{48,16},{64,32},{80,48},{96,64},{112,80},{... | collective-permute-start | bytes 344072 | tf_op jit(solution)/shard_map/ppermute | solution.py:165
  79.8 27.6 %collective-permute-start.10 = (f32[416,512]{1,0:T(8,128)S(1)}, f32[416,512]{1,0:T(8,128)S(1)}, u32[]{:S(2)}, u32[]{:S(2)}) collective-permute-start(f32[416,512]{1,0:T(8,128)S(1)} %get-tuple-element.47), channel_id=1, source_target_pairs={{0,256},{256,0},{1,257},{257,1},{2,258},{258,2},{3,259},{259,3},{4... | collective-permute-start | bytes 2555912 | tf_op jit(solution)/shard_map/ppermute | solution.py:195
  84.8 23.7 %collective-permute-start.6 = (f16[224,128]{1,0:T(8,128)(2,1)S(1)}, f16[224,128]{1,0:T(8,128)(2,1)S(1)}, u32[]{:S(2)}, u32[]{:S(2)}) collective-permute-start(f16[224,128]{1,0:T(8,128)(2,1)S(1)} %convert_element_type.68), channel_id=1, source_target_pairs={{0,128},{16,384},{64,192},{80,448},{128,0},{144,256},{192,64},{208... | collective-permute-start | bytes 172040 | tf_op jit(solution)/shard_map/ppermute | solution.py:172
  91.2 17.4 %collective-permute-start.7 = (f16[224,128]{1,0:T(8,128)(2,1)S(1)}, f16[224,128]{1,0:T(8,128)(2,1)S(1)}, u32[]{:S(2)}, u32[]{:S(2)}) collective-permute-start(f16[224,128]{1,0:T(8,128)(2,1)S(1)} %convert_element_type.69), channel_id=1, source_target_pairs={{0,64},{16,320},{64,128},{80,384},{128,192},{144,448},{192,0},{208... | collective-permute-start | bytes 172040 | tf_op jit(solution)/shard_map/ppermute | solution.py:172
  98.6 12.0 %collective-permute-start.8 = (f16[224,128]{1,0:T(8,128)(2,1)S(1)}, f16[224,128]{1,0:T(8,128)(2,1)S(1)}, u32[]{:S(2)}, u32[]{:S(2)}) collective-permute-start(f16[224,128]{1,0:T(8,128)(2,1)S(1)} %convert_element_type.70), channel_id=1, source_target_pairs={{0,192},{16,448},{64,0},{80,256},{128,64},{144,320},{192,128},{208... | collective-permute-start | bytes 172040 | tf_op jit(solution)/shard_map/ppermute | solution.py:172
  101.0 9.7 %collective-permute-start.9 = (f16[224,128]{1,0:T(8,128)(2,1)S(1)}, f16[224,128]{1,0:T(8,128)(2,1)S(1)}, u32[]{:S(2)}, u32[]{:S(2)}) collective-permute-start(f16[224,128]{1,0:T(8,128)(2,1)S(1)} %convert_element_type.71), channel_id=1, source_target_pairs={{0,0},{16,256},{64,64},{80,320},{128,128},{144,384},{192,192},{208... | collective-permute-start | bytes 172040 | tf_op jit(solution)/shard_map/ppermute | solution.py:172

commit v8 on v7

--- a/solution.py
+++ b/solution.py
@@ -186,9 +186,9 @@
     grad, tokens, their_weight = lax.optimization_barrier((grad, tokens, their_weight))
     blocks = grad.reshape(2, 2, 4, 2, 64, feats)
 
-    halves = [k.astype(jnp.float16) for k in keep_part(True, place, blocks, down_weight, their_weight, tokens)]
+    halves = [k.astype(jnp.float16) for k in keep_part(True, place, blocks, down_weight, their_weight, tokens[:16])]
     near = [shift(h, Z, step) for h, step in zip(halves, (1, -1, 2, -2), strict=True)]
-    (kept,) = keep_part(False, place, blocks, down_weight, their_weight, tokens)
+    (kept,) = keep_part(False, place, blocks, down_weight, their_weight, tokens[:16])
     own, theirs = weight_part(place, tokens.reshape(8, 2, 64, hid), grad.reshape(2, 2, 512, feats))
     near, kept, theirs = lax.optimization_barrier((near, kept, theirs))
     merged = merge(place, [kept] + [n.astype(jnp.float32) for n in near])

time: 112 us -> 115 us (1.027)
  blocking collectives: 38.8 us -> 41.1 us
  Pallas kernels: 7.64 us -> 6.4 us
    all_gather x1, blocking collectives: 38.8 us -> 41.1 us  [shards(): tokens = lax.all_gather(hidden, Z, axis=0, tiled=True)]
    pallas_call x2, Pallas kernels: 4.14 us -> 2.93 us  [keep_part(): pl.pallas_call(functools.partial(keep_kernel, for_others), out_shape=tupl...]
  transfers between devices with their start and end apart: 12 -> 12, of which waited for: 2 -> 3; matrix products, arithmetic and copies ran while one was open for 1% -> 1% of each run, Pallas kernels for 4% -> 3%
where the time goes in v8:
time: 115 us; the launch traced here: 114 us
  starting transfers between devices  55 us (48%)
  blocking collectives  41.1 us (36%)
  Pallas kernels  6.4 us (6%)
  waiting for transfers between devices  5.49 us (5%)
  local copies, waits for them, and re-layouts  3.22 us (3%)
  other arithmetic  1.5 us (1%)
    all_gather x1, blocking collectives, shards(): tokens = lax.all_gather(hidden, Z, axis=0, tiled=True)  41.1 us
    ppermute x4, starting transfers between devices, to_owner(): return lax.ppermute(array, ('xl',) + FAR + ('z0',), pairs)  22.8 us
    ppermute x4, starting transfers between devices, shift(): lax.ppermute(array, axes, [(i, (i + step) % size) for i in range(size)])  15.1 us
    all_to_all x1, starting transfers between devices, shards(): grad = lax.all_to_all(copies, ('xl',) + TENSOR, 0, 0)  9.76 us
    ppermute x1, starting transfers between devices, shards(): got = lax.ppermute(theirs, 'xl', SWAP)  3.36 us
    ppermute x1, waiting for transfers between devices, shards(): hidden = lax.ppermute(hidden, ('xl', 'z0'), TURN)  2.98 us
    pallas_call x2, Pallas kernels, keep_part(): pl.pallas_call(functools.partial(keep_kernel, for_others), out_shape=tupl...  2.93 us
    broadcast_in_dim x1, local copies, waits for them, and re-layouts, shards(): jnp.broadcast_to(out_grad.reshape(2, 1, 64, feats), (2, 16, 64, feats))  2.48 us
  transfers between devices with their start and end apart: 12, of which 3 were waited for; matrix products, arithmetic and copies ran while one was open for 1% of the time, Pallas kernels for 3%

profile of v8, /device:TPU:6, one launch (start us, length us, event | category | flops | bytes accessed | tf_op | source)
XLA Modules:
  0.0 113.7 jit_solution(1927802725122319783)
XLA Ops:
  0.6 2.5 %broadcast_in_dim.8 = bf16[2,16,64,512]{3,2,1,0:T(8,128)(2,1)} broadcast(bf16[2,64,512]{2,1,0:T(8,128)(2,1)} %bitcast.13), dimensions={0,2,3} | broadcast | bytes 2228224 | tf_op jit(solution)/shard_map/broadcast_in_dim | solution.py:183
  3.1 9.8 %all-to-all-start = ((bf16[32,64,512]{2,1,0:T(8,128)(2,1)}), bf16[32,64,512]{2,1,0:T(8,128)(2,1)S(1)}, u32[]{:S(2)}, u32[]{:S(2)}) async-start(bf16[32,64,512]{2,1,0:T(8,128)(2,1)} %bitcast.12), calls=%async_computation | async-start | bytes 4194304 | tf_op jit(solution)/shard_map/all_to_all | solution.py:184
  13.0 2.1 %collective-permute-start = (bf16[64,416]{1,0:T(8,128)(2,1)S(1)}, bf16[64,416]{1,0:T(8,128)(2,1)S(1)}, u32[]{:S(2)}, u32[]{:S(2)}) collective-permute-start(bf16[64,416]{1,0:T(8,128)(2,1)S(1)} %fusion.4), channel_id=1, source_target_pairs={{0,0},{16,256},{256,16},{272,272},{1,1},{17,257},{257,17},{273,273... | collective-permute-start | bytes 159752 | tf_op jit(solution)/shard_map/ppermute | solution.py:181
  15.0 1.9 %collective-permute-start.1 = (bf16[416,512]{1,0:T(8,128)(2,1)S(1)}, bf16[416,512]{1,0:T(8,128)(2,1)S(1)}, u32[]{:S(2)}, u32[]{:S(2)}) collective-permute-start(bf16[416,512]{1,0:T(8,128)(2,1)S(1)} %copy-done), channel_id=1, source_target_pairs={{0,256},{256,0},{1,257},{257,1},{2,258},{258,2},{3,259},{259,3},{4... | collective-permute-start | bytes 1277960 | tf_op jit(solution)/shard_map/ppermute | solution.py:182
  17.0 0.1 pad_add_fusion.place_ref
  17.0 3.0 %collective-permute-done = bf16[64,416]{1,0:T(8,128)(2,1)S(1)} collective-permute-done((bf16[64,416]{1,0:T(8,128)(2,1)S(1)}, bf16[64,416]{1,0:T(8,128)(2,1)S(1)}, u32[]{:S(2)}, u32[]{:S(2)}) %collective-permute-start) | collective-permute-done | bytes 53280 | tf_op jit(solution)/shard_map/ppermute | solution.py:181
  20.0 41.1 %all_gather.3 = bf16[1024,416]{1,0:T(8,128)(2,1)} all-gather(bf16[64,416]{1,0:T(8,128)(2,1)S(1)} %collective-permute-done), channel_id=1, replica_groups=mesh['xl'=2,'z3'=2,'z2'=2,'z1'=2,'z0'=2,'y1'=2,'y0'=2,'xh'=2,'c'=2] {'z3..., dimensions={0}, use_global_device_ids=true | all-gather | bytes 905216 | tf_op jit(solution)/shard_map/all_gather | solution.py:185
  61.1 0.0 collective-permute-done.1.their_weight_ref
  61.2 0.0 all-to-all-done
  61.2 0.7 slice.4.tokens_ref
  61.9 1.8 %keep_others.1 = (f32[4,224,128]{2,1,0:T(8,128)S(1)}, f32[4,224,128]{2,1,0:T(8,128)S(1)}, f32[2,224,128]{2,1,0:T(8,128)S(1)}, f32[2,224,128]{2,1,0:T(8,128)S(1)}) custom-call(s32[3]{0:T(128)S(1)} %pad_add_fusion.place_ref, bf16[2,2,4,2,64,512]{5,4,3,2,1,0:T(8,128)(2,1)S(1)} %bitcast.8, bf16[416,512]{1,0:T(8,128)(2,1)S(1)} %copy-done, ...), custom_call_target="tpu_custom_call" | custom-call | flops 268435456 | bytes 3145728 | tf_op jit(solution)/shard_map/keep_others/pallas_call | solution.py:73
  63.7 2.4 %collective-permute-start.2 = (f16[4,224,128]{2,1,0:T(8,128)(2,1)S(1)}, f16[4,224,128]{2,1,0:T(8,128)(2,1)S(1)}, u32[]{:S(2)}, u32[]{:S(2)}) collective-permute-start(f16[4,224,128]{2,1,0:T(8,128)(2,1)S(1)} %convert_element_type.60), channel_id=1, source_target_pairs={{0,16},{16,32},{32,48},{48,64},{64,80},{80,96},{96,112},{112,128},... | collective-permute-start | bytes 688136 | tf_op jit(solution)/shard_map/ppermute | solution.py:165
  66.1 4.8 %collective-permute-start.3 = (f16[4,224,128]{2,1,0:T(8,128)(2,1)S(1)}, f16[4,224,128]{2,1,0:T(8,128)(2,1)S(1)}, u32[]{:S(2)}, u32[]{:S(2)}) collective-permute-start(f16[4,224,128]{2,1,0:T(8,128)(2,1)S(1)} %convert_element_type.61), channel_id=1, source_target_pairs={{0,240},{16,0},{32,16},{48,32},{64,48},{80,64},{96,80},{112,96},{1... | collective-permute-start | bytes 688136 | tf_op jit(solution)/shard_map/ppermute | solution.py:165
  71.0 1.9 %collective-permute-start.4 = (f16[2,224,128]{2,1,0:T(8,128)(2,1)S(1)}, f16[2,224,128]{2,1,0:T(8,128)(2,1)S(1)}, u32[]{:S(2)}, u32[]{:S(2)}) collective-permute-start(f16[2,224,128]{2,1,0:T(8,128)(2,1)S(1)} %convert_element_type.62), channel_id=1, source_target_pairs={{0,32},{16,48},{32,64},{48,80},{64,96},{80,112},{96,128},{112,144}... | collective-permute-start | bytes 344072 | tf_op jit(solution)/shard_map/ppermute | solution.py:165
  72.9 6.0 %collective-permute-start.5 = (f16[2,224,128]{2,1,0:T(8,128)(2,1)S(1)}, f16[2,224,128]{2,1,0:T(8,128)(2,1)S(1)}, u32[]{:S(2)}, u32[]{:S(2)}) collective-permute-start(f16[2,224,128]{2,1,0:T(8,128)(2,1)S(1)} %convert_element_type.63), channel_id=1, source_target_pairs={{0,224},{16,240},{32,0},{48,16},{64,32},{80,48},{96,64},{112,80},{... | collective-permute-start | bytes 344072 | tf_op jit(solution)/shard_map/ppermute | solution.py:165
  79.0 1.1 %keep_own.1.own_ref = f32[4,208,128]{2,1,0:T(8,128)S(1)} custom-call(s32[3]{0:T(128)S(1)} %pad_add_fusion.place_ref, bf16[2,2,4,2,64,512]{5,4,3,2,1,0:T(8,128)(2,1)S(1)} %bitcast.9, bf16[416,512]{1,0:T(8,128)(2,1)S(1)} %copy-done, bf16[416,512]{1,0:T(8,128)(2,1)S(1)} %collective-permute-done.1.their_weight_ref, bf16[16,416]{1,0:T(8,128)(2,1)S(1)} %slice.4.tokens_ref), custom_call_target="tpu_custom_call" | custom-call | flops 268435456 | bytes 3145728 | tf_op jit(solution)/shard_map/keep_own/pallas_call | solution.py:73
  80.1 1.6 %weight_part.1 = (f32[416,512]{1,0:T(8,128)S(1)}, f32[416,512]{1,0:T(8,128)S(1)}) custom-call(s32[3]{0:T(128)S(1)} %pad_add_fusion.place_ref, bf16[8,2,64,416]{3,2,1,0:T(8,128)(2,1)S(1)} %bitcast.11, bf16[2,2,512,512]{3,2,1,0:T(8,128)(2,1)S(1)} %bitcast.10), custom_call_target="tpu_custom_call" | custom-call | flops 1073741824 | bytes 5242880 | tf_op jit(solution)/shard_map/weight_part/pallas_call | solution.py:152
  81.8 0.0 collective-permute-done.4
  81.8 0.6 collective-permute-done.5
  82.3 0.0 collective-permute-done.2
  82.3 0.0 collective-permute-done.3
  82.3 3.4 %collective-permute-start.10 = (f32[416,512]{1,0:T(8,128)S(1)}, f32[416,512]{1,0:T(8,128)S(1)}, u32[]{:S(2)}, u32[]{:S(2)}) collective-permute-start(f32[416,512]{1,0:T(8,128)S(1)} %get-tuple-element.47), channel_id=1, source_target_pairs={{0,256},{256,0},{1,257},{257,1},{2,258},{258,2},{3,259},{259,3},{4... | collective-permute-start | bytes 2555912 | tf_op jit(solution)/shard_map/ppermute | solution.py:195
  85.8 1.1 merge_parts.1
  87.0 6.6 %collective-permute-start.6 = (f16[224,128]{1,0:T(8,128)(2,1)S(1)}, f16[224,128]{1,0:T(8,128)(2,1)S(1)}, u32[]{:S(2)}, u32[]{:S(2)}) collective-permute-start(f16[224,128]{1,0:T(8,128)(2,1)S(1)} %convert_element_type.68), channel_id=1, source_target_pairs={{0,128},{16,384},{64,192},{80,448},{128,0},{144,256},{192,64},{208... | collective-permute-start | bytes 172040 | tf_op jit(solution)/shard_map/ppermute | solution.py:172
  93.6 6.8 %collective-permute-start.7 = (f16[224,128]{1,0:T(8,128)(2,1)S(1)}, f16[224,128]{1,0:T(8,128)(2,1)S(1)}, u32[]{:S(2)}, u32[]{:S(2)}) collective-permute-start(f16[224,128]{1,0:T(8,128)(2,1)S(1)} %convert_element_type.69), channel_id=1, source_target_pairs={{0,64},{16,320},{64,128},{80,384},{128,192},{144,448},{192,0},{208... | collective-permute-start | bytes 172040 | tf_op jit(solution)/shard_map/ppermute | solution.py:172
  100.4 3.0 %collective-permute-start.8 = (f16[224,128]{1,0:T(8,128)(2,1)S(1)}, f16[224,128]{1,0:T(8,128)(2,1)S(1)}, u32[]{:S(2)}, u32[]{:S(2)}) collective-permute-start(f16[224,128]{1,0:T(8,128)(2,1)S(1)} %convert_element_type.70), channel_id=1, source_target_pairs={{0,192},{16,448},{64,0},{80,256},{128,64},{144,320},{192,128},{208... | collective-permute-start | bytes 172040 | tf_op jit(solution)/shard_map/ppermute | solution.py:172
  103.4 6.4 %collective-permute-start.9 = (f16[224,128]{1,0:T(8,128)(2,1)S(1)}, f16[224,128]{1,0:T(8,128)(2,1)S(1)}, u32[]{:S(2)}, u32[]{:S(2)}) collective-permute-start(f16[224,128]{1,0:T(8,128)(2,1)S(1)} %convert_element_type.71), channel_id=1, source_target_pairs={{0,0},{16,256},{64,64},{80,320},{128,128},{144,384},{192,192},{208... | collective-permute-start | bytes 172040 | tf_op jit(solution)/shard_map/ppermute | solution.py:172
  109.8 0.0 collective-permute-done.10
  109.8 1.1 add_multiply_fusion
  110.9 0.0 collective-permute-done.7
  110.9 1.9 %collective-permute-done.8 = f16[224,128]{1,0:T(8,128)(2,1)S(1)} collective-permute-done((f16[224,128]{1,0:T(8,128)(2,1)S(1)}, f16[224,128]{1,0:T(8,128)(2,1)S(1)}, u32[]{:S(2)}, u32[]{:S(2)}) %collective-permute-start.8) | collective-permute-done | bytes 57376 | tf_op jit(solution)/shard_map/ppermute | solution.py:172
  112.9 0.7 finish_grads.1
  (27 shorter events, 0.4 us)
Async XLA Ops:
  3.1 9.8 %copy-start.2 = (bf16[64,416]{1,0:T(8,128)(2,1)S(1)}, bf16[64,416]{1,0:T(8,128)(2,1)}, u32[]{:S(2)}) copy-start(bf16[64,416]{1,0:T(8,128)(2,1)} %up_ref.1) | copy-start | bytes 159748
  3.1 9.8 %copy-start.3 = (bf16[64,416]{1,0:T(8,128)(2,1)S(1)}, bf16[64,416]{1,0:T(8,128)(2,1)}, u32[]{:S(2)}) copy-start(bf16[64,416]{1,0:T(8,128)(2,1)} %gate_ref.1) | copy-start | bytes 159748
  3.1 11.9 %copy-start = (bf16[416,512]{1,0:T(8,128)(2,1)S(1)}, bf16[416,512]{1,0:T(8,128)(2,1)}, u32[]{:S(2)}) copy-start(bf16[416,512]{1,0:T(8,128)(2,1)} %own_weight_ref.3) | copy-start | bytes 1277956
  3.1 58.0 %all-to-all-start = ((bf16[32,64,512]{2,1,0:T(8,128)(2,1)}), bf16[32,64,512]{2,1,0:T(8,128)(2,1)S(1)}, u32[]{:S(2)}, u32[]{:S(2)}) async-start(bf16[32,64,512]{2,1,0:T(8,128)(2,1)} %bitcast.12), calls=%async_computation | async-start | bytes 4194304 | tf_op jit(solution)/shard_map/all_to_all | solution.py:184
  13.0 7.1 %collective-permute-start = (bf16[64,416]{1,0:T(8,128)(2,1)S(1)}, bf16[64,416]{1,0:T(8,128)(2,1)S(1)}, u32[]{:S(2)}, u32[]{:S(2)}) collective-permute-start(bf16[64,416]{1,0:T(8,128)(2,1)S(1)} %fusion.4), channel_id=1, source_target_pairs={{0,0},{16,256},{256,16},{272,272},{1,1},{17,257},{257,17},{273,273... | collective-permute-start | bytes 159752 | tf_op jit(solution)/shard_map/ppermute | solution.py:181
  15.0 46.1 %collective-permute-start.1 = (bf16[416,512]{1,0:T(8,128)(2,1)S(1)}, bf16[416,512]{1,0:T(8,128)(2,1)S(1)}, u32[]{:S(2)}, u32[]{:S(2)}) collective-permute-start(bf16[416,512]{1,0:T(8,128)(2,1)S(1)} %copy-done), channel_id=1, source_target_pairs={{0,256},{256,0},{1,257},{257,1},{2,258},{258,2},{3,259},{259,3},{4... | collective-permute-start | bytes 1277960 | tf_op jit(solution)/shard_map/ppermute | solution.py:182
  63.7 18.6 %collective-permute-start.2 = (f16[4,224,128]{2,1,0:T(8,128)(2,1)S(1)}, f16[4,224,128]{2,1,0:T(8,128)(2,1)S(1)}, u32[]{:S(2)}, u32[]{:S(2)}) collective-permute-start(f16[4,224,128]{2,1,0:T(8,128)(2,1)S(1)} %convert_element_type.60), channel_id=1, source_target_pairs={{0,16},{16,32},{32,48},{48,64},{64,80},{80,96},{96,112},{112,128},... | collective-permute-start | bytes 688136 | tf_op jit(solution)/shard_map/ppermute | solution.py:165
  66.1 14.0 %copy-start.1 = (bf16[1024,416]{1,0:T(8,128)(2,1)S(1)}, bf16[1024,416]{1,0:T(8,128)(2,1)}, u32[]{:S(2)}) copy-start(bf16[1024,416]{1,0:T(8,128)(2,1)} %all_gather.3) | copy-start | bytes 2555908
  66.1 16.2 %collective-permute-start.3 = (f16[4,224,128]{2,1,0:T(8,128)(2,1)S(1)}, f16[4,224,128]{2,1,0:T(8,128)(2,1)S(1)}, u32[]{:S(2)}, u32[]{:S(2)}) collective-permute-start(f16[4,224,128]{2,1,0:T(8,128)(2,1)S(1)} %convert_element_type.61), channel_id=1, source_target_pairs={{0,240},{16,0},{32,16},{48,32},{64,48},{80,64},{96,80},{112,96},{1... | collective-permute-start | bytes 688136 | tf_op jit(solution)/shard_map/ppermute | solution.py:165
  71.0 10.8 %collective-permute-start.4 = (f16[2,224,128]{2,1,0:T(8,128)(2,1)S(1)}, f16[2,224,128]{2,1,0:T(8,128)(2,1)S(1)}, u32[]{:S(2)}, u32[]{:S(2)}) collective-permute-start(f16[2,224,128]{2,1,0:T(8,128)(2,1)S(1)} %convert_element_type.62), channel_id=1, source_target_pairs={{0,32},{16,48},{32,64},{48,80},{64,96},{80,112},{96,128},{112,144}... | collective-permute-start | bytes 344072 | tf_op jit(solution)/shard_map/ppermute | solution.py:165
  72.9 9.4 %collective-permute-start.5 = (f16[2,224,128]{2,1,0:T(8,128)(2,1)S(1)}, f16[2,224,128]{2,1,0:T(8,128)(2,1)S(1)}, u32[]{:S(2)}, u32[]{:S(2)}) collective-permute-start(f16[2,224,128]{2,1,0:T(8,128)(2,1)S(1)} %convert_element_type.63), channel_id=1, source_target_pairs={{0,224},{16,240},{32,0},{48,16},{64,32},{80,48},{96,64},{112,80},{... | collective-permute-start | bytes 344072 | tf_op jit(solution)/shard_map/ppermute | solution.py:165
  82.3 27.5 %collective-permute-start.10 = (f32[416,512]{1,0:T(8,128)S(1)}, f32[416,512]{1,0:T(8,128)S(1)}, u32[]{:S(2)}, u32[]{:S(2)}) collective-permute-start(f32[416,512]{1,0:T(8,128)S(1)} %get-tuple-element.47), channel_id=1, source_target_pairs={{0,256},{256,0},{1,257},{257,1},{2,258},{258,2},{3,259},{259,3},{4... | collective-permute-start | bytes 2555912 | tf_op jit(solution)/shard_map/ppermute | solution.py:195
  87.0 23.9 %collective-permute-start.6 = (f16[224,128]{1,0:T(8,128)(2,1)S(1)}, f16[224,128]{1,0:T(8,128)(2,1)S(1)}, u32[]{:S(2)}, u32[]{:S(2)}) collective-permute-start(f16[224,128]{1,0:T(8,128)(2,1)S(1)} %convert_element_type.68), channel_id=1, source_target_pairs={{0,128},{16,384},{64,192},{80,448},{128,0},{144,256},{192,64},{208... | collective-permute-start | bytes 172040 | tf_op jit(solution)/shard_map/ppermute | solution.py:172
  93.6 17.4 %collective-permute-start.7 = (f16[224,128]{1,0:T(8,128)(2,1)S(1)}, f16[224,128]{1,0:T(8,128)(2,1)S(1)}, u32[]{:S(2)}, u32[]{:S(2)}) collective-permute-start(f16[224,128]{1,0:T(8,128)(2,1)S(1)} %convert_element_type.69), channel_id=1, source_target_pairs={{0,64},{16,320},{64,128},{80,384},{128,192},{144,448},{192,0},{208... | collective-permute-start | bytes 172040 | tf_op jit(solution)/shard_map/ppermute | solution.py:172
  100.4 12.5 %collective-permute-start.8 = (f16[224,128]{1,0:T(8,128)(2,1)S(1)}, f16[224,128]{1,0:T(8,128)(2,1)S(1)}, u32[]{:S(2)}, u32[]{:S(2)}) collective-permute-start(f16[224,128]{1,0:T(8,128)(2,1)S(1)} %convert_element_type.70), channel_id=1, source_target_pairs={{0,192},{16,448},{64,0},{80,256},{128,64},{144,320},{192,128},{208... | collective-permute-start | bytes 172040 | tf_op jit(solution)/shard_map/ppermute | solution.py:172
  103.4 9.5 %collective-permute-start.9 = (f16[224,128]{1,0:T(8,128)(2,1)S(1)}, f16[224,128]{1,0:T(8,128)(2,1)S(1)}, u32[]{:S(2)}, u32[]{:S(2)}) collective-permute-start(f16[224,128]{1,0:T(8,128)(2,1)S(1)} %convert_element_type.71), channel_id=1, source_target_pairs={{0,0},{16,256},{64,64},{80,320},{128,128},{144,384},{192,192},{208... | collective-permute-start | bytes 172040 | tf_op jit(solution)/shard_map/ppermute | solution.py:172

commit v9 on v7

--- a/solution.py
+++ b/solution.py
@@ -44,9 +44,8 @@
     return lax.dot_general(rows, weight, (((1,), (1,)), ((), ())), preferred_element_type=jnp.float32)
 
 
-def keep_kernel(for_others, place_ref, grad_ref, own_weight_ref, their_weight_ref, tokens_ref, *refs):
-    del tokens_ref
-    out_refs, padded = refs[:-1], refs[-1]
+def keep_kernel(for_others, place_ref, grad_ref, own_weight_ref, their_weight_ref, *refs):
+    out_refs, padded = refs[1 if for_others else 0 : -1], refs[-1]
     hid, feats = own_weight_ref.shape
     xl, low = place_ref[0], place_ref[1]
     padded[:, hid:] = jnp.zeros_like(padded[:, hid:])
@@ -68,18 +67,18 @@
                 out_refs[2 + far // 2][far % 2] = encode(vals)
 
 
-def keep_part(for_others, place, grad, own_weight, their_weight, tokens):
+def keep_part(for_others, place, grad, own_weight, their_weight, *tokens):
     shapes = [(4, 224, LANES), (4, 224, LANES), (2, 224, LANES), (2, 224, LANES)] if for_others else [(4, 208, LANES)]
     return pl.pallas_call(
         functools.partial(keep_kernel, for_others),
         out_shape=tuple(jax.ShapeDtypeStruct(s, jnp.float32) for s in shapes),
-        in_specs=[scalars] + [whole] * 4,
+        in_specs=[scalars] + [whole] * (3 + len(tokens)),
         out_specs=(whole,) * len(shapes),
         scratch_shapes=[pltpu.VMEM((2, 512, own_weight.shape[1]), own_weight.dtype)],
         compiler_params=pltpu.CompilerParams(vmem_limit_bytes=VMEM_BYTES),
         cost_estimate=pl.CostEstimate(flops=2 * 256 * 1024 * 512, bytes_accessed=3 << 20, transcendentals=0),
         name="keep_others" if for_others else "keep_own",
-    )(place, grad, own_weight, their_weight, tokens)
+    )(place, grad, own_weight, their_weight, *tokens)
 
 
 def merge_kernel(place_ref, own_ref, up1_ref, down1_ref, up2_ref, down2_ref, *out_refs):
@@ -188,7 +187,7 @@
 
     halves = [k.astype(jnp.float16) for k in keep_part(True, place, blocks, down_weight, their_weight, tokens)]
     near = [shift(h, Z, step) for h, step in zip(halves, (1, -1, 2, -2), strict=True)]
-    (kept,) = keep_part(False, place, blocks, down_weight, their_weight, tokens)
+    (kept,) = keep_part(False, place, blocks, down_weight, their_weight)
     own, theirs = weight_part(place, tokens.reshape(8, 2, 64, hid), grad.reshape(2, 2, 512, feats))
     near, kept, theirs = lax.optimization_barrier((near, kept, theirs))
     merged = merge(place, [kept] + [n.astype(jnp.float32) for n in near])

time: 112 us -> 112 us (level)
  no operation moved by 1% of the time
where the time goes in v9:
time: 112 us; the launch traced here: 111 us
  starting transfers between devices  55 us (49%)
  blocking collectives  38.8 us (35%)
  Pallas kernels  7.64 us (7%)
  waiting for transfers between devices  5.12 us (5%)
  local copies, waits for them, and re-layouts  2.49 us (2%)
  other arithmetic  1.49 us (1%)
    all_gather x1, blocking collectives, shards(): tokens = lax.all_gather(hidden, Z, axis=0, tiled=True)  38.8 us
    ppermute x4, starting transfers between devices, to_owner(): return lax.ppermute(array, ('xl',) + FAR + ('z0',), pairs)  22.5 us
    ppermute x4, starting transfers between devices, shift(): lax.ppermute(array, axes, [(i, (i + step) % size) for i in range(size)])  15 us
    all_to_all x1, starting transfers between devices, shards(): grad = lax.all_to_all(copies, ('xl',) + TENSOR, 0, 0)  9.76 us
    pallas_call x2, Pallas kernels, keep_part(): pl.pallas_call(functools.partial(keep_kernel, for_others), out_shape=tupl...  4.14 us
    ppermute x1, starting transfers between devices, shards(): got = lax.ppermute(theirs, 'xl', SWAP)  3.71 us
    ppermute x1, waiting for transfers between devices, shards(): hidden = lax.ppermute(hidden, ('xl', 'z0'), TURN)  2.99 us
    broadcast_in_dim x1, local copies, waits for them, and re-layouts, shards(): jnp.broadcast_to(out_grad.reshape(2, 1, 64, feats), (2, 16, 64, feats))  2.48 us
  transfers between devices with their start and end apart: 12, of which 2 were waited for; matrix products, arithmetic and copies ran while one was open for 1% of the time, Pallas kernels for 4%

profile of v9, /device:TPU:6, one launch (start us, length us, event | category | flops | bytes accessed | tf_op | source)
XLA Modules:
  0.0 111.5 jit_solution(2562813109196909591)
XLA Ops:
  0.6 2.5 %broadcast_in_dim.8 = bf16[2,16,64,512]{3,2,1,0:T(8,128)(2,1)} broadcast(bf16[2,64,512]{2,1,0:T(8,128)(2,1)} %bitcast.13), dimensions={0,2,3} | broadcast | bytes 2228224 | tf_op jit(solution)/shard_map/broadcast_in_dim | solution.py:182
  3.1 9.8 %all-to-all-start = ((bf16[32,64,512]{2,1,0:T(8,128)(2,1)}), bf16[32,64,512]{2,1,0:T(8,128)(2,1)S(1)}, u32[]{:S(2)}, u32[]{:S(2)}) async-start(bf16[32,64,512]{2,1,0:T(8,128)(2,1)} %bitcast.12), calls=%async_computation | async-start | bytes 4194304 | tf_op jit(solution)/shard_map/all_to_all | solution.py:183
  13.0 2.1 %collective-permute-start = (bf16[64,416]{1,0:T(8,128)(2,1)S(1)}, bf16[64,416]{1,0:T(8,128)(2,1)S(1)}, u32[]{:S(2)}, u32[]{:S(2)}) collective-permute-start(bf16[64,416]{1,0:T(8,128)(2,1)S(1)} %fusion.4), channel_id=1, source_target_pairs={{0,0},{16,256},{256,16},{272,272},{1,1},{17,257},{257,17},{273,273... | collective-permute-start | bytes 159752 | tf_op jit(solution)/shard_map/ppermute | solution.py:180
  15.0 1.9 %collective-permute-start.1 = (bf16[416,512]{1,0:T(8,128)(2,1)}, bf16[416,512]{1,0:T(8,128)(2,1)}, u32[]{:S(2)}, u32[]{:S(2)}) collective-permute-start(bf16[416,512]{1,0:T(8,128)(2,1)} %own_weight_ref.3), channel_id=1, source_target_pairs={{0,256},{256,0},{1,257},{257,1},{2,258},{258,2},{3,259},{259,3},{4... | collective-permute-start | bytes 1277960 | tf_op jit(solution)/shard_map/ppermute | solution.py:181
  17.0 0.1 pad_add_fusion.place_ref
  17.0 3.0 %collective-permute-done = bf16[64,416]{1,0:T(8,128)(2,1)S(1)} collective-permute-done((bf16[64,416]{1,0:T(8,128)(2,1)S(1)}, bf16[64,416]{1,0:T(8,128)(2,1)S(1)}, u32[]{:S(2)}, u32[]{:S(2)}) %collective-permute-start) | collective-permute-done | bytes 53280 | tf_op jit(solution)/shard_map/ppermute | solution.py:180
  20.0 38.8 %all_gather.3.refs_0_ = bf16[1024,416]{1,0:T(8,128)(2,1)S(1)} all-gather(bf16[64,416]{1,0:T(8,128)(2,1)S(1)} %collective-permute-done), channel_id=1, replica_groups=mesh['xl'=2,'z3'=2,'z2'=2,'z1'=2,'z0'=2,'y1'=2,'y0'=2,'xh'=2,'c'=2] {'z3..., dimensions={0}, use_global_device_ids=true | all-gather | bytes 905216 | tf_op jit(solution)/shard_map/all_gather | solution.py:184
  58.8 0.0 collective-permute-done.1.their_weight_ref
  58.8 0.0 all-to-all-done
  58.8 2.4 %keep_others.1 = (f32[4,224,128]{2,1,0:T(8,128)S(1)}, f32[4,224,128]{2,1,0:T(8,128)S(1)}, f32[2,224,128]{2,1,0:T(8,128)S(1)}, f32[2,224,128]{2,1,0:T(8,128)S(1)}) custom-call(s32[3]{0:T(128)S(1)} %pad_add_fusion.place_ref, bf16[2,2,4,2,64,512]{5,4,3,2,1,0:T(8,128)(2,1)S(1)} %bitcast.8, bf16[416,512]{1,0:T(8,128)(2,1)} %own_weight_ref.3, ...), custom_call_target="tpu_custom_call" | custom-call | flops 268435456 | bytes 3145728 | tf_op jit(solution)/shard_map/keep_others/pallas_call | solution.py:72
  61.3 2.4 %collective-permute-start.2 = (f16[4,224,128]{2,1,0:T(8,128)(2,1)S(1)}, f16[4,224,128]{2,1,0:T(8,128)(2,1)S(1)}, u32[]{:S(2)}, u32[]{:S(2)}) collective-permute-start(f16[4,224,128]{2,1,0:T(8,128)(2,1)S(1)} %convert_element_type.60), channel_id=1, source_target_pairs={{0,16},{16,32},{32,48},{48,64},{64,80},{80,96},{96,112},{112,128},... | collective-permute-start | bytes 688136 | tf_op jit(solution)/shard_map/ppermute | solution.py:164
  63.7 4.7 %collective-permute-start.3 = (f16[4,224,128]{2,1,0:T(8,128)(2,1)S(1)}, f16[4,224,128]{2,1,0:T(8,128)(2,1)S(1)}, u32[]{:S(2)}, u32[]{:S(2)}) collective-permute-start(f16[4,224,128]{2,1,0:T(8,128)(2,1)S(1)} %convert_element_type.61), channel_id=1, source_target_pairs={{0,240},{16,0},{32,16},{48,32},{64,48},{80,64},{96,80},{112,96},{1... | collective-permute-start | bytes 688136 | tf_op jit(solution)/shard_map/ppermute | solution.py:164
  68.4 1.9 %collective-permute-start.4 = (f16[2,224,128]{2,1,0:T(8,128)(2,1)S(1)}, f16[2,224,128]{2,1,0:T(8,128)(2,1)S(1)}, u32[]{:S(2)}, u32[]{:S(2)}) collective-permute-start(f16[2,224,128]{2,1,0:T(8,128)(2,1)S(1)} %convert_element_type.62), channel_id=1, source_target_pairs={{0,32},{16,48},{32,64},{48,80},{64,96},{80,112},{96,128},{112,144}... | collective-permute-start | bytes 344072 | tf_op jit(solution)/shard_map/ppermute | solution.py:164
  70.4 6.0 %collective-permute-start.5 = (f16[2,224,128]{2,1,0:T(8,128)(2,1)S(1)}, f16[2,224,128]{2,1,0:T(8,128)(2,1)S(1)}, u32[]{:S(2)}, u32[]{:S(2)}) collective-permute-start(f16[2,224,128]{2,1,0:T(8,128)(2,1)S(1)} %convert_element_type.63), channel_id=1, source_target_pairs={{0,224},{16,240},{32,0},{48,16},{64,32},{80,48},{96,64},{112,80},{... | collective-permute-start | bytes 344072 | tf_op jit(solution)/shard_map/ppermute | solution.py:164
  76.4 1.7 %keep_own.1.own_ref = f32[4,208,128]{2,1,0:T(8,128)S(1)} custom-call(s32[3]{0:T(128)S(1)} %pad_add_fusion.place_ref, bf16[2,2,4,2,64,512]{5,4,3,2,1,0:T(8,128)(2,1)S(1)} %bitcast.9, bf16[416,512]{1,0:T(8,128)(2,1)} %own_weight_ref.3, bf16[416,512]{1,0:T(8,128)(2,1)} %collective-permute-done.1.their_weight_ref), custom_call_target="tpu_custom_call" | custom-call | flops 268435456 | bytes 3145728 | tf_op jit(solution)/shard_map/keep_own/pallas_call | solution.py:72
  78.2 1.6 %weight_part.1 = (f32[416,512]{1,0:T(8,128)S(1)}, f32[416,512]{1,0:T(8,128)S(1)}) custom-call(s32[3]{0:T(128)S(1)} %pad_add_fusion.place_ref, bf16[8,2,64,416]{3,2,1,0:T(8,128)(2,1)S(1)} %bitcast.11, bf16[2,2,512,512]{3,2,1,0:T(8,128)(2,1)S(1)} %bitcast.10), custom_call_target="tpu_custom_call" | custom-call | flops 1073741824 | bytes 5242880 | tf_op jit(solution)/shard_map/weight_part/pallas_call | solution.py:151
  79.8 0.0 collective-permute-done.4
  79.8 0.0 collective-permute-done.5
  79.8 0.0 collective-permute-done.2
  79.8 0.0 collective-permute-done.3
  79.8 3.7 %collective-permute-start.10 = (f32[416,512]{1,0:T(8,128)S(1)}, f32[416,512]{1,0:T(8,128)S(1)}, u32[]{:S(2)}, u32[]{:S(2)}) collective-permute-start(f32[416,512]{1,0:T(8,128)S(1)} %get-tuple-element.47), channel_id=1, source_target_pairs={{0,256},{256,0},{1,257},{257,1},{2,258},{258,2},{3,259},{259,3},{4... | collective-permute-start | bytes 2555912 | tf_op jit(solution)/shard_map/ppermute | solution.py:194
  83.7 1.1 %merge_parts.1 = (f32[224,128]{1,0:T(8,128)S(1)}, f32[224,128]{1,0:T(8,128)S(1)}, f32[224,128]{1,0:T(8,128)S(1)}, f32[224,128]{1,0:T(8,128)S(1)}) custom-call(s32[3]{0:T(128)S(1)} %pad_add_fusion.place_ref, f32[4,208,128]{2,1,0:T(8,128)S(1)} %keep_own.1.own_ref, f32[4,224,128]{2,1,0:T(8,128)S(1)} %convert_element_type.64.up1_ref, ...), custom_call_target="tpu_custom_call" | custom-call | flops 1048576 | bytes 1048576 | tf_op jit(solution)/shard_map/merge_parts/pallas_call | solution.py:97
  84.8 6.3 %collective-permute-start.6 = (f16[224,128]{1,0:T(8,128)(2,1)S(1)}, f16[224,128]{1,0:T(8,128)(2,1)S(1)}, u32[]{:S(2)}, u32[]{:S(2)}) collective-permute-start(f16[224,128]{1,0:T(8,128)(2,1)S(1)} %convert_element_type.68), channel_id=1, source_target_pairs={{0,128},{16,384},{64,192},{80,448},{128,0},{144,256},{192,64},{208... | collective-permute-start | bytes 172040 | tf_op jit(solution)/shard_map/ppermute | solution.py:171
  91.2 7.4 %collective-permute-start.7 = (f16[224,128]{1,0:T(8,128)(2,1)S(1)}, f16[224,128]{1,0:T(8,128)(2,1)S(1)}, u32[]{:S(2)}, u32[]{:S(2)}) collective-permute-start(f16[224,128]{1,0:T(8,128)(2,1)S(1)} %convert_element_type.69), channel_id=1, source_target_pairs={{0,64},{16,320},{64,128},{80,384},{128,192},{144,448},{192,0},{208... | collective-permute-start | bytes 172040 | tf_op jit(solution)/shard_map/ppermute | solution.py:171
  98.6 2.3 %collective-permute-start.8 = (f16[224,128]{1,0:T(8,128)(2,1)S(1)}, f16[224,128]{1,0:T(8,128)(2,1)S(1)}, u32[]{:S(2)}, u32[]{:S(2)}) collective-permute-start(f16[224,128]{1,0:T(8,128)(2,1)S(1)} %convert_element_type.70), channel_id=1, source_target_pairs={{0,192},{16,448},{64,0},{80,256},{128,64},{144,320},{192,128},{208... | collective-permute-start | bytes 172040 | tf_op jit(solution)/shard_map/ppermute | solution.py:171
  101.0 6.4 %collective-permute-start.9 = (f16[224,128]{1,0:T(8,128)(2,1)S(1)}, f16[224,128]{1,0:T(8,128)(2,1)S(1)}, u32[]{:S(2)}, u32[]{:S(2)}) collective-permute-start(f16[224,128]{1,0:T(8,128)(2,1)S(1)} %convert_element_type.71), channel_id=1, source_target_pairs={{0,0},{16,256},{64,64},{80,320},{128,128},{144,384},{192,192},{208... | collective-permute-start | bytes 172040 | tf_op jit(solution)/shard_map/ppermute | solution.py:171
  107.5 1.1 add_multiply_fusion
  108.5 0.0 collective-permute-done.6
  108.5 0.0 collective-permute-done.7
  108.6 2.1 %collective-permute-done.8 = f16[224,128]{1,0:T(8,128)(2,1)S(1)} collective-permute-done((f16[224,128]{1,0:T(8,128)(2,1)S(1)}, f16[224,128]{1,0:T(8,128)(2,1)S(1)}, u32[]{:S(2)}, u32[]{:S(2)}) %collective-permute-start.8) | collective-permute-done | bytes 57376 | tf_op jit(solution)/shard_map/ppermute | solution.py:171
  110.7 0.0 collective-permute-done.9
  110.7 0.7 finish_grads.1
  (22 shorter events, 0.4 us)
Async XLA Ops:
  3.1 9.8 %copy-start = (bf16[64,416]{1,0:T(8,128)(2,1)S(1)}, bf16[64,416]{1,0:T(8,128)(2,1)}, u32[]{:S(2)}) copy-start(bf16[64,416]{1,0:T(8,128)(2,1)} %up_ref.1) | copy-start | bytes 159748
  3.1 9.8 %copy-start.1 = (bf16[64,416]{1,0:T(8,128)(2,1)S(1)}, bf16[64,416]{1,0:T(8,128)(2,1)}, u32[]{:S(2)}) copy-start(bf16[64,416]{1,0:T(8,128)(2,1)} %gate_ref.1) | copy-start | bytes 159748
  3.1 55.7 %all-to-all-start = ((bf16[32,64,512]{2,1,0:T(8,128)(2,1)}), bf16[32,64,512]{2,1,0:T(8,128)(2,1)S(1)}, u32[]{:S(2)}, u32[]{:S(2)}) async-start(bf16[32,64,512]{2,1,0:T(8,128)(2,1)} %bitcast.12), calls=%async_computation | async-start | bytes 4194304 | tf_op jit(solution)/shard_map/all_to_all | solution.py:183
  13.0 7.1 %collective-permute-start = (bf16[64,416]{1,0:T(8,128)(2,1)S(1)}, bf16[64,416]{1,0:T(8,128)(2,1)S(1)}, u32[]{:S(2)}, u32[]{:S(2)}) collective-permute-start(bf16[64,416]{1,0:T(8,128)(2,1)S(1)} %fusion.4), channel_id=1, source_target_pairs={{0,0},{16,256},{256,16},{272,272},{1,1},{17,257},{257,17},{273,273... | collective-permute-start | bytes 159752 | tf_op jit(solution)/shard_map/ppermute | solution.py:180
  15.0 43.8 %collective-permute-start.1 = (bf16[416,512]{1,0:T(8,128)(2,1)}, bf16[416,512]{1,0:T(8,128)(2,1)}, u32[]{:S(2)}, u32[]{:S(2)}) collective-permute-start(bf16[416,512]{1,0:T(8,128)(2,1)} %own_weight_ref.3), channel_id=1, source_target_pairs={{0,256},{256,0},{1,257},{257,1},{2,258},{258,2},{3,259},{259,3},{4... | collective-permute-start | bytes 1277960 | tf_op jit(solution)/shard_map/ppermute | solution.py:181
  61.3 18.5 %collective-permute-start.2 = (f16[4,224,128]{2,1,0:T(8,128)(2,1)S(1)}, f16[4,224,128]{2,1,0:T(8,128)(2,1)S(1)}, u32[]{:S(2)}, u32[]{:S(2)}) collective-permute-start(f16[4,224,128]{2,1,0:T(8,128)(2,1)S(1)} %convert_element_type.60), channel_id=1, source_target_pairs={{0,16},{16,32},{32,48},{48,64},{64,80},{80,96},{96,112},{112,128},... | collective-permute-start | bytes 688136 | tf_op jit(solution)/shard_map/ppermute | solution.py:164
  63.7 16.1 %collective-permute-start.3 = (f16[4,224,128]{2,1,0:T(8,128)(2,1)S(1)}, f16[4,224,128]{2,1,0:T(8,128)(2,1)S(1)}, u32[]{:S(2)}, u32[]{:S(2)}) collective-permute-start(f16[4,224,128]{2,1,0:T(8,128)(2,1)S(1)} %convert_element_type.61), channel_id=1, source_target_pairs={{0,240},{16,0},{32,16},{48,32},{64,48},{80,64},{96,80},{112,96},{1... | collective-permute-start | bytes 688136 | tf_op jit(solution)/shard_map/ppermute | solution.py:164
  68.4 11.4 %collective-permute-start.4 = (f16[2,224,128]{2,1,0:T(8,128)(2,1)S(1)}, f16[2,224,128]{2,1,0:T(8,128)(2,1)S(1)}, u32[]{:S(2)}, u32[]{:S(2)}) collective-permute-start(f16[2,224,128]{2,1,0:T(8,128)(2,1)S(1)} %convert_element_type.62), channel_id=1, source_target_pairs={{0,32},{16,48},{32,64},{48,80},{64,96},{80,112},{96,128},{112,144}... | collective-permute-start | bytes 344072 | tf_op jit(solution)/shard_map/ppermute | solution.py:164
  70.4 9.4 %collective-permute-start.5 = (f16[2,224,128]{2,1,0:T(8,128)(2,1)S(1)}, f16[2,224,128]{2,1,0:T(8,128)(2,1)S(1)}, u32[]{:S(2)}, u32[]{:S(2)}) collective-permute-start(f16[2,224,128]{2,1,0:T(8,128)(2,1)S(1)} %convert_element_type.63), channel_id=1, source_target_pairs={{0,224},{16,240},{32,0},{48,16},{64,32},{80,48},{96,64},{112,80},{... | collective-permute-start | bytes 344072 | tf_op jit(solution)/shard_map/ppermute | solution.py:164
  79.8 27.6 %collective-permute-start.10 = (f32[416,512]{1,0:T(8,128)S(1)}, f32[416,512]{1,0:T(8,128)S(1)}, u32[]{:S(2)}, u32[]{:S(2)}) collective-permute-start(f32[416,512]{1,0:T(8,128)S(1)} %get-tuple-element.47), channel_id=1, source_target_pairs={{0,256},{256,0},{1,257},{257,1},{2,258},{258,2},{3,259},{259,3},{4... | collective-permute-start | bytes 2555912 | tf_op jit(solution)/shard_map/ppermute | solution.py:194
  84.8 23.7 %collective-permute-start.6 = (f16[224,128]{1,0:T(8,128)(2,1)S(1)}, f16[224,128]{1,0:T(8,128)(2,1)S(1)}, u32[]{:S(2)}, u32[]{:S(2)}) collective-permute-start(f16[224,128]{1,0:T(8,128)(2,1)S(1)} %convert_element_type.68), channel_id=1, source_target_pairs={{0,128},{16,384},{64,192},{80,448},{128,0},{144,256},{192,64},{208... | collective-permute-start | bytes 172040 | tf_op jit(solution)/shard_map/ppermute | solution.py:171
  91.2 17.4 %collective-permute-start.7 = (f16[224,128]{1,0:T(8,128)(2,1)S(1)}, f16[224,128]{1,0:T(8,128)(2,1)S(1)}, u32[]{:S(2)}, u32[]{:S(2)}) collective-permute-start(f16[224,128]{1,0:T(8,128)(2,1)S(1)} %convert_element_type.69), channel_id=1, source_target_pairs={{0,64},{16,320},{64,128},{80,384},{128,192},{144,448},{192,0},{208... | collective-permute-start | bytes 172040 | tf_op jit(solution)/shard_map/ppermute | solution.py:171
  98.6 12.0 %collective-permute-start.8 = (f16[224,128]{1,0:T(8,128)(2,1)S(1)}, f16[224,128]{1,0:T(8,128)(2,1)S(1)}, u32[]{:S(2)}, u32[]{:S(2)}) collective-permute-start(f16[224,128]{1,0:T(8,128)(2,1)S(1)} %convert_element_type.70), channel_id=1, source_target_pairs={{0,192},{16,448},{64,0},{80,256},{128,64},{144,320},{192,128},{208... | collective-permute-start | bytes 172040 | tf_op jit(solution)/shard_map/ppermute | solution.py:171
  101.0 9.7 %collective-permute-start.9 = (f16[224,128]{1,0:T(8,128)(2,1)S(1)}, f16[224,128]{1,0:T(8,128)(2,1)S(1)}, u32[]{:S(2)}, u32[]{:S(2)}) collective-permute-start(f16[224,128]{1,0:T(8,128)(2,1)S(1)} %convert_element_type.71), channel_id=1, source_target_pairs={{0,0},{16,256},{64,64},{80,320},{128,128},{144,384},{192,192},{208... | collective-permute-start | bytes 172040 | tf_op jit(solution)/shard_map/ppermute | solution.py:171
